TPU v7x, 128 devices: a whole 4x4x4 slice. The times are simulated.
128 devices in a mesh: section: 16 (over y, z_lo, core), tp: 8 (over x, z_hi).
Axes of the slice: x: 4, y: 4, z: 4 (z_hi: 2, z_lo: 2; z = z_hi * 2 + z_lo), core: 2. Of those that a mesh axis runs over, the one named last changes fastest.
Arguments:
- inputs: bfloat16 [3, 128, 6144], P(None, None, 'tp'), may hold values from -6 to 6
- cotangents: bfloat16 [3, 128, 6144], P(None, None, 'tp'), may hold values from -6 to 6
- carried: bfloat16 [16, 128, 6144], P('section', None, 'tp'), may hold values from -6 to 6
- pending: bfloat16 [16, 128, 6144], P('section', None, 'tp'), may hold values from -6 to 6
- stash: bfloat16 [16, 8, 128, 6144], P('section', None, None, 'tp'), may hold values from -6 to 6
- stash_plan: int32 [16, 4, 2], replicated, may hold values from 0 to 7, as said below
- gain: float32 [16, 6144], P('section'), may hold values from 0.5 to 2
- key_gain: float32 [16, 6144], P('section', 'tp'), may hold values from -4 to 4
- w_value: bfloat16 [16, 6144, 6144], P('section', None, 'tp'), may hold values from -0.078125 to 0.078125
- w_out: bfloat16 [16, 6144, 6144], P('section', 'tp'), may hold values from -0.078125 to 0.078125
Outputs:
- forward_out: bfloat16 [16, 4, 128, 6144], P('section', None, None, 'tp')
- input_grad: bfloat16 [16, 4, 128, 6144], P('section', None, None, 'tp')
Inputs may be any that keep to these rules, and one draw needn't show every extreme that they name: stash_plan[s, t, 0] is 0 if the stashed input of section s for step t is held by section s itself and 1 if by section 15 - s; stash_plan[s, t, 1] is its slot in the holder's stash: below 4 for a section's own blocks, 4 or above for blocks of its mirror; no slot of a holder is named twice.
All inputs are finite; a program needn't handle non-finite values.
Results may differ from a plain program's by a relative error of at most 0.034.
Values may be sent and summed in bfloat16 or wider, within the bound.
No kernel may reach another device: no remote copies, remote signals or barrier semaphores. Data moves between devices by JAX's collectives and lax.ppermute only.
A program may use at most 128 MiB of HBM per device.

v0:
```python
import math

import jax
import jax.numpy as jnp
from jax import lax
from jax.sharding import PartitionSpec as P

HEAD = 128


EPSILON = 1e-05


def from_behind(array, axis, by):
    peers = lax.axis_size(axis)
    pairs = [(i, i + by) for i in range(peers) if 0 <= i + by < peers]
    return lax.ppermute(array, axis, pairs)


def per_device(
    inputs, cotangents, carried, pending, stash, stash_plan, gain, key_gain, w_value, w_out
):
    groups = lax.axis_size("tp")
    feat_width = key_gain.shape[-1]
    full_width = feat_width * groups
    gain_full = gain[0]
    feat_offset = lax.axis_index("tp") * feat_width
    gain_row = lax.dynamic_slice_in_dim(gain_full, feat_offset, feat_width, 0)
    key_row = key_gain[0]
    value_local = w_value[0]
    out_local = w_out[0]
    section_index = lax.axis_index("section")
    section_count = lax.axis_size("section")
    mirror = section_count - 1 - section_index
    held_blocks = stash[0]
    token_rows = carried.shape[1]
    piece_rows = token_rows // section_count

    def normalize(block_in):
        values32 = block_in.astype(jnp.float32)
        totals = lax.psum(
            (jnp.sum(values32, -1, keepdims=True), jnp.sum(values32 * values32, -1, keepdims=True)),
            "tp",
        )
        row_mean = totals[0] / full_width
        variance = totals[1] / full_width - row_mean * row_mean
        inv_std = lax.rsqrt(variance + EPSILON)
        centered = (values32 - row_mean) * inv_std
        normed = (centered * gain_row).astype(jnp.bfloat16)
        values = jnp.dot(
            lax.all_gather(normed, "tp", axis=1, tiled=True),
            value_local,
            preferred_element_type=jnp.float32,
        )
        return (centered, inv_std, normed, values.astype(jnp.bfloat16))

    def attention_probs(normed):
        queries = normed.reshape(token_rows, -1, HEAD)
        keys_in = (
            (normed.astype(jnp.float32) * key_row)
            .astype(jnp.bfloat16)
            .reshape(token_rows, -1, HEAD)
        )
        scores = jnp.einsum(
            "qhd,khd->hqk", queries, keys_in, preferred_element_type=jnp.float32
        ) / math.sqrt(HEAD)
        causal = jnp.tril(jnp.ones((token_rows, token_rows), dtype=bool))
        scores = jnp.where(causal[None], scores, -1e30)
        probs = jax.nn.softmax(scores, axis=-1)
        return (queries, keys_in, probs)

    fwd_input = carried[0]
    grad_input = pending[0]
    forward_list = []
    backward_list = []
    for step_index in range(inputs.shape[0] + 1):
        if step_index > 0:
            received = from_behind(forward_list[-1], "section", 1)
            fwd_input = jnp.where(section_index == 0, inputs[step_index - 1], received)
            received_grad = from_behind(backward_list[-1], "section", -1)
            grad_input = jnp.where(
                section_index == section_count - 1, cotangents[step_index - 1], received_grad
            )
        forward_centered, forward_inv_std, forward_normed, forward_values = normalize(fwd_input)
        forward_queries, forward_keys_in, forward_probs = attention_probs(forward_normed)
        forward_weights_bf = forward_probs.astype(jnp.bfloat16)
        mixed = jnp.einsum(
            "hqk,khd->qhd",
            forward_weights_bf,
            forward_values.reshape(token_rows, -1, HEAD),
            preferred_element_type=jnp.float32,
        ).astype(jnp.bfloat16)
        partial_out = jnp.dot(
            mixed.reshape(token_rows, feat_width), out_local, preferred_element_type=jnp.float32
        )
        head_sum = lax.psum_scatter(
            partial_out.astype(jnp.bfloat16), "tp", scatter_dimension=1, tiled=True
        ).astype(jnp.float32)
        forward_list.append((fwd_input.astype(jnp.float32) + head_sum).astype(jnp.bfloat16))
        sending = held_blocks[stash_plan[mirror, step_index, 1]]
        pieces = sending.reshape(section_count, piece_rows, feat_width)
        spread = lax.all_to_all(pieces, "section", split_axis=0, concat_axis=0, tiled=True)
        spread = spread[::-1]
        sending = lax.all_to_all(
            spread, "section", split_axis=0, concat_axis=0, tiled=True
        ).reshape(token_rows, feat_width)
        side = stash_plan[section_index, step_index, 0]
        own_block = held_blocks[stash_plan[section_index, step_index, 1]]
        backward_centered, backward_inv_std, backward_normed, backward_values = normalize(
            jnp.where(side == 0, own_block, sending)
        )
        backward_queries, backward_keys_in, backward_probs = attention_probs(backward_normed)
        weights_bf = backward_probs.astype(jnp.bfloat16)
        grad_attn = lax.dot_general(
            lax.all_gather(grad_input, "tp", axis=1, tiled=True),
            out_local,
            (((1,), (1,)), ((), ())),
            preferred_element_type=jnp.float32,
        )
        grad_attn = grad_attn.astype(jnp.bfloat16).reshape(token_rows, -1, HEAD)
        values3 = backward_values.reshape(token_rows, -1, HEAD)
        grad_probs = jnp.einsum(
            "qhd,khd->hqk", grad_attn, values3, preferred_element_type=jnp.float32
        )
        grad_values = jnp.einsum(
            "hqk,qhd->khd", weights_bf, grad_attn, preferred_element_type=jnp.float32
        ).astype(jnp.bfloat16)
        grad_scores = (
            backward_probs
            * (grad_probs - jnp.sum(grad_probs * backward_probs, -1, keepdims=True))
            / math.sqrt(HEAD)
        ).astype(jnp.bfloat16)
        grad_query = jnp.einsum(
            "hqk,khd->qhd", grad_scores, backward_keys_in, preferred_element_type=jnp.float32
        )
        grad_keys = jnp.einsum(
            "hqk,qhd->khd", grad_scores, backward_queries, preferred_element_type=jnp.float32
        )
        grad_direct = (
            grad_query.reshape(token_rows, -1) + grad_keys.reshape(token_rows, -1) * key_row
        )
        partial_in = lax.dot_general(
            grad_values.reshape(token_rows, feat_width),
            value_local,
            (((1,), (1,)), ((), ())),
            preferred_element_type=jnp.float32,
        )
        grad_normed = (
            lax.psum_scatter(
                partial_in.astype(jnp.bfloat16), "tp", scatter_dimension=1, tiled=True
            ).astype(jnp.float32)
            + grad_direct
        )
        grad_scaled = grad_normed * gain_row
        backward_totals = lax.psum(
            (
                jnp.sum(grad_scaled, -1, keepdims=True),
                jnp.sum(grad_scaled * backward_centered, -1, keepdims=True),
            ),
            "tp",
        )
        grad_block = backward_inv_std * (
            grad_scaled
            - backward_totals[0] / full_width
            - backward_centered * (backward_totals[1] / full_width)
        )
        backward_list.append((grad_input.astype(jnp.float32) + grad_block).astype(jnp.bfloat16))
    return (jnp.stack(forward_list, 0)[None], jnp.stack(backward_list, 0)[None])


def solution(mesh):
    return jax.shard_map(
        per_device,
        mesh=mesh,
        in_specs=(
            P(None, None, "tp"),
            P(None, None, "tp"),
            P("section", None, "tp"),
            P("section", None, "tp"),
            P("section", None, None, "tp"),
            P(),
            P("section", None),
            P("section", "tp"),
            P("section", None, "tp"),
            P("section", "tp", None),
        ),
        out_specs=(P("section", None, None, "tp"), P("section", None, None, "tp")),
        check_vma=False,
    )
```

profile of v0, /device:TPU:8, one launch (start us, length us, event | category | flops | bytes accessed | tf_op | source)
XLA Modules:
  0.0 1489.4 jit_solution(1038103647813009191)
XLA Ops:
  19.4 11.2 all_to_all.40
  30.5 9.8 all_to_all.41
  40.3 9.6 all_to_all.42
  108.9 24.7 %all-reduce.4 = (f32[128,1]{0,1:T(1,128)S(1)}, f32[128,1]{0,1:T(1,128)S(1)}) all-reduce(f32[128,1]{0,1:T(1,128)S(1)} %bitcast.472, f32[128,1]{0,1:T(1,128)S(1)} %bitcast.473), channel_id=1, replica_groups=mesh['section'=16,'tp'=8] {'tp'}, use_global_device_ids=true, to_apply=%region_31.32 | all-reduce | flops 256 | bytes 2048 | tf_op jit(solution)/shard_map/psum | solution.py:41
  137.1 7.5 fusion.141
  145.1 8.2 fusion.52
  153.6 28.6 %all-gather.22.cloned.1.call-done = bf16[128,6144]{1,0:T(8,128)(2,1)} async-done(((bf16[128,768]{1,0:T(8,128)(2,1)}), bf16[128,6144]{1,0:T(8,128)(2,1)}) %all-gather.22.cloned.1.call-update) | async-done | bytes 1572880 | tf_op jit(solution)/shard_map/all_gather | solution.py:51
  193.9 65.0 %reduce-scatter.17.cloned.1.call-done = bf16[128,768]{1,0:T(8,128)(2,1)} async-done(((bf16[128,6144]{1,0:T(8,128)(2,1)}), bf16[128,768]{1,0:T(8,128)(2,1)}) %reduce-scatter.17.cloned.1.call-update) | async-done | bytes 196624 | tf_op jit(solution)/shard_map/reduce_scatter | solution.py:149
  260.1 21.5 %all-reduce.3 = (f32[128,1]{0,1:T(1,128)S(1)}, f32[128,1]{0,1:T(1,128)S(1)}, f32[128,1]{0,1:T(1,128)S(1)}, f32[128,1]{0,1:T(1,128)S(1)}, f32[128,1]{0,1:T(1,128)S(1)}, /*index=5*/f32[128,1]{0,1:T(1,128)S(1)}) all-reduce(f32[128,1]{0,1:T(1,128)S(1)} %bitcast.461, ...), channel_id=1, replica_groups=mesh['section'=16,'tp'=8] {'tp'}, use_global_device_ids=true, to_apply=%region_3.0 | all-reduce | flops 768 | bytes 6144 | tf_op jit(solution)/shard_map/psum | solution.py:41
  292.0 46.8 %all-gather.24.cloned.1.call-done = bf16[128,6144]{1,0:T(8,128)(2,1)} async-done(((bf16[128,768]{1,0:T(8,128)(2,1)}), bf16[128,6144]{1,0:T(8,128)(2,1)}) %all-gather.24.cloned.1.call-update) | async-done | bytes 1572880 | tf_op jit(solution)/shard_map/all_gather | solution.py:115
  346.7 8.2 fusion.55
  355.0 36.2 %all-gather.26.cloned.1.call-done = bf16[128,6144]{1,0:T(8,128)(2,1)} async-done(((bf16[128,768]{1,0:T(8,128)(2,1)}), bf16[128,6144]{1,0:T(8,128)(2,1)}) %all-gather.26.cloned.1.call-update) | async-done | bytes 1572880 | tf_op jit(solution)/shard_map/all_gather | solution.py:51
  401.6 66.2 %reduce-scatter.19.cloned.1.call-done = bf16[128,768]{1,0:T(8,128)(2,1)} async-done(((bf16[128,6144]{1,0:T(8,128)(2,1)}), bf16[128,768]{1,0:T(8,128)(2,1)}) %reduce-scatter.19.cloned.1.call-update) | async-done | bytes 196624 | tf_op jit(solution)/shard_map/reduce_scatter | solution.py:149
  470.9 49.5 %all-gather.14.cloned.1.call-done = bf16[128,6144]{1,0:T(8,128)(2,1)} async-done(((bf16[128,768]{1,0:T(8,128)(2,1)}), bf16[128,6144]{1,0:T(8,128)(2,1)}) %all-gather.14.cloned.1.call-update) | async-done | bytes 1572880 | tf_op jit(solution)/shard_map/all_gather | solution.py:51
  532.7 73.0 %reduce-scatter.9.cloned.1.call-done = bf16[128,768]{1,0:T(8,128)(2,1)} async-done(((bf16[128,6144]{1,0:T(8,128)(2,1)}), bf16[128,768]{1,0:T(8,128)(2,1)}) %reduce-scatter.9.cloned.1.call-update) | async-done | bytes 196624 | tf_op jit(solution)/shard_map/reduce_scatter | solution.py:96
  615.7 21.3 %all-reduce.2 = (f32[128,1]{0,1:T(1,128)S(1)}, f32[128,1]{0,1:T(1,128)S(1)}, f32[128,1]{0,1:T(1,128)S(1)}, f32[128,1]{0,1:T(1,128)S(1)}, f32[128,1]{0,1:T(1,128)S(1)}, /*index=5*/f32[128,1]{0,1:T(1,128)S(1)}) all-reduce(f32[128,1]{0,1:T(1,128)S(1)} %bitcast.465, ...), channel_id=1, replica_groups=mesh['section'=16,'tp'=8] {'tp'}, use_global_device_ids=true, to_apply=%region_10.11 | all-reduce | flops 768 | bytes 6144 | tf_op jit(solution)/shard_map/psum | solution.py:41
  646.5 46.8 %all-gather.28.cloned.1.call-done = bf16[128,6144]{1,0:T(8,128)(2,1)} async-done(((bf16[128,768]{1,0:T(8,128)(2,1)}), bf16[128,6144]{1,0:T(8,128)(2,1)}) %all-gather.28.cloned.1.call-update) | async-done | bytes 1572880 | tf_op jit(solution)/shard_map/all_gather | solution.py:115
  701.3 8.2 fusion.58
  710.0 35.8 %all-gather.30.cloned.1.call-done = bf16[128,6144]{1,0:T(8,128)(2,1)} async-done(((bf16[128,768]{1,0:T(8,128)(2,1)}), bf16[128,6144]{1,0:T(8,128)(2,1)}) %all-gather.30.cloned.1.call-update) | async-done | bytes 1572880 | tf_op jit(solution)/shard_map/all_gather | solution.py:51
  752.7 69.8 %reduce-scatter.21.cloned.1.call-done = bf16[128,768]{1,0:T(8,128)(2,1)} async-done(((bf16[128,6144]{1,0:T(8,128)(2,1)}), bf16[128,768]{1,0:T(8,128)(2,1)}) %reduce-scatter.21.cloned.1.call-update) | async-done | bytes 196624 | tf_op jit(solution)/shard_map/reduce_scatter | solution.py:149
  826.1 48.8 %all-gather.16.cloned.1.call-done = bf16[128,6144]{1,0:T(8,128)(2,1)} async-done(((bf16[128,768]{1,0:T(8,128)(2,1)}), bf16[128,6144]{1,0:T(8,128)(2,1)}) %all-gather.16.cloned.1.call-update) | async-done | bytes 1572880 | tf_op jit(solution)/shard_map/all_gather | solution.py:51
  887.3 73.1 %reduce-scatter.11.cloned.1.call-done = bf16[128,768]{1,0:T(8,128)(2,1)} async-done(((bf16[128,6144]{1,0:T(8,128)(2,1)}), bf16[128,768]{1,0:T(8,128)(2,1)}) %reduce-scatter.11.cloned.1.call-update) | async-done | bytes 196624 | tf_op jit(solution)/shard_map/reduce_scatter | solution.py:96
  970.3 21.3 %all-reduce.1 = (f32[128,1]{0,1:T(1,128)S(1)}, f32[128,1]{0,1:T(1,128)S(1)}, f32[128,1]{0,1:T(1,128)S(1)}, f32[128,1]{0,1:T(1,128)S(1)}, f32[128,1]{0,1:T(1,128)S(1)}, /*index=5*/f32[128,1]{0,1:T(1,128)S(1)}) all-reduce(f32[128,1]{0,1:T(1,128)S(1)} %bitcast.467, ...), channel_id=1, replica_groups=mesh['section'=16,'tp'=8] {'tp'}, use_global_device_ids=true, to_apply=%region_17.18 | all-reduce | flops 768 | bytes 6144 | tf_op jit(solution)/shard_map/psum | solution.py:41
  1001.3 46.6 %all-gather.32.cloned.1.call-done = bf16[128,6144]{1,0:T(8,128)(2,1)} async-done(((bf16[128,768]{1,0:T(8,128)(2,1)}), bf16[128,6144]{1,0:T(8,128)(2,1)}) %all-gather.32.cloned.1.call-update) | async-done | bytes 1572880 | tf_op jit(solution)/shard_map/all_gather | solution.py:115
  1055.8 8.2 fusion.61
  1064.1 36.2 %all-gather.34.cloned.1.call-done = bf16[128,6144]{1,0:T(8,128)(2,1)} async-done(((bf16[128,768]{1,0:T(8,128)(2,1)}), bf16[128,6144]{1,0:T(8,128)(2,1)}) %all-gather.34.cloned.1.call-update) | async-done | bytes 1572880 | tf_op jit(solution)/shard_map/all_gather | solution.py:51
  1110.7 66.2 %reduce-scatter.23.cloned.1.call-done = bf16[128,768]{1,0:T(8,128)(2,1)} async-done(((bf16[128,6144]{1,0:T(8,128)(2,1)}), bf16[128,768]{1,0:T(8,128)(2,1)}) %reduce-scatter.23.cloned.1.call-update) | async-done | bytes 196624 | tf_op jit(solution)/shard_map/reduce_scatter | solution.py:149
  1180.5 48.8 %all-gather.18.cloned.1.call-done = bf16[128,6144]{1,0:T(8,128)(2,1)} async-done(((bf16[128,768]{1,0:T(8,128)(2,1)}), bf16[128,6144]{1,0:T(8,128)(2,1)}) %all-gather.18.cloned.1.call-update) | async-done | bytes 1572880 | tf_op jit(solution)/shard_map/all_gather | solution.py:51
  1241.6 73.1 %reduce-scatter.13.cloned.1.call-done = bf16[128,768]{1,0:T(8,128)(2,1)} async-done(((bf16[128,6144]{1,0:T(8,128)(2,1)}), bf16[128,768]{1,0:T(8,128)(2,1)}) %reduce-scatter.13.cloned.1.call-update) | async-done | bytes 196624 | tf_op jit(solution)/shard_map/reduce_scatter | solution.py:96
  1324.7 21.3 %all-reduce = (f32[128,1]{0,1:T(1,128)S(1)}, f32[128,1]{0,1:T(1,128)S(1)}, f32[128,1]{0,1:T(1,128)S(1)}, f32[128,1]{0,1:T(1,128)S(1)}) all-reduce(f32[128,1]{0,1:T(1,128)S(1)} %bitcast.469, f32[128,1]{0,1:T(1,128)S(1)} %bitcast.468, f32[128,1]{0,1:T(1,128)S(1)} %bitcast.459, ...), channel_id=1, replica_groups=mesh['section'=16,'tp'=8] {'tp'}, use_global_device_ids=true, to_apply=%region_24.25 | all-reduce | flops 512 | bytes 4096 | tf_op jit(solution)/shard_map/psum | solution.py:41
  1348.6 46.3 %all-gather.20.cloned.1.call-done = bf16[128,6144]{1,0:T(8,128)(2,1)} async-done(((bf16[128,768]{1,0:T(8,128)(2,1)}), bf16[128,6144]{1,0:T(8,128)(2,1)}) %all-gather.20.cloned.1.call-update) | async-done | bytes 1572880 | tf_op jit(solution)/shard_map/all_gather | solution.py:51
  1408.5 71.9 %reduce-scatter.15.cloned.1.call-done = bf16[128,768]{1,0:T(8,128)(2,1)} async-done(((bf16[128,6144]{1,0:T(8,128)(2,1)}), bf16[128,768]{1,0:T(8,128)(2,1)}) %reduce-scatter.15.cloned.1.call-update) | async-done | bytes 196624 | tf_op jit(solution)/shard_map/reduce_scatter | solution.py:96
  (233 shorter events, 246.7 us)
Async XLA Ops:
  7.2 130.0 %all-gather.36.cloned.1.call-start = ((), (), s32[]{:S(2)}) async-start(), calls=%async_computation.35 | async-start | bytes 1769472 | tf_op jit(solution)/shard_map/all_gather | solution.py:115
  49.9 10.6 all-to-all-start
  60.5 10.6 all-to-all-start.7
  71.1 10.6 all-to-all-start.5
  81.7 10.6 all-to-all-start.3
  92.3 15.6 %all-to-all-start.1 = ((bf16[16,8,768]{2,1,0:T(8,128)(2,1)}), bf16[16,8,768]{2,1,0:T(8,128)(2,1)S(1)}, u32[]{:S(2)}, u32[]{:S(2)}) async-start(bf16[16,8,768]{2,1,0:T(8,128)(2,1)} %rev.12), calls=%async_computation.5 | async-start | bytes 393216 | tf_op jit(solution)/shard_map/all_to_all | solution.py:104
  97.7 84.4 %all-gather.22.cloned.1.call-start = ((), (), s32[]{:S(2)}) async-start(), calls=%async_computation.25 | async-start | bytes 1769472 | tf_op jit(solution)/shard_map/all_gather | solution.py:51
  134.5 124.4 %reduce-scatter.17.cloned.1.call-start = ((), (), s32[]{:S(2)}) async-start(), calls=%async_computation.24 | async-start | bytes 1769472 | tf_op jit(solution)/shard_map/reduce_scatter | solution.py:149
  153.3 185.5 %all-gather.24.cloned.1.call-start = ((), (), s32[]{:S(2)}) async-start(), calls=%async_computation.26 | async-start | bytes 1769472 | tf_op jit(solution)/shard_map/all_gather | solution.py:115
  282.7 5.1 collective-permute-start.3
  289.5 101.7 %all-gather.26.cloned.1.call-start = ((), (), s32[]{:S(2)}) async-start(), calls=%async_computation.28 | async-start | bytes 1769472 | tf_op jit(solution)/shard_map/all_gather | solution.py:51
  290.4 177.4 %reduce-scatter.19.cloned.1.call-start = ((), (), s32[]{:S(2)}) async-start(), calls=%async_computation.27 | async-start | bytes 1769472 | tf_op jit(solution)/shard_map/reduce_scatter | solution.py:149
  354.9 165.4 %all-gather.14.cloned.1.call-start = ((), (), s32[]{:S(2)}) async-start(), calls=%async_computation.16 | async-start | bytes 1769472 | tf_op jit(solution)/shard_map/all_gather | solution.py:51
  469.7 136.1 %reduce-scatter.9.cloned.1.call-start = ((), (), s32[]{:S(2)}) async-start(), calls=%async_computation.17 | async-start | bytes 1769472 | tf_op jit(solution)/shard_map/reduce_scatter | solution.py:96
  532.6 112.3 %copy-start.7 = (bf16[1,1,128,768]{3,2,1,0:T(8,128)(2,1)S(1)}, bf16[1,1,128,768]{3,2,1,0:T(8,128)(2,1)}, u32[]{:S(2)}) copy-start(bf16[1,1,128,768]{3,2,1,0:T(8,128)(2,1)} %get-tuple-element.72) | copy-start | bytes 589828
  532.7 160.7 %all-gather.28.cloned.1.call-start = ((), (), s32[]{:S(2)}) async-start(), calls=%async_computation.29 | async-start | bytes 1769472 | tf_op jit(solution)/shard_map/all_gather | solution.py:115
  606.7 7.9 collective-permute-start
  637.2 5.1 collective-permute-start.4
  644.0 101.7 %all-gather.30.cloned.1.call-start = ((), (), s32[]{:S(2)}) async-start(), calls=%async_computation.31 | async-start | bytes 1769472 | tf_op jit(solution)/shard_map/all_gather | solution.py:51
  644.9 177.5 %reduce-scatter.21.cloned.1.call-start = ((), (), s32[]{:S(2)}) async-start(), calls=%async_computation.30 | async-start | bytes 1769472 | tf_op jit(solution)/shard_map/reduce_scatter | solution.py:149
  709.5 165.4 %all-gather.16.cloned.1.call-start = ((), (), s32[]{:S(2)}) async-start(), calls=%async_computation.18 | async-start | bytes 1769472 | tf_op jit(solution)/shard_map/all_gather | solution.py:51
  824.4 135.9 %reduce-scatter.11.cloned.1.call-start = ((), (), s32[]{:S(2)}) async-start(), calls=%async_computation.19 | async-start | bytes 1769472 | tf_op jit(solution)/shard_map/reduce_scatter | solution.py:96
  887.2 160.7 %all-gather.32.cloned.1.call-start = ((), (), s32[]{:S(2)}) async-start(), calls=%async_computation.32 | async-start | bytes 1769472 | tf_op jit(solution)/shard_map/all_gather | solution.py:115
  961.3 7.9 collective-permute-start.1
  991.8 5.1 collective-permute-start.5
  998.6 101.7 %all-gather.34.cloned.1.call-start = ((), (), s32[]{:S(2)}) async-start(), calls=%async_computation.34 | async-start | bytes 1769472 | tf_op jit(solution)/shard_map/all_gather | solution.py:51
  999.5 177.4 %reduce-scatter.23.cloned.1.call-start = ((), (), s32[]{:S(2)}) async-start(), calls=%async_computation.33 | async-start | bytes 1769472 | tf_op jit(solution)/shard_map/reduce_scatter | solution.py:149
  1064.0 165.2 %all-gather.18.cloned.1.call-start = ((), (), s32[]{:S(2)}) async-start(), calls=%async_computation.20 | async-start | bytes 1769472 | tf_op jit(solution)/shard_map/all_gather | solution.py:51
  1178.8 135.9 %reduce-scatter.13.cloned.1.call-start = ((), (), s32[]{:S(2)}) async-start(), calls=%async_computation.21 | async-start | bytes 1769472 | tf_op jit(solution)/shard_map/reduce_scatter | solution.py:96
  1241.6 153.3 %all-gather.20.cloned.1.call-start = ((), (), s32[]{:S(2)}) async-start(), calls=%async_computation.22 | async-start | bytes 1769472 | tf_op jit(solution)/shard_map/all_gather | solution.py:51
  1315.7 7.9 collective-permute-start.2
  1346.9 133.5 %reduce-scatter.15.cloned.1.call-start = ((), (), s32[]{:S(2)}) async-start(), calls=%async_computation.23 | async-start | bytes 1769472 | tf_op jit(solution)/shard_map/reduce_scatter | solution.py:96
  (11 other events, 685.4 us)
Sparse Core Ops, SparseCore 0:
  10.4 55.3 all-gather.35
  134.6 47.4 all-gather.21
  185.9 72.9 reduce-scatter.16
  289.6 49.1 all-gather.23
  341.6 49.5 all-gather.25
  394.8 72.9 reduce-scatter.18
  470.7 49.6 all-gather.13
  532.8 72.9 reduce-scatter.8
  644.1 49.2 all-gather.27
  696.1 49.5 all-gather.29
  749.5 72.9 reduce-scatter.20
  825.2 49.5 all-gather.15
  887.4 72.9 reduce-scatter.10
  998.7 49.1 all-gather.31
  1050.7 49.5 all-gather.33
  1103.9 72.9 reduce-scatter.22
  1179.7 49.5 all-gather.17
  1241.7 72.9 reduce-scatter.12
  1347.0 47.8 all-gather.19
  1407.3 72.9 reduce-scatter.14
where the time goes:
time: 1500 us; the launch traced here: 1490 us
  waiting for transfers between devices  1070 us (71%)
  matrix products  148 us (10%)
  blocking collectives  141 us (9%)
  starting transfers between devices  40.7 us (3%)
  between operations  33.2 us (2%)
  other arithmetic  30.9 us (2%)
  local copies, waits for them, and re-layouts  21.9 us (1%)
    all_gather x8, waiting for transfers between devices, normalize(): lax.all_gather(normed, 'tp', axis=1, tiled=True)  330 us
    reduce_scatter x4, waiting for transfers between devices, per_device(): lax.psum_scatter(partial_out.astype(jnp.bfloat16), 'tp', scatter_dimensio...  291 us
    reduce_scatter x4, waiting for transfers between devices, per_device(): lax.psum_scatter(partial_in.astype(jnp.bfloat16), 'tp', scatter_dimension...  267 us
    all_gather x4, waiting for transfers between devices, per_device(): lax.all_gather(grad_input, 'tp', axis=1, tiled=True)  140 us
    psum x5, blocking collectives, normalize(): lax.psum((jnp.sum(values32, -1, keepdims=True), jnp.sum(values32 * values...  110 us
    dot_general x8, matrix products, normalize(): jnp.dot(lax.all_gather(normed, 'tp', axis=1, tiled=True), value_local, pr...  44.4 us
    dot_general x4, matrix products, per_device(): lax.dot_general(grad_values.reshape(token_rows, feat_width), value_local,...  32.8 us
    all_to_all x3, blocking collectives, per_device(): lax.all_to_all(pieces, 'section', split_axis=0, concat_axis=0, tiled=True)  30.6 us
  transfers between devices with their start and end apart: 31, of which 29 were waited for; matrix products, arithmetic and copies ran while one was open for 9% of the time, Pallas kernels for 0%

commit v1 on v0

v1 whole, which is shorter than its diff:
```python
import math

import jax
import jax.numpy as jnp
from jax import lax
from jax.experimental import pallas as pl
from jax.experimental.pallas import tpu as pltpu
from jax.sharding import PartitionSpec as P

HEAD = 128
EPSILON = 1e-05
RINGX = 4
PEERS = 8
BF16 = jnp.bfloat16
F32 = jnp.float32
NT = (((1,), (1,)), ((), ()))
NN = (((1,), (0,)), ((), ()))
TN = (((0,), (0,)), ((), ()))
VMEM = pl.BlockSpec(memory_space=pltpu.VMEM)
SMEM = pl.BlockSpec(memory_space=pltpu.SMEM)


def params():
    return pltpu.CompilerParams(
        dimension_semantics=("arbitrary",), vmem_limit_bytes=24 * 1024 * 1024
    )


def cost(flops, nbytes):
    return pl.CostEstimate(flops=flops, bytes_accessed=nbytes, transcendentals=0)


def place(i, dx, dz):
    return ((i // 2 + dx) % RINGX) * 2 + ((i % 2) ^ dz)


def shift(array, dx, dz):
    return lax.ppermute(array, "tp", [(i, place(i, dx, dz)) for i in range(PEERS)])


def from_behind(array, by):
    peers = lax.axis_size("section")
    pairs = [(i, i + by) for i in range(peers) if 0 <= i + by < peers]
    return lax.ppermute(array, "section", pairs)


def gather(own, axis):
    partner = shift(own, 0, 1)
    pair = jnp.stack([own, partner])
    behind = shift(pair, -1, 0)
    ahead = shift(pair, 1, 0)
    half = pair.shape[axis] // 2
    first = shift(lax.slice_in_dim(behind, 0, half, axis=axis), -1, 0)
    second = shift(lax.slice_in_dim(ahead, half, 2 * half, axis=axis), 1, 0)
    return own, partner, behind, first, second, ahead


def scatter_sum(here, far_first, far_second, plus, minus, axis):
    half = far_first.shape[axis]
    got_first = shift(far_first, 1, 0)
    got_second = shift(far_second, -1, 0)

    def add(a, b):
        return (a.astype(F32) + b.astype(F32)).astype(BF16)

    plus = jnp.concatenate(
        [
            add(lax.slice_in_dim(plus, 0, half, axis=axis), got_first),
            lax.slice_in_dim(plus, half, 2 * half, axis=axis),
        ],
        axis,
    )
    minus = jnp.concatenate(
        [
            lax.slice_in_dim(minus, 0, half, axis=axis),
            add(lax.slice_in_dim(minus, half, 2 * half, axis=axis), got_second),
        ],
        axis,
    )
    got_plus = shift(plus, 1, 0)
    got_minus = shift(minus, -1, 0)
    total = here.astype(F32) + got_plus.astype(F32) + got_minus.astype(F32)
    return total[0] + shift(total[1].astype(BF16), 0, 1).astype(F32)


def softmax_scores(queries, keys, tokens):
    scores = lax.dot_general(queries, keys, NT, preferred_element_type=F32) / math.sqrt(HEAD)
    rows = lax.broadcasted_iota(jnp.int32, (tokens, tokens), 0)
    columns = lax.broadcasted_iota(jnp.int32, (tokens, tokens), 1)
    scores = jnp.where(columns <= rows, scores, -1e30)
    raised = jnp.exp(scores - jnp.max(scores, -1, keepdims=True))
    return raised / jnp.sum(raised, -1, keepdims=True)


def layer_body(stashed, tokens, width, *refs):
    idx, own, partner, plus, far_first, far_second, minus, gain, key_row, weight = refs[:10]
    if stashed:
        out_values, out_probs, out_normed, out_centered, out_inv = refs[10:15]
    else:
        (out_mixed,) = refs[10:11]
    pieces, total, normed_own, mean_ref, inv_ref = refs[-5:]
    step = pl.program_id(0)
    half = tokens // 2
    full = width * PEERS

    @pl.when(step == 0)
    def _():
        pieces[0] = own[...]
        pieces[1] = partner[...]
        pieces[2:4] = plus[...]
        pieces[4:6, :half] = far_first[...]
        pieces[4:6, half:] = far_second[...]
        pieces[6:8] = minus[...]
        sums = jnp.zeros((tokens, HEAD), F32)
        squares = jnp.zeros((tokens, HEAD), F32)
        for r in range(PEERS):
            for c in range(width // HEAD):
                x = pieces[r, :, c * HEAD : (c + 1) * HEAD].astype(F32)
                sums += x
                squares += x * x
        mean = jnp.sum(sums, -1, keepdims=True) / full
        variance = jnp.sum(squares, -1, keepdims=True) / full - mean * mean
        mean_ref[...] = jnp.broadcast_to(mean, (tokens, HEAD))
        inv_ref[...] = jnp.broadcast_to(lax.rsqrt(variance + EPSILON), (tokens, HEAD))
        total[...] = jnp.zeros_like(total)

    centered = (pieces[step].astype(F32) - mean_ref[:, :1]) * inv_ref[:, :1]
    normed = (centered * gain[0]).astype(BF16)

    @pl.when(step == 0)
    def _():
        normed_own[...] = normed

    total[...] += lax.dot_general(normed, weight[...], NN, preferred_element_type=F32)

    if stashed:
        share = tokens // PEERS
        rows = pl.ds(pl.multiple_of(idx[0] * share, share), share)
        out_centered[...] = (pieces[step, rows, :].astype(F32) - mean_ref[rows, :1]) * inv_ref[
            rows, :1
        ]

        @pl.when(step == 0)
        def _():
            out_inv[...] = inv_ref[rows, :]

    @pl.when(step == PEERS - 1)
    def _():
        values = total[...].astype(BF16)
        if stashed:
            out_values[...] = values
            out_normed[...] = normed_own[...]
        for h in range(width // HEAD):
            part = slice(h * HEAD, (h + 1) * HEAD)
            queries = normed_own[:, part]
            keys = (queries.astype(F32) * key_row[:, part]).astype(BF16)
            probs = softmax_scores(queries, keys, tokens)
            if stashed:
                out_probs[h] = probs
            else:
                out_mixed[:, part] = lax.dot_general(
                    probs.astype(BF16), values[:, part], NN, preferred_element_type=F32
                ).astype(BF16)


def layer_call(stashed, idx, pieces, gain, key_row, weight):
    tokens, width = pieces[0].shape
    full = width * PEERS
    share = tokens // PEERS
    if stashed:
        out_shape = (
            jax.ShapeDtypeStruct((tokens, width), BF16),
            jax.ShapeDtypeStruct((width // HEAD, tokens, tokens), F32),
            jax.ShapeDtypeStruct((tokens, width), BF16),
            jax.ShapeDtypeStruct((share, full), F32),
            jax.ShapeDtypeStruct((share, HEAD), F32),
        )
        out_specs = (
            pl.BlockSpec((tokens, width), lambda r, idx: (0, 0)),
            pl.BlockSpec((width // HEAD, tokens, tokens), lambda r, idx: (0, 0, 0)),
            pl.BlockSpec((tokens, width), lambda r, idx: (0, 0)),
            pl.BlockSpec((share, width), lambda r, idx: (0, idx[r])),
            pl.BlockSpec((share, HEAD), lambda r, idx: (0, 0)),
        )
    else:
        out_shape = jax.ShapeDtypeStruct((tokens, width), BF16)
        out_specs = pl.BlockSpec((tokens, width), lambda r, idx: (0, 0))

    def body(*refs):
        layer_body(stashed, tokens, width, *refs)

    def whole(array):
        zeros = (0,) * array.ndim
        return pl.BlockSpec(array.shape, lambda r, idx: zeros)

    return pl.pallas_call(
        body,
        out_shape=out_shape,
        grid_spec=pltpu.PrefetchScalarGridSpec(
            num_scalar_prefetch=1,
            grid=(PEERS,),
            in_specs=[whole(p) for p in pieces]
            + [
                pl.BlockSpec((1, 1, width), lambda r, idx: (idx[r], 0, 0)),
                whole(key_row),
                pl.BlockSpec((width, width), lambda r, idx: (idx[r], 0)),
            ],
            out_specs=out_specs,
            scratch_shapes=[
                pltpu.VMEM((PEERS, tokens, width), BF16),
                pltpu.VMEM((tokens, width), F32),
                pltpu.VMEM((tokens, width), BF16),
                pltpu.VMEM((tokens, HEAD), F32),
                pltpu.VMEM((tokens, HEAD), F32),
            ],
        ),
        compiler_params=params(),
        cost_estimate=cost(2 * tokens * full * width, 2 * full * width),
        name="stash_layer" if stashed else "mix_layer",
    )(idx, *pieces, gain, key_row, weight)


def far_call(idx, mixed, weight):
    tokens, width = mixed.shape

    def body(idx, mixed, weight, first, second):
        product = lax.dot_general(
            mixed[...], weight[...], NN, preferred_element_type=F32
        ).astype(BF16)
        first[0] = product[: tokens // 2]
        second[0] = product[tokens // 2 :]

    half = pl.BlockSpec((1, tokens // 2, width), lambda r, idx: (r, 0, 0))
    return pl.pallas_call(
        body,
        out_shape=[jax.ShapeDtypeStruct((2, tokens // 2, width), BF16)] * 2,
        grid_spec=pltpu.PrefetchScalarGridSpec(
            num_scalar_prefetch=1,
            grid=(2,),
            in_specs=[
                pl.BlockSpec((tokens, width), lambda r, idx: (0, 0)),
                pl.BlockSpec((width, width), lambda r, idx: (0, idx[4 + r])),
            ],
            out_specs=[half, half],
        ),
        compiler_params=params(),
        cost_estimate=cost(4 * tokens * width * width, 4 * width * width),
        name="project_far",
    )(idx, mixed, weight)


def near_call(idx, mixed, weight):
    tokens, width = mixed.shape

    def order(r, idx):
        return idx[lax.select(r < 2, r + 2, lax.select(r < 4, r + 4, r - 4))]

    def body(idx, mixed, weight, plus, minus, here):
        step = pl.program_id(0)
        product = lax.dot_general(
            mixed[...], weight[...], NN, preferred_element_type=F32
        ).astype(BF16)

        @pl.when(step < 2)
        def _():
            plus[0] = product

        @pl.when((step >= 2) & (step < 4))
        def _():
            minus[0] = product

        @pl.when(step >= 4)
        def _():
            here[0] = product

    def pair(first):
        return pl.BlockSpec(
            (1, tokens, width), lambda r, idx: (jnp.clip(r - first, 0, 1), 0, 0)
        )

    return pl.pallas_call(
        body,
        out_shape=[jax.ShapeDtypeStruct((2, tokens, width), BF16)] * 3,
        grid_spec=pltpu.PrefetchScalarGridSpec(
            num_scalar_prefetch=1,
            grid=(6,),
            in_specs=[
                pl.BlockSpec((tokens, width), lambda r, idx: (0, 0)),
                pl.BlockSpec((width, width), lambda r, idx: (0, order(r, idx))),
            ],
            out_specs=[pair(0), pair(2), pair(4)],
        ),
        compiler_params=params(),
        cost_estimate=cost(12 * tokens * width * width, 12 * width * width),
        name="project_near",
    )(idx, mixed, weight)


def attention_grad_call(idx, pieces, stashed, key_row, weight):
    share, full = pieces[0].shape
    tokens = share * PEERS
    width = full // PEERS
    values, probs, normed = stashed

    def body(
        idx, own, partner, plus, far_first, far_second, minus, values, probs, normed, key_row,
        weight, out_values, out_direct, grads, total, sort_values, sort_direct,
    ):
        step = pl.program_id(0)

        def rows(r):
            return pl.ds(pl.multiple_of(idx[r] * share, share), share)

        @pl.when(step == 0)
        def _():
            grads[rows(0)] = own[...]
            grads[rows(1)] = partner[...]
            for dz in range(2):
                grads[rows(2 + dz)] = plus[dz]
                grads[rows(4 + dz), : full // 2] = far_first[dz]
                grads[rows(4 + dz), full // 2 :] = far_second[dz]
                grads[rows(6 + dz)] = minus[dz]
            total[...] = jnp.zeros_like(total)

        columns = pl.ds(pl.multiple_of(step * width, HEAD), width)
        total[...] += lax.dot_general(
            grads[:, columns], weight[...], NT, preferred_element_type=F32
        )

        @pl.when(step == PEERS - 1)
        def _():
            for h in range(width // HEAD):
                part = slice(h * HEAD, (h + 1) * HEAD)
                grad_mixed = total[:, part].astype(BF16)
                weights = probs[h]
                grad_probs = lax.dot_general(
                    grad_mixed, values[:, part], NT, preferred_element_type=F32
                )
                grad_values = lax.dot_general(
                    weights.astype(BF16), grad_mixed, TN, preferred_element_type=F32
                )
                grad_scores = (
                    weights
                    * (grad_probs - jnp.sum(grad_probs * weights, -1, keepdims=True))
                    / math.sqrt(HEAD)
                ).astype(BF16)
                queries = normed[:, part]
                keys = (queries.astype(F32) * key_row[:, part]).astype(BF16)
                grad_query = lax.dot_general(grad_scores, keys, NN, preferred_element_type=F32)
                grad_keys = lax.dot_general(grad_scores, queries, TN, preferred_element_type=F32)
                sort_values[:, part] = grad_values.astype(BF16)
                sort_direct[:, part] = grad_query + grad_keys * key_row[:, part]
            for r in range(PEERS):
                out_values[r * share : (r + 1) * share] = sort_values[rows(r)]
                out_direct[r * share : (r + 1) * share] = sort_direct[rows(r)]

    def whole(array):
        zeros = (0,) * array.ndim
        return pl.BlockSpec(array.shape, lambda r, idx: zeros)

    result = pl.BlockSpec((tokens, width), lambda r, idx: (0, 0))
    return pl.pallas_call(
        body,
        out_shape=(
            jax.ShapeDtypeStruct((tokens, width), BF16),
            jax.ShapeDtypeStruct((tokens, width), F32),
        ),
        grid_spec=pltpu.PrefetchScalarGridSpec(
            num_scalar_prefetch=1,
            grid=(PEERS,),
            in_specs=[whole(p) for p in pieces]
            + [whole(values), whole(probs), whole(normed), whole(key_row)]
            + [pl.BlockSpec((width, width), lambda r, idx: (0, r))],
            out_specs=(result, result),
            scratch_shapes=[
                pltpu.VMEM((tokens, full), BF16),
                pltpu.VMEM((tokens, width), F32),
                pltpu.VMEM((tokens, width), BF16),
                pltpu.VMEM((tokens, width), F32),
            ],
        ),
        compiler_params=params(),
        cost_estimate=cost(2 * tokens * full * width, 2 * full * width),
        name="attention_grad",
    )(idx, *pieces, values, probs, normed, key_row, weight)


def back_project_call(idx, grad_values, direct, weight):
    tokens, width = grad_values.shape
    full = width * PEERS
    share = tokens // PEERS

    def body(idx, grad_values, direct, weight, here, plus, far_first, far_second, minus):
        step = pl.program_id(0)
        product = lax.dot_general(
            grad_values[...], weight[...], NT, preferred_element_type=F32
        )
        mine = (step == idx[0]).astype(F32)
        product = (product + direct[...] * mine).astype(BF16)

        def piece(r):
            return product[r * share : (r + 1) * share]

        for dz in range(2):
            here[dz] = piece(dz)
            plus[dz] = piece(2 + dz)
            minus[dz] = piece(6 + dz)

        @pl.when(step < PEERS // 2)
        def _():
            for dz in range(2):
                far_first[dz] = piece(4 + dz)

        @pl.when(step >= PEERS // 2)
        def _():
            for dz in range(2):
                far_second[dz] = piece(4 + dz)

    part = pl.BlockSpec((2, share, width), lambda c, idx: (0, 0, c))
    return pl.pallas_call(
        body,
        out_shape=[
            jax.ShapeDtypeStruct((2, share, full // (2 if k in (2, 3) else 1)), BF16)
            for k in range(5)
        ],
        grid_spec=pltpu.PrefetchScalarGridSpec(
            num_scalar_prefetch=1,
            grid=(PEERS,),
            in_specs=[
                pl.BlockSpec((tokens, width), lambda c, idx: (0, 0)),
                pl.BlockSpec((tokens, width), lambda c, idx: (0, 0)),
                pl.BlockSpec((width, width), lambda c, idx: (c, 0)),
            ],
            out_specs=[
                part,
                part,
                pl.BlockSpec((2, share, width), lambda c, idx: (0, 0, jnp.minimum(c, 3))),
                pl.BlockSpec((2, share, width), lambda c, idx: (0, 0, jnp.maximum(c - 4, 0))),
                part,
            ],
        ),
        compiler_params=params(),
        cost_estimate=cost(2 * tokens * full * width, 2 * full * width),
        name="back_project",
    )(idx, grad_values, direct, weight)


def to_tokens(array):
    return lax.all_to_all(array, "tp", split_axis=1, concat_axis=2, tiled=True)


def to_features(array):
    return lax.all_to_all(array, "tp", split_axis=2, concat_axis=1, tiled=True)


def per_device(
    inputs, cotangents, carried, pending, stash, stash_plan, gain, key_gain, w_value, w_out
):
    steps = inputs.shape[0] + 1
    width = key_gain.shape[-1]
    full = gain.shape[-1]
    me = lax.axis_index("tp")
    idx = jnp.stack([place(me, r // 2, r % 2) for r in range(PEERS)]).astype(jnp.int32)
    section = lax.axis_index("section")
    sections = lax.axis_size("section")
    mirror = sections - 1 - section
    gain_full = gain[0]
    gain_blocks = gain[0].reshape(PEERS, 1, width)
    value_local = w_value[0]
    out_local = w_out[0]
    held = stash[0]

    def stashed_inputs(first, last):
        sending = jnp.stack([held[stash_plan[mirror, t, 1]] for t in range(first, last)])
        got = lax.ppermute(sending, "section", [(i, sections - 1 - i) for i in range(sections)])
        return [
            jnp.where(
                stash_plan[section, t, 0] == 0, held[stash_plan[section, t, 1]], got[t - first]
            )
            for t in range(first, last)
        ]

    stash_in = stashed_inputs(0, 1) + stashed_inputs(1, steps)
    grad_tokens = to_tokens(jnp.concatenate([pending, cotangents], 0))

    fwd_input = carried[0]
    grad_input = grad_tokens[0]
    forward_list = []
    backward_list = []
    for t in range(steps):
        if t > 0:
            received = from_behind(forward_list[-1], 1)
            fwd_input = jnp.where(section == 0, inputs[t - 1], received)
            received_grad = from_behind(backward_list[-1], -1)
            grad_input = jnp.where(section == sections - 1, grad_tokens[t], received_grad)
        mixed = layer_call(
            False, idx, gather(fwd_input, 1), gain_blocks, key_gain, value_local
        )
        far_first, far_second = far_call(idx, mixed, out_local)
        plus, minus, here = near_call(idx, mixed, out_local)
        head_sum = scatter_sum(here, far_first, far_second, plus, minus, 1)
        forward_list.append((fwd_input.astype(F32) + head_sum).astype(BF16))

        values, probs, normed, centered, inv_std = layer_call(
            True, idx, gather(stash_in[t], 1), gain_blocks, key_gain, value_local
        )
        grad_values, direct = attention_grad_call(
            idx, gather(grad_input, 2), (values, probs, normed), key_gain, out_local
        )
        here, plus, far_first, far_second, minus = back_project_call(
            idx, grad_values, direct, value_local
        )
        grad_normed = scatter_sum(here, far_first, far_second, plus, minus, 2)
        grad_scaled = grad_normed * gain_full
        first_mean = jnp.sum(grad_scaled, -1, keepdims=True) / full
        second_mean = jnp.sum(grad_scaled * centered, -1, keepdims=True) / full
        grad_block = inv_std[:, :1] * (grad_scaled - first_mean - centered * second_mean)
        backward_list.append((grad_input.astype(F32) + grad_block).astype(BF16))
    backward = jnp.concatenate(
        [to_features(jnp.stack(backward_list[:-1])), to_features(backward_list[-1][None])]
    )
    return (jnp.stack(forward_list, 0)[None], backward[None])


def solution(mesh):
    return jax.shard_map(
        per_device,
        mesh=mesh,
        in_specs=(
            P(None, None, "tp"),
            P(None, None, "tp"),
            P("section", None, "tp"),
            P("section", None, "tp"),
            P("section", None, None, "tp"),
            P(),
            P("section", None),
            P("section", "tp"),
            P("section", None, "tp"),
            P("section", "tp", None),
        ),
        out_specs=(P("section", None, None, "tp"), P("section", None, None, "tp")),
        check_vma=False,
    )
```

time: 1500 us -> 627 us (0.42)
  waiting for transfers between devices: 1070 us -> 148 us
  matrix products: 148 us -> 0 us
  starting transfers between devices: 40.7 us -> 186 us
  blocking collectives: 141 us -> 0 us
  Pallas kernels: 0 us -> 122 us
  local copies, waits for them, and re-layouts: 21.9 us -> 77.5 us
  other arithmetic: 30.9 us -> 62.2 us
    reduce_scatter x8 -> x0, waiting for transfers between devices: 558 us -> none  [the longest x4 291 us: per_device(): lax.psum_scatter(partial_out.astype(jnp.bfloat16), 'tp', scatter_dimensio...]
    all_gather x12 -> x0, waiting for transfers between devices: 470 us -> none  [the longest x8 330 us: normalize(): lax.all_gather(normed, 'tp', axis=1, tiled=True)]
    ppermute x6 -> x108, starting transfers between devices: 11.7 us -> 171 us  [the longest x100 155 us: shift(): lax.ppermute(array, 'tp', [(i, place(i, dx, dz)) for i in range(PEERS)])]
    dot_general x48 -> x0, matrix products: 148 us -> none  [the longest x8 44.4 us: normalize(): jnp.dot(lax.all_gather(normed, 'tp', axis=1, tiled=True), value_local, pr...]
    pallas_call x0 -> x24, Pallas kernels: none -> 122 us  [the longest x8 50.8 us: layer_call(): pl.pallas_call(body, out_shape=out_shape, grid_spec=pltpu.PrefetchScalarG...]
    ppermute x6 -> x108, waiting for transfers between devices: 27.2 us -> 143 us  [the longest x100 142 us: shift(): lax.ppermute(array, 'tp', [(i, place(i, dx, dz)) for i in range(PEERS)])]
    psum x5 -> x0, blocking collectives: 110 us -> none  [normalize(): lax.psum((jnp.sum(values32, -1, keepdims=True), jnp.sum(values32 * values...]
    unnamed x28 -> x104, local copies, waits for them, and re-layouts: 1.64 us -> 45.7 us
  transfers between devices with their start and end apart: 31 -> 111, of which waited for: 29 -> 40; matrix products, arithmetic and copies ran while one was open for 9% -> 17% of each run, Pallas kernels for 0% -> 20%
where the time goes in v1:
time: 627 us; the launch traced here: 616 us
  starting transfers between devices  186 us (30%)
  waiting for transfers between devices  148 us (24%)
  Pallas kernels  122 us (19%)
  local copies, waits for them, and re-layouts  77.5 us (12%)
  other arithmetic  62.2 us (10%)
  between operations  19.8 us (3%)
    ppermute x100, starting transfers between devices, shift(): lax.ppermute(array, 'tp', [(i, place(i, dx, dz)) for i in range(PEERS)])  155 us
    ppermute x100, waiting for transfers between devices, shift(): lax.ppermute(array, 'tp', [(i, place(i, dx, dz)) for i in range(PEERS)])  142 us
    pallas_call x8, Pallas kernels, layer_call(): pl.pallas_call(body, out_shape=out_shape, grid_spec=pltpu.PrefetchScalarG...  50.8 us
    unnamed x104, local copies, waits for them, and re-layouts  45.7 us
    unnamed x6, other arithmetic  34.3 us
    pallas_call x4, Pallas kernels, attention_grad_call(): pl.pallas_call(body, out_shape=(jax.ShapeDtypeStruct((tokens, width), BF1...  30.5 us
    pallas_call x4, Pallas kernels, back_project_call(): pl.pallas_call(body, out_shape=[jax.ShapeDtypeStruct((2, share, full // (...  21.3 us
    ppermute x6, starting transfers between devices, from_behind(): return lax.ppermute(array, 'section', pairs)  13.4 us
  transfers between devices with their start and end apart: 111, of which 40 were waited for; matrix products, arithmetic and copies ran while one was open for 17% of the time, Pallas kernels for 20%

profile of v1, /device:TPU:8, one launch (start us, length us, event | category | flops | bytes accessed | tf_op | source)
XLA Modules:
  0.0 615.7 jit_solution(9315423325022417194)
XLA Ops:
  24.2 21.9 %collective-permute-done.refs_2_ = bf16[128,768]{1,0:T(8,128)(2,1)S(1)} collective-permute-done((bf16[128,768]{1,0:T(8,128)(2,1)S(1)}, bf16[128,768]{1,0:T(8,128)(2,1)S(1)}, u32[]{:S(2)}, u32[]{:S(2)}) %collective-permute-start) | collective-permute-done | bytes 196640 | tf_op jit(solution)/shard_map/ppermute | solution.py:38
  80.1 7.0 %mix_layer.4.mixed = bf16[128,768]{1,0:T(8,128)(2,1)S(1)} custom-call(s32[8]{0:T(128)S(1)} %stack.159.refs_0_.idx, bf16[128,768]{1,0:T(8,128)(2,1)S(1)} %bitcast.286, bf16[128,768]{1,0:T(8,128)(2,1)S(1)} %collective-permute-done.refs_2_, bf16[2,128,768]{2,1,0:T(8,128)(2,1)S(1)} %collective-permute-done.1.refs_3_, ...), custom_call_target="tpu_custom_call" | custom-call | flops 1207959552 | bytes 9437184 | tf_op jit(solution)/shard_map/mix_layer/pallas_call | solution.py:196
  116.6 5.1 collective-permute-done.6
  125.2 5.7 stash_layer.4
  130.9 7.6 %attention_grad.4 = (bf16[128,768]{1,0:T(8,128)(2,1)S(1)}, f32[128,768]{1,0:T(8,128)S(1)}) custom-call(s32[8]{0:T(128)S(1)} %stack.159.refs_0_.idx, bf16[16,6144]{1,0:T(8,128)(2,1)S(1)} %bitcast.288, bf16[16,6144]{1,0:T(8,128)(2,1)S(1)} %collective-permute-done.49.partner, bf16[2,16,6144]{2,1,0:T(8,128)(2,1)S(1)} %collective-permute-done.50.plus, ...), custom_call_target="tpu_custom_call" | custom-call | flops 1207959552 | bytes 9437184 | tf_op jit(solution)/shard_map/attention_grad/pallas_call | solution.py:362
  138.6 5.3 back_project.4
  190.1 6.3 %collective-permute-done.15.refs_5_ = bf16[2,64,768]{2,1,0:T(8,128)(2,1)S(1)} collective-permute-done((bf16[2,64,768]{2,1,0:T(8,128)(2,1)S(1)}, bf16[2,64,768]{2,1,0:T(8,128)(2,1)S(1)}, u32[]{:S(2)}, u32[]{:S(2)}) %collective-permute-start.15) | collective-permute-done | bytes 196640 | tf_op jit(solution)/shard_map/ppermute | solution.py:38
  200.1 7.0 %mix_layer.5.mixed = bf16[128,768]{1,0:T(8,128)(2,1)S(1)} custom-call(s32[8]{0:T(128)S(1)} %stack.159.refs_0_.idx, bf16[128,768]{1,0:T(8,128)(2,1)S(1)} %bitcast_select_fusion.10.refs_1_, bf16[128,768]{1,0:T(8,128)(2,1)S(1)} %collective-permute-done.11.refs_2_, bf16[2,128,768]{2,1,0:T(8,128)(2,1)S(1)} %collective-permute-done.12.refs_3_, ...), custom_call_target="tpu_custom_call" | custom-call | flops 1207959552 | bytes 9437184 | tf_op jit(solution)/shard_map/mix_layer/pallas_call | solution.py:196
  228.2 14.1 %collective-permute-done.65.refs_5_ = bf16[2,64,768]{2,1,0:T(8,128)(2,1)S(1)} collective-permute-done((bf16[2,64,768]{2,1,0:T(8,128)(2,1)S(1)}, bf16[2,64,768]{2,1,0:T(8,128)(2,1)S(1)}, u32[]{:S(2)}, u32[]{:S(2)}) %collective-permute-start.65) | collective-permute-done | bytes 196640 | tf_op jit(solution)/shard_map/ppermute | solution.py:38
  245.9 5.7 stash_layer.5
  258.8 7.6 %attention_grad.5 = (bf16[128,768]{1,0:T(8,128)(2,1)S(1)}, f32[128,768]{1,0:T(8,128)S(1)}) custom-call(s32[8]{0:T(128)S(1)} %stack.159.refs_0_.idx, bf16[16,6144]{1,0:T(8,128)(2,1)S(1)} %broadcast_select_fusion.2.own, bf16[16,6144]{1,0:T(8,128)(2,1)S(1)} %collective-permute-done.66.partner, bf16[2,16,6144]{2,1,0:T(8,128)(2,1)S(1)} %collective-permute-done.67.plus, ...), custom_call_target="tpu_custom_call" | custom-call | flops 1207959552 | bytes 9437184 | tf_op jit(solution)/shard_map/attention_grad/pallas_call | solution.py:362
  266.4 5.3 back_project.5
  283.4 8.5 %collective-permute-done.72 = bf16[2,16,6144]{2,1,0:T(8,128)(2,1)S(1)} collective-permute-done((bf16[2,16,6144]{2,1,0:T(8,128)(2,1)S(1)}, bf16[2,16,6144]{2,1,0:T(8,128)(2,1)S(1)}, u32[]{:S(2)}, u32[]{:S(2)}) %collective-permute-start.72) | collective-permute-done | bytes 393248 | tf_op jit(solution)/shard_map/ppermute | solution.py:38
  320.8 7.0 %mix_layer.6.mixed = bf16[128,768]{1,0:T(8,128)(2,1)S(1)} custom-call(s32[8]{0:T(128)S(1)} %stack.159.refs_0_.idx, bf16[128,768]{1,0:T(8,128)(2,1)S(1)} %bitcast_select_fusion.9.refs_1_, bf16[128,768]{1,0:T(8,128)(2,1)S(1)} %collective-permute-done.22.refs_2_, bf16[2,128,768]{2,1,0:T(8,128)(2,1)S(1)} %collective-permute-done.23.refs_3_, ...), custom_call_target="tpu_custom_call" | custom-call | flops 1207959552 | bytes 9437184 | tf_op jit(solution)/shard_map/mix_layer/pallas_call | solution.py:196
  345.3 14.8 %collective-permute-done.81.refs_5_ = bf16[2,64,768]{2,1,0:T(8,128)(2,1)S(1)} collective-permute-done((bf16[2,64,768]{2,1,0:T(8,128)(2,1)S(1)}, bf16[2,64,768]{2,1,0:T(8,128)(2,1)S(1)}, u32[]{:S(2)}, u32[]{:S(2)}) %collective-permute-start.81) | collective-permute-done | bytes 196640 | tf_op jit(solution)/shard_map/ppermute | solution.py:38
  361.8 5.7 stash_layer.6
  374.6 7.6 %attention_grad.6 = (bf16[128,768]{1,0:T(8,128)(2,1)S(1)}, f32[128,768]{1,0:T(8,128)S(1)}) custom-call(s32[8]{0:T(128)S(1)} %stack.159.refs_0_.idx, bf16[16,6144]{1,0:T(8,128)(2,1)S(1)} %broadcast_select_fusion.1.own, bf16[16,6144]{1,0:T(8,128)(2,1)S(1)} %collective-permute-done.82.partner, bf16[2,16,6144]{2,1,0:T(8,128)(2,1)S(1)} %collective-permute-done.83.plus, ...), custom_call_target="tpu_custom_call" | custom-call | flops 1207959552 | bytes 9437184 | tf_op jit(solution)/shard_map/attention_grad/pallas_call | solution.py:362
  382.3 5.3 back_project.6
  402.2 5.7 collective-permute-done.88
  430.3 5.7 stash_layer.7
  436.1 7.0 %mix_layer.7.mixed = bf16[128,768]{1,0:T(8,128)(2,1)S(1)} custom-call(s32[8]{0:T(128)S(1)} %stack.159.refs_0_.idx, bf16[128,768]{1,0:T(8,128)(2,1)S(1)} %bitcast_select_fusion.8.refs_1_, bf16[128,768]{1,0:T(8,128)(2,1)S(1)} %collective-permute-done.33.refs_2_, bf16[2,128,768]{2,1,0:T(8,128)(2,1)S(1)} %collective-permute-done.34.refs_3_, ...), custom_call_target="tpu_custom_call" | custom-call | flops 1207959552 | bytes 9437184 | tf_op jit(solution)/shard_map/mix_layer/pallas_call | solution.py:196
  450.6 6.2 %copy.35 = bf16[3,16,6144]{1,0,2:T(4,128)(2,1)} copy(bf16[3,16,6144]{2,1,0:T(8,128)(2,1)S(1)} %pad_maximum_fusion.2) | data formatting | bytes 1179648 | tf_op jit(solution)/shard_map/stack | solution.py:520
  456.8 8.8 %reshape.82 = bf16[8,2,18432]{2,1,0:T(2,128)(2,1)} reshape(bf16[6144,3,16]{2,1,0:T(4,128)(2,1)} %bitcast.302) | data formatting | bytes 1179648
  465.7 6.5 %all-to-all-start.1 = ((bf16[8,2,18432]{2,1,0:T(2,128)(2,1)}), bf16[8,2,18432]{2,1,0:T(2,128)(2,1)S(1)}, u32[]{:S(2)}, u32[]{:S(2)}) async-start(bf16[8,2,18432]{2,1,0:T(2,128)(2,1)} %reshape.82), calls=%async_computation.1 | async-start | bytes 1179648 | tf_op jit(solution)/shard_map/all_to_all | solution.py:453
  496.2 7.6 %attention_grad.7 = (bf16[128,768]{1,0:T(8,128)(2,1)S(1)}, f32[128,768]{1,0:T(8,128)S(1)}) custom-call(s32[8]{0:T(128)S(1)} %stack.159.refs_0_.idx, bf16[16,6144]{1,0:T(8,128)(2,1)S(1)} %broadcast_select_fusion.own, bf16[16,6144]{1,0:T(8,128)(2,1)S(1)} %collective-permute-done.98.partner, bf16[2,16,6144]{2,1,0:T(8,128)(2,1)S(1)} %collective-permute-done.99.plus, ...), custom_call_target="tpu_custom_call" | custom-call | flops 1207959552 | bytes 9437184 | tf_op jit(solution)/shard_map/attention_grad/pallas_call | solution.py:362
  503.8 5.3 back_project.7
  512.7 4.9 collective-permute-done.103
  526.4 7.4 %reshape.83 = bf16[6144,3,16]{2,1,0:T(4,128)(2,1)} reshape(bf16[8,2,18432]{2,1,0:T(2,128)(2,1)S(1)} %all-to-all-done.1) | data formatting | bytes 1179648
  533.8 9.0 %copy.36 = bf16[3,8,16,768]{3,2,1,0:T(8,128)(2,1)} copy(bf16[3,8,16,768]{2,0,3,1:T(4,128)(2,1)} %bitcast.303) | data formatting | bytes 1179648 | tf_op jit(solution)/shard_map/all_to_all | solution.py:453
  553.1 5.1 copy.37
  558.7 34.3 %reduce.8 = bf16[6144,16]{1,0:T(8,128)(2,1)S(1)} reduce(bf16[6144,1,16]{2,1,0:T(2,128)(2,1)} %bitcast.304, bf16[]{:T(256)} %broadcast.74), dimensions={1}, to_apply=%bitcast.223.reduce_sub_computation | reduce | bytes 393218
  602.9 5.2 all-to-all-done.2
  (472 shorter events, 329.2 us)
Async XLA Ops:
  11.3 47.9 %collective-permute-start.60 = (bf16[3,128,768]{2,1,0:T(8,128)(2,1)S(1)}, bf16[3,128,768]{2,1,0:T(8,128)(2,1)S(1)}, u32[]{:S(2)}, u32[]{:S(2)}) collective-permute-start(bf16[3,128,768]{2,1,0:T(8,128)(2,1)S(1)} %pad_maximum_fusion.1), channel_id=1, source_target_pairs={{0,120},{8,112},{16,104},{24,96},{32,88},{40,80},{48,72},{56,64},{... | collective-permute-start | bytes 1769480 | tf_op jit(solution)/shard_map/ppermute | solution.py:475
  13.7 32.4 %collective-permute-start = (bf16[128,768]{1,0:T(8,128)(2,1)S(1)}, bf16[128,768]{1,0:T(8,128)(2,1)S(1)}, u32[]{:S(2)}, u32[]{:S(2)}) collective-permute-start(bf16[128,768]{1,0:T(8,128)(2,1)S(1)} %bitcast.285), channel_id=1, source_target_pairs={{0,1},{1,0},{2,3},{3,2},{4,5},{5,4},{6,7},{7,6},{8,9},{9,8},{10,11... | collective-permute-start | bytes 589832 | tf_op jit(solution)/shard_map/ppermute | solution.py:38
  17.3 41.8 %collective-permute-start.43 = (bf16[1,128,768]{2,1,0:T(8,128)(2,1)S(1)}, bf16[1,128,768]{2,1,0:T(8,128)(2,1)S(1)}, u32[]{:S(2)}, u32[]{:S(2)}) collective-permute-start(bf16[1,128,768]{2,1,0:T(8,128)(2,1)S(1)} %get-tuple-element.154), channel_id=1, source_target_pairs={{0,120},{8,112},{16,104},{24,96},{32,88},{40,80},{48,72},{56,64},{... | collective-permute-start | bytes 589832 | tf_op jit(solution)/shard_map/ppermute | solution.py:475
  19.9 46.4 %all-to-all-start = ((bf16[4,128,768]{2,0,1:T(4,128)(2,1)}), bf16[4,128,768]{2,0,1:T(4,128)(2,1)}, u32[]{:S(2)}, u32[]{:S(2)}) async-start(bf16[4,128,768]{2,0,1:T(4,128)(2,1)} %pad_maximum_fusion), calls=%async_computation | async-start | bytes 1572864 | tf_op jit(solution)/shard_map/all_to_all | solution.py:449
  69.5 29.5 %collective-permute-start.49 = (bf16[16,6144]{1,0:T(8,128)(2,1)S(1)}, bf16[16,6144]{1,0:T(8,128)(2,1)S(1)}, u32[]{:S(2)}, u32[]{:S(2)}) collective-permute-start(bf16[16,6144]{1,0:T(8,128)(2,1)S(1)} %bitcast.287), channel_id=1, source_target_pairs={{0,1},{1,0},{2,3},{3,2},{4,5},{5,4},{6,7},{7,6},{8,9},{9,8},{10,11... | collective-permute-start | bytes 589832 | tf_op jit(solution)/shard_map/ppermute | solution.py:38
  73.1 33.2 %collective-permute-start.45 = (bf16[2,128,768]{2,1,0:T(8,128)(2,1)S(1)}, bf16[2,128,768]{2,1,0:T(8,128)(2,1)S(1)}, u32[]{:S(2)}, u32[]{:S(2)}) collective-permute-start(bf16[2,128,768]{2,1,0:T(8,128)(2,1)S(1)} %pad_maximum_fusion.15), channel_id=1, source_target_pairs={{0,6},{1,7},{2,0},{3,1},{4,2},{5,3},{6,4},{7,5},{8,14},{9,15},{10,... | collective-permute-start | bytes 1179656 | tf_op jit(solution)/shard_map/ppermute | solution.py:38
  76.4 32.0 %collective-permute-start.47 = (bf16[2,128,768]{2,1,0:T(8,128)(2,1)S(1)}, bf16[2,128,768]{2,1,0:T(8,128)(2,1)S(1)}, u32[]{:S(2)}, u32[]{:S(2)}) collective-permute-start(bf16[2,128,768]{2,1,0:T(8,128)(2,1)S(1)} %pad_maximum_fusion.15), channel_id=1, source_target_pairs={{0,2},{1,3},{2,4},{3,5},{4,6},{5,7},{6,0},{7,1},{8,10},{9,11},{10,... | collective-permute-start | bytes 1179656 | tf_op jit(solution)/shard_map/ppermute | solution.py:38
  108.4 47.3 %collective-permute-start.61 = (bf16[128,768]{1,0:T(8,128)(2,1)S(1)}, bf16[128,768]{1,0:T(8,128)(2,1)S(1)}, u32[]{:S(2)}, u32[]{:S(2)}) collective-permute-start(bf16[128,768]{1,0:T(8,128)(2,1)S(1)} %get-tuple-element.149.refs_1_), channel_id=1, source_target_pairs={{0,1},{1,0},{2,3},{3,2},{4,5},{5,4},{6,7},{7,6},{8,9},{9,8},{10,11... | collective-permute-start | bytes 589832 | tf_op jit(solution)/shard_map/ppermute | solution.py:38
  178.7 45.7 %collective-permute-start.64 = (bf16[2,128,768]{2,1,0:T(8,128)(2,1)}, bf16[2,128,768]{2,1,0:T(8,128)(2,1)S(1)}, u32[]{:S(2)}, u32[]{:S(2)}) collective-permute-start(bf16[2,128,768]{2,1,0:T(8,128)(2,1)} %pad_maximum_fusion.19), channel_id=1, source_target_pairs={{0,2},{1,3},{2,4},{3,5},{4,6},{5,7},{6,0},{7,1},{8,10},{9,11},{10,... | collective-permute-start | bytes 1179656 | tf_op jit(solution)/shard_map/ppermute | solution.py:38
  179.8 48.4 %collective-permute-start.63 = (bf16[2,64,768]{2,1,0:T(8,128)(2,1)S(1)}, bf16[2,64,768]{2,1,0:T(8,128)(2,1)S(1)}, u32[]{:S(2)}, u32[]{:S(2)}) collective-permute-start(bf16[2,64,768]{2,1,0:T(8,128)(2,1)S(1)} %slice.384), channel_id=1, source_target_pairs={{0,6},{1,7},{2,0},{3,1},{4,2},{5,3},{6,4},{7,5},{8,14},{9,15},{10,... | collective-permute-start | bytes 589832 | tf_op jit(solution)/shard_map/ppermute | solution.py:38
  186.1 32.8 %collective-permute-start.66 = (bf16[16,6144]{1,0:T(8,128)(2,1)S(1)}, bf16[16,6144]{1,0:T(8,128)(2,1)S(1)}, u32[]{:S(2)}, u32[]{:S(2)}) collective-permute-start(bf16[16,6144]{1,0:T(8,128)(2,1)S(1)} %broadcast_select_fusion.2.own), channel_id=1, source_target_pairs={{0,1},{1,0},{2,3},{3,2},{4,5},{5,4},{6,7},{7,6},{8,9},{9,8},{10,11... | collective-permute-start | bytes 589832 | tf_op jit(solution)/shard_map/ppermute | solution.py:38
  219.0 32.7 %collective-permute-start.67 = (bf16[2,16,6144]{2,1,0:T(8,128)(2,1)S(1)}, bf16[2,16,6144]{2,1,0:T(8,128)(2,1)S(1)}, u32[]{:S(2)}, u32[]{:S(2)}) collective-permute-start(bf16[2,16,6144]{2,1,0:T(8,128)(2,1)S(1)} %pad_maximum_fusion.20), channel_id=1, source_target_pairs={{0,6},{1,7},{2,0},{3,1},{4,2},{5,3},{6,4},{7,5},{8,14},{9,15},{10,... | collective-permute-start | bytes 1179656 | tf_op jit(solution)/shard_map/ppermute | solution.py:38
  219.2 32.5 %collective-permute-start.69 = (bf16[2,16,6144]{2,1,0:T(8,128)(2,1)S(1)}, bf16[2,16,6144]{2,1,0:T(8,128)(2,1)S(1)}, u32[]{:S(2)}, u32[]{:S(2)}) collective-permute-start(bf16[2,16,6144]{2,1,0:T(8,128)(2,1)S(1)} %pad_maximum_fusion.20), channel_id=1, source_target_pairs={{0,2},{1,3},{2,4},{3,5},{4,6},{5,7},{6,0},{7,1},{8,10},{9,11},{10,... | collective-permute-start | bytes 1179656 | tf_op jit(solution)/shard_map/ppermute | solution.py:38
  224.3 29.6 %collective-permute-start.17 = (bf16[2,128,768]{2,1,0:T(8,128)(2,1)S(1)}, bf16[2,128,768]{2,1,0:T(8,128)(2,1)S(1)}, u32[]{:S(2)}, u32[]{:S(2)}) collective-permute-start(bf16[2,128,768]{2,1,0:T(8,128)(2,1)S(1)} %pad_maximum_fusion.7), channel_id=1, source_target_pairs={{0,2},{1,3},{2,4},{3,5},{4,6},{5,7},{6,0},{7,1},{8,10},{9,11},{10,... | collective-permute-start | bytes 1179656 | tf_op jit(solution)/shard_map/ppermute | solution.py:38
  224.4 29.5 %collective-permute-start.19 = (bf16[2,128,768]{2,1,0:T(8,128)(2,1)S(1)}, bf16[2,128,768]{2,1,0:T(8,128)(2,1)S(1)}, u32[]{:S(2)}, u32[]{:S(2)}) collective-permute-start(bf16[2,128,768]{2,1,0:T(8,128)(2,1)S(1)} %pad_maximum_fusion.8), channel_id=1, source_target_pairs={{0,6},{1,7},{2,0},{3,1},{4,2},{5,3},{6,4},{7,5},{8,14},{9,15},{10,... | collective-permute-start | bytes 1179656 | tf_op jit(solution)/shard_map/ppermute | solution.py:38
  242.4 39.9 %collective-permute-start.77 = (bf16[128,768]{1,0:T(8,128)(2,1)S(1)}, bf16[128,768]{1,0:T(8,128)(2,1)S(1)}, u32[]{:S(2)}, u32[]{:S(2)}) collective-permute-start(bf16[128,768]{1,0:T(8,128)(2,1)S(1)} %get-tuple-element.151.refs_1_), channel_id=1, source_target_pairs={{0,1},{1,0},{2,3},{3,2},{4,5},{5,4},{6,7},{7,6},{8,9},{9,8},{10,11... | collective-permute-start | bytes 589832 | tf_op jit(solution)/shard_map/ppermute | solution.py:38
  303.0 38.5 %collective-permute-start.80 = (bf16[2,128,768]{2,1,0:T(8,128)(2,1)S(1)}, bf16[2,128,768]{2,1,0:T(8,128)(2,1)S(1)}, u32[]{:S(2)}, u32[]{:S(2)}) collective-permute-start(bf16[2,128,768]{2,1,0:T(8,128)(2,1)S(1)} %pad_maximum_fusion.23), channel_id=1, source_target_pairs={{0,2},{1,3},{2,4},{3,5},{4,6},{5,7},{6,0},{7,1},{8,10},{9,11},{10,... | collective-permute-start | bytes 1179656 | tf_op jit(solution)/shard_map/ppermute | solution.py:38
  303.1 42.1 %collective-permute-start.79 = (bf16[2,64,768]{2,1,0:T(8,128)(2,1)S(1)}, bf16[2,64,768]{2,1,0:T(8,128)(2,1)S(1)}, u32[]{:S(2)}, u32[]{:S(2)}) collective-permute-start(bf16[2,64,768]{2,1,0:T(8,128)(2,1)S(1)} %slice.392), channel_id=1, source_target_pairs={{0,6},{1,7},{2,0},{3,1},{4,2},{5,3},{6,4},{7,5},{8,14},{9,15},{10,... | collective-permute-start | bytes 589832 | tf_op jit(solution)/shard_map/ppermute | solution.py:38
  336.1 31.5 %collective-permute-start.83 = (bf16[2,16,6144]{2,1,0:T(8,128)(2,1)S(1)}, bf16[2,16,6144]{2,1,0:T(8,128)(2,1)S(1)}, u32[]{:S(2)}, u32[]{:S(2)}) collective-permute-start(bf16[2,16,6144]{2,1,0:T(8,128)(2,1)S(1)} %pad_maximum_fusion.24), channel_id=1, source_target_pairs={{0,6},{1,7},{2,0},{3,1},{4,2},{5,3},{6,4},{7,5},{8,14},{9,15},{10,... | collective-permute-start | bytes 1179656 | tf_op jit(solution)/shard_map/ppermute | solution.py:38
  336.8 30.8 %collective-permute-start.85 = (bf16[2,16,6144]{2,1,0:T(8,128)(2,1)S(1)}, bf16[2,16,6144]{2,1,0:T(8,128)(2,1)S(1)}, u32[]{:S(2)}, u32[]{:S(2)}) collective-permute-start(bf16[2,16,6144]{2,1,0:T(8,128)(2,1)S(1)} %pad_maximum_fusion.24), channel_id=1, source_target_pairs={{0,2},{1,3},{2,4},{3,5},{4,6},{5,7},{6,0},{7,1},{8,10},{9,11},{10,... | collective-permute-start | bytes 1179656 | tf_op jit(solution)/shard_map/ppermute | solution.py:38
  341.3 28.4 %collective-permute-start.28 = (bf16[2,128,768]{2,1,0:T(8,128)(2,1)S(1)}, bf16[2,128,768]{2,1,0:T(8,128)(2,1)S(1)}, u32[]{:S(2)}, u32[]{:S(2)}) collective-permute-start(bf16[2,128,768]{2,1,0:T(8,128)(2,1)S(1)} %pad_maximum_fusion.10), channel_id=1, source_target_pairs={{0,2},{1,3},{2,4},{3,5},{4,6},{5,7},{6,0},{7,1},{8,10},{9,11},{10,... | collective-permute-start | bytes 1179656 | tf_op jit(solution)/shard_map/ppermute | solution.py:38
  341.4 28.3 %collective-permute-start.30 = (bf16[2,128,768]{2,1,0:T(8,128)(2,1)S(1)}, bf16[2,128,768]{2,1,0:T(8,128)(2,1)S(1)}, u32[]{:S(2)}, u32[]{:S(2)}) collective-permute-start(bf16[2,128,768]{2,1,0:T(8,128)(2,1)S(1)} %pad_maximum_fusion.11), channel_id=1, source_target_pairs={{0,6},{1,7},{2,0},{3,1},{4,2},{5,3},{6,4},{7,5},{8,14},{9,15},{10,... | collective-permute-start | bytes 1179656 | tf_op jit(solution)/shard_map/ppermute | solution.py:38
  360.2 37.9 %collective-permute-start.93 = (bf16[128,768]{1,0:T(8,128)(2,1)S(1)}, bf16[128,768]{1,0:T(8,128)(2,1)S(1)}, u32[]{:S(2)}, u32[]{:S(2)}) collective-permute-start(bf16[128,768]{1,0:T(8,128)(2,1)S(1)} %get-tuple-element.150.refs_1_), channel_id=1, source_target_pairs={{0,1},{1,0},{2,3},{3,2},{4,5},{5,4},{6,7},{7,6},{8,9},{9,8},{10,11... | collective-permute-start | bytes 589832 | tf_op jit(solution)/shard_map/ppermute | solution.py:38
  445.2 39.5 %collective-permute-start.38 = (bf16[2,64,768]{2,1,0:T(8,128)(2,1)}, bf16[2,64,768]{2,1,0:T(8,128)(2,1)}, u32[]{:S(2)}, u32[]{:S(2)}) collective-permute-start(bf16[2,64,768]{2,1,0:T(8,128)(2,1)} %get-tuple-element.87), channel_id=1, source_target_pairs={{0,2},{1,3},{2,4},{3,5},{4,6},{5,7},{6,0},{7,1},{8,10},{9,11},{10,... | collective-permute-start | bytes 589832 | tf_op jit(solution)/shard_map/ppermute | solution.py:38
  446.4 36.1 %collective-permute-start.99 = (bf16[2,16,6144]{2,1,0:T(8,128)(2,1)}, bf16[2,16,6144]{2,1,0:T(8,128)(2,1)S(1)}, u32[]{:S(2)}, u32[]{:S(2)}) collective-permute-start(bf16[2,16,6144]{2,1,0:T(8,128)(2,1)} %pad_maximum_fusion.28), channel_id=1, source_target_pairs={{0,6},{1,7},{2,0},{3,1},{4,2},{5,3},{6,4},{7,5},{8,14},{9,15},{10,... | collective-permute-start | bytes 1179656 | tf_op jit(solution)/shard_map/ppermute | solution.py:38
  449.6 33.8 %collective-permute-start.101 = (bf16[2,16,6144]{2,1,0:T(8,128)(2,1)}, bf16[2,16,6144]{2,1,0:T(8,128)(2,1)S(1)}, u32[]{:S(2)}, u32[]{:S(2)}) collective-permute-start(bf16[2,16,6144]{2,1,0:T(8,128)(2,1)} %pad_maximum_fusion.28), channel_id=1, source_target_pairs={{0,2},{1,3},{2,4},{3,5},{4,6},{5,7},{6,0},{7,1},{8,10},{9,11},{10,... | collective-permute-start | bytes 1179656 | tf_op jit(solution)/shard_map/ppermute | solution.py:38
  465.7 60.8 %all-to-all-start.1 = ((bf16[8,2,18432]{2,1,0:T(2,128)(2,1)}), bf16[8,2,18432]{2,1,0:T(2,128)(2,1)S(1)}, u32[]{:S(2)}, u32[]{:S(2)}) async-start(bf16[8,2,18432]{2,1,0:T(2,128)(2,1)} %reshape.82), calls=%async_computation.1 | async-start | bytes 1179648 | tf_op jit(solution)/shard_map/all_to_all | solution.py:453
  479.1 30.2 %collective-permute-start.40 = (bf16[2,64,768]{2,1,0:T(8,128)(2,1)S(1)}, bf16[2,64,768]{2,1,0:T(8,128)(2,1)S(1)}, u32[]{:S(2)}, u32[]{:S(2)}) collective-permute-start(bf16[2,64,768]{2,1,0:T(8,128)(2,1)S(1)} %copy-done.14), channel_id=1, source_target_pairs={{0,6},{1,7},{2,0},{3,1},{4,2},{5,3},{6,4},{7,5},{8,14},{9,15},{10,... | collective-permute-start | bytes 589832 | tf_op jit(solution)/shard_map/ppermute | solution.py:38
  486.4 56.4 %collective-permute-start.39 = (bf16[2,128,768]{2,1,0:T(8,128)(2,1)}, bf16[2,128,768]{2,1,0:T(8,128)(2,1)}, u32[]{:S(2)}, u32[]{:S(2)}) collective-permute-start(bf16[2,128,768]{2,1,0:T(8,128)(2,1)} %pad_maximum_fusion.13), channel_id=1, source_target_pairs={{0,2},{1,3},{2,4},{3,5},{4,6},{5,7},{6,0},{7,1},{8,10},{9,11},{10,... | collective-permute-start | bytes 1179656 | tf_op jit(solution)/shard_map/ppermute | solution.py:38
  509.4 33.5 %collective-permute-start.41 = (bf16[2,128,768]{2,1,0:T(8,128)(2,1)S(1)}, bf16[2,128,768]{2,1,0:T(8,128)(2,1)}, u32[]{:S(2)}, u32[]{:S(2)}) collective-permute-start(bf16[2,128,768]{2,1,0:T(8,128)(2,1)S(1)} %pad_maximum_fusion.14), channel_id=1, source_target_pairs={{0,6},{1,7},{2,0},{3,1},{4,2},{5,3},{6,4},{7,5},{8,14},{9,15},{10,... | collective-permute-start | bytes 1179656 | tf_op jit(solution)/shard_map/ppermute | solution.py:38
  518.5 25.6 %collective-permute-start.104 = (bf16[2,16,6144]{2,1,0:T(8,128)(2,1)}, bf16[2,16,6144]{2,1,0:T(8,128)(2,1)}, u32[]{:S(2)}, u32[]{:S(2)}) collective-permute-start(bf16[2,16,6144]{2,1,0:T(8,128)(2,1)} %pad_maximum_fusion.29), channel_id=1, source_target_pairs={{0,2},{1,3},{2,4},{3,5},{4,6},{5,7},{6,0},{7,1},{8,10},{9,11},{10,... | collective-permute-start | bytes 1179656 | tf_op jit(solution)/shard_map/ppermute | solution.py:38
  548.9 51.0 %collective-permute-start.42 = (bf16[128,768]{1,0:T(8,128)(2,1)S(1)}, bf16[128,768]{1,0:T(8,128)(2,1)}, u32[]{:S(2)}, u32[]{:S(2)}) collective-permute-start(bf16[128,768]{1,0:T(8,128)(2,1)S(1)} %fusion.25), channel_id=1, source_target_pairs={{0,1},{1,0},{2,3},{3,2},{4,5},{5,4},{6,7},{7,6},{8,9},{9,8},{10,11... | collective-permute-start | bytes 589832 | tf_op jit(solution)/shard_map/ppermute | solution.py:38
  (125 other events, 1615.5 us)

commit v2 on v1

v2 whole, which is shorter than its diff:
```python
import math

import jax
import jax.numpy as jnp
from jax import lax
from jax.experimental import pallas as pl
from jax.experimental.pallas import tpu as pltpu
from jax.sharding import PartitionSpec as P

HEAD = 128
EPSILON = 1e-05
RINGX = 4
PEERS = 8
BF16 = jnp.bfloat16
VMEM_LIMIT = 46 * 1024 * 1024
F32 = jnp.float32
HBM = pl.BlockSpec(memory_space=pl.ANY)
NT = (((1,), (1,)), ((), ()))
NN = (((1,), (0,)), ((), ()))
TN = (((0,), (0,)), ((), ()))


def params():
    return pltpu.CompilerParams(
        dimension_semantics=("arbitrary",), vmem_limit_bytes=VMEM_LIMIT
    )


def cost(flops, nbytes):
    return pl.CostEstimate(flops=1, bytes_accessed=1, transcendentals=0)


def place(i, dx, dz):
    return ((i // 2 + dx) % RINGX) * 2 + ((i % 2) ^ dz)


def shift(array, dx, dz):
    return lax.ppermute(array, "tp", [(i, place(i, dx, dz)) for i in range(PEERS)])


def hop(array, by, cross):
    peers = lax.axis_size("section")
    pairs = [
        (i * PEERS + j, (i + by) * PEERS + (j ^ cross))
        for i in range(peers)
        if 0 <= i + by < peers
        for j in range(PEERS)
    ]
    return lax.ppermute(array, ("section", "tp"), pairs)


def partner_in(array, section):
    pairs = [(section * PEERS + j, section * PEERS + (j ^ 1)) for j in range(PEERS)]
    return lax.ppermute(array, ("section", "tp"), pairs)


def add(a, b):
    return (a.astype(F32) + b.astype(F32)).astype(BF16)


class Order:
    def __init__(self):
        self.token = jnp.zeros((), F32)

    def pin(self, *arrays):
        self.token, *arrays = lax.optimization_barrier((self.token, *arrays))
        return arrays if len(arrays) > 1 else arrays[0]


class Gather:
    def __init__(self, order, pair):
        self.order = order
        self.pair = order.pin(pair)
        far = shift(self.pair, 2, 0)
        self.rest = shift(self.pair, -1, 0), far, shift(self.pair, 1, 0)

    def done(self):
        return self.pair, *self.order.pin(*self.rest)


class ScatterSum:
    def __init__(self, order, far, plus, minus):
        self.order = order
        far, plus, minus = order.pin(far, plus, minus)
        self.got = shift(far, 2, 0), shift(plus, 1, 0), shift(minus, -1, 0)

    def done(self):
        return self.order.pin(*self.got)


class Hop:
    def __init__(self, order, part, by):
        self.order = order
        part = order.pin(part)
        self.got = hop(part, by, 0), hop(part, by, 1)

    def done(self, at_edge, edge_pair):
        same, cross = self.order.pin(*self.got)
        return jnp.where(at_edge, edge_pair, add(same, cross[::-1]))


def whole(array):
    zeros = (0,) * array.ndim
    return pl.BlockSpec(array.shape, lambda r, idx: zeros)


def per_head(heads, product):
    return jnp.concatenate([product(slice(h * HEAD, (h + 1) * HEAD)) for h in range(heads)], 0)


def softmax_scores(queries, keys, tokens, heads):
    scores = per_head(
        heads,
        lambda p: lax.dot_general(queries[:, p], keys[:, p], NT, preferred_element_type=F32),
    )
    scores = scores / math.sqrt(HEAD)
    rows = lax.broadcasted_iota(jnp.int32, scores.shape, 0) % tokens
    columns = lax.broadcasted_iota(jnp.int32, scores.shape, 1)
    scores = jnp.where(columns <= rows, scores, -1e30)
    raised = jnp.exp(scores - jnp.max(scores, -1, keepdims=True))
    return raised / jnp.sum(raised, -1, keepdims=True)


def row_block(tiles, k):
    return tiles.at[k]


def column_block(tiles, k):
    return tiles.at[PEERS + k]


def tile_call(w_value, w_out):
    width = w_value.shape[1]

    def body(w_value, w_out, tiles):
        tiles[0, 0] = w_value[...]
        tiles[1, 0] = w_out[...]

    tiles = pl.pallas_call(
        body,
        out_shape=jax.ShapeDtypeStruct((2, PEERS, width, width), BF16),
        grid=(PEERS,),
        in_specs=[
            pl.BlockSpec((width, width), lambda k: (k, 0)),
            pl.BlockSpec((width, width), lambda k: (0, k)),
        ],
        out_specs=pl.BlockSpec((2, 1, width, width), lambda k: (0, k, 0, 0)),
        compiler_params=params(),
        cost_estimate=cost(1, 1),
        name="weight_tiles",
    )(w_value, w_out)
    return tiles.reshape(2 * PEERS, width, width)


def stream_scratch(count, width):
    return [pltpu.VMEM((count, width, width), BF16), pltpu.SemaphoreType.DMA((count,))]


def wait_block(weight, blocks, sems, step, block_of):
    pltpu.make_async_copy(block_of(weight, 0), blocks.at[step], sems.at[step]).wait()


def layer_body(stashed, natural, tokens, width, *refs):
    idx = refs[0]
    if natural:
        pieces, rest = refs[1], refs[2:]
    else:
        pairs, pieces, rest = refs[1:5], refs[-1], refs[5:-1]
    gain, gain_own, key_row, weight = rest[:4]
    if stashed:
        out_values, out_probs, out_normed, out_centered, out_inv = rest[4:9]
    else:
        (out_mixed,) = rest[4:5]
    total, normed_own, mean_ref, inv_ref, weights, blocks, sems = rest[-7:]
    step = pl.program_id(0)
    full = width * PEERS
    heads = width // HEAD

    @pl.when(step == 0)
    def _():
        for k in range(PEERS):
            pltpu.make_async_copy(row_block(weight, idx[k]), blocks.at[k], sems.at[k]).start()
        if not natural:
            for k in range(RINGX):
                pieces[2 * k : 2 * k + 2] = pairs[k][...]
        sums = jnp.zeros((tokens, HEAD), F32)
        squares = jnp.zeros((tokens, HEAD), F32)
        for r in range(PEERS):
            for c in range(heads):
                x = pieces[r, :, c * HEAD : (c + 1) * HEAD].astype(F32)
                sums += x
                squares += x * x
        mean = jnp.sum(sums, -1, keepdims=True) / full
        variance = jnp.sum(squares, -1, keepdims=True) / full - mean * mean
        mean_ref[...] = jnp.broadcast_to(mean, (tokens, HEAD))
        inv_ref[...] = jnp.broadcast_to(lax.rsqrt(variance + EPSILON), (tokens, HEAD))
        total[...] = jnp.zeros_like(total)
        mine = (pieces[idx[PEERS]].astype(F32) - mean_ref[:, :1]) * inv_ref[:, :1]
        normed_own[...] = (mine * gain_own[0]).astype(BF16)
        keys = (normed_own[...].astype(F32) * key_row[...]).astype(BF16)
        probs = softmax_scores(normed_own[...], keys, tokens, heads)
        if stashed:
            out_probs[...] = probs
            out_normed[...] = normed_own[...]
        else:
            weights[...] = probs.astype(BF16)

    centered = (pieces[step].astype(F32) - mean_ref[:, :1]) * inv_ref[:, :1]
    normed = (centered * gain[0]).astype(BF16)
    wait_block(weight, blocks, sems, step, row_block)
    total[...] += lax.dot_general(normed, blocks[step], NN, preferred_element_type=F32)

    if stashed:
        share = tokens // PEERS
        for dz in range(2):
            rows = pl.ds(pl.multiple_of(idx[PEERS + 1 + dz] * share, share), share)
            out_centered[dz, 0] = (
                pieces[step, rows, :].astype(F32) - mean_ref[rows, :1]
            ) * inv_ref[rows, :1]
            out_inv[dz] = inv_ref[rows, :]

    @pl.when(step == PEERS - 1)
    def _():
        values = total[...].astype(BF16)
        if stashed:
            out_values[...] = values
        else:
            for h in range(heads):
                part = slice(h * HEAD, (h + 1) * HEAD)
                out_mixed[:, part] = lax.dot_general(
                    weights[h * tokens : (h + 1) * tokens],
                    values[:, part],
                    NN,
                    preferred_element_type=F32,
                ).astype(BF16)


def layer_call(stashed, idx, pieces, gain, key_row, weight):
    natural = len(pieces) == 1
    tokens, width = pieces[0].shape[-2:]
    full = width * PEERS
    share = tokens // PEERS
    heads = width // HEAD
    if stashed:
        out_shape = (
            jax.ShapeDtypeStruct((tokens, width), BF16),
            jax.ShapeDtypeStruct((heads * tokens, tokens), F32),
            jax.ShapeDtypeStruct((tokens, width), BF16),
            jax.ShapeDtypeStruct((2, PEERS, share, width), F32),
            jax.ShapeDtypeStruct((2, share, HEAD), F32),
        )
        out_specs = (
            pl.BlockSpec((tokens, width), lambda r, idx: (0, 0)),
            pl.BlockSpec((heads * tokens, tokens), lambda r, idx: (0, 0)),
            pl.BlockSpec((tokens, width), lambda r, idx: (0, 0)),
            pl.BlockSpec((2, 1, share, width), lambda r, idx: (0, idx[r], 0, 0)),
            pl.BlockSpec((2, share, HEAD), lambda r, idx: (0, 0, 0)),
        )
    else:
        out_shape = jax.ShapeDtypeStruct((tokens, width), BF16)
        out_specs = pl.BlockSpec((tokens, width), lambda r, idx: (0, 0))

    def body(*refs):
        layer_body(stashed, natural, tokens, width, *refs)

    scratch = [
        pltpu.VMEM((tokens, width), F32),
        pltpu.VMEM((tokens, width), BF16),
        pltpu.VMEM((tokens, HEAD), F32),
        pltpu.VMEM((tokens, HEAD), F32),
        pltpu.VMEM((heads * tokens, tokens), BF16),
    ] + stream_scratch(PEERS, width)
    if not natural:
        scratch.append(pltpu.VMEM((PEERS, tokens, width), BF16))
    return pl.pallas_call(
        body,
        out_shape=out_shape,
        grid_spec=pltpu.PrefetchScalarGridSpec(
            num_scalar_prefetch=1,
            grid=(PEERS,),
            in_specs=[whole(p) for p in pieces]
            + [
                pl.BlockSpec((1, 1, width), lambda r, idx: (idx[r], 0, 0)),
                pl.BlockSpec((1, 1, width), lambda r, idx: (idx[PEERS + 1], 0, 0)),
                whole(key_row),
                HBM,
            ],
            out_specs=out_specs,
            scratch_shapes=scratch,
        ),
        compiler_params=params(),
        cost_estimate=cost(2 * tokens * full * width, 2 * full * width),
        name="stash_layer" if stashed else "mix_layer",
    )(idx, *pieces, gain, gain, key_row, weight)


def project_call(idx, mixed, tiles):
    tokens, width = mixed.shape
    order = (4, 5, 2, 3, 6, 7, 0, 1)

    def body(idx, mixed, tiles, far, plus, minus, here, blocks, sems):
        copies = [
            pltpu.make_async_copy(column_block(tiles, idx[r]), blocks.at[k], sems.at[k])
            for k, r in enumerate(order)
        ]
        for each in copies:
            each.start()
        for k in range(len(order)):
            copies[k].wait()
            (far, plus, minus, here)[k // 2][k % 2] = lax.dot_general(
                mixed[...], blocks[k], NN, preferred_element_type=F32
            ).astype(BF16)

    pair = pl.BlockSpec((2, tokens, width), lambda r, idx: (0, 0, 0))
    return pl.pallas_call(
        body,
        out_shape=[jax.ShapeDtypeStruct((2, tokens, width), BF16)] * RINGX,
        grid_spec=pltpu.PrefetchScalarGridSpec(
            num_scalar_prefetch=1,
            grid=(1,),
            in_specs=[whole(mixed), HBM],
            out_specs=[pair] * RINGX,
            scratch_shapes=stream_scratch(PEERS, width),
        ),
        compiler_params=params(),
        cost_estimate=cost(16 * tokens * width * width, 16 * width * width),
        name="project",
    )(idx, mixed, tiles)


def sent_call(plan, place, held):
    _, tokens, width = held.shape
    steps = plan.shape[1]

    def body(plan, place, held, out):
        out[...] = held[...]

    def slot(t, plan, place):
        return plan[(place[0] * steps + t) * 2 + 1], 0, 0

    return pl.pallas_call(
        body,
        out_shape=jax.ShapeDtypeStruct((steps, tokens, width), BF16),
        grid_spec=pltpu.PrefetchScalarGridSpec(
            num_scalar_prefetch=2,
            grid=(steps,),
            in_specs=[pl.BlockSpec((1, tokens, width), slot)],
            out_specs=pl.BlockSpec((1, tokens, width), lambda t, plan, place: (t, 0, 0)),
        ),
        compiler_params=params(),
        cost_estimate=cost(1, 1),
        name="sent_blocks",
    )(plan.reshape(-1), place, held)


def chosen_call(plan, place, held, got, first):
    count, tokens, width = got.shape
    steps = plan.shape[1]

    def body(plan, place, held, got, out):
        side = plan[(place[1] * steps + first + pl.program_id(0)) * 2]

        @pl.when(side == 0)
        def _():
            out[...] = held[...]

        @pl.when(side != 0)
        def _():
            out[...] = got[...]

    def slot(t, plan, place):
        return plan[(place[1] * steps + first + t) * 2 + 1], 0, 0

    block = pl.BlockSpec((1, tokens, width), lambda t, plan, place: (t, 0, 0))
    return pl.pallas_call(
        body,
        out_shape=jax.ShapeDtypeStruct(got.shape, BF16),
        grid_spec=pltpu.PrefetchScalarGridSpec(
            num_scalar_prefetch=2,
            grid=(count,),
            in_specs=[pl.BlockSpec((1, tokens, width), slot), block],
            out_specs=block,
        ),
        compiler_params=params(),
        cost_estimate=cost(1, 1),
        name="chosen_blocks",
    )(plan.reshape(-1), place, held, got)


def attention_grad_call(idx, pieces, stashed, key_row, weight):
    share, width = pieces[0].shape[-2:]
    tokens = share * PEERS
    full = width * PEERS
    values, probs, normed = stashed

    def body(
        idx, pair, plus, far, minus, values, probs, normed, key_row,
        weight, out_values, out_direct, grads, total, sort_values, sort_direct, blocks, sems,
    ):
        step = pl.program_id(0)
        heads = width // HEAD

        def rows(r):
            return pl.ds(pl.multiple_of(idx[r] * share, share), share)

        @pl.when(step == 0)
        def _():
            for k in range(PEERS):
                pltpu.make_async_copy(
                    column_block(weight, k), blocks.at[k], sems.at[k]
                ).start()
            for k, part in enumerate((pair, plus, far, minus)):
                for dz in range(2):
                    for c in range(PEERS):
                        grads[c, rows(2 * k + dz)] = part[dz, c]
            total[...] = jnp.zeros_like(total)

        wait_block(weight, blocks, sems, step, column_block)
        total[...] += lax.dot_general(
            grads[step], blocks[step], NT, preferred_element_type=F32
        )

        @pl.when(step == PEERS - 1)
        def _():
            grad_mixed = total[...].astype(BF16)
            grad_probs = per_head(
                heads,
                lambda p: lax.dot_general(
                    grad_mixed[:, p], values[:, p], NT, preferred_element_type=F32
                ),
            )
            weights = probs[...]
            grad_scores = (
                weights
                * (grad_probs - jnp.sum(grad_probs * weights, -1, keepdims=True))
                / math.sqrt(HEAD)
            ).astype(BF16)
            weights = weights.astype(BF16)
            queries = normed[...]
            keys = (queries.astype(F32) * key_row[...]).astype(BF16)
            for h in range(heads):
                part = slice(h * HEAD, (h + 1) * HEAD)
                rows_of = slice(h * tokens, (h + 1) * tokens)
                grad_values = lax.dot_general(
                    weights[rows_of], grad_mixed[:, part], TN, preferred_element_type=F32
                )
                grad_query = lax.dot_general(
                    grad_scores[rows_of], keys[:, part], NN, preferred_element_type=F32
                )
                grad_keys = lax.dot_general(
                    grad_scores[rows_of], queries[:, part], TN, preferred_element_type=F32
                )
                sort_values[:, part] = grad_values.astype(BF16)
                sort_direct[:, part] = grad_query + grad_keys * key_row[:, part]
            for r in range(PEERS):
                out_values[r * share : (r + 1) * share] = sort_values[rows(r)]
                out_direct[r * share : (r + 1) * share] = sort_direct[rows(r)]

    result = pl.BlockSpec((tokens, width), lambda r, idx: (0, 0))
    return pl.pallas_call(
        body,
        out_shape=(
            jax.ShapeDtypeStruct((tokens, width), BF16),
            jax.ShapeDtypeStruct((tokens, width), F32),
        ),
        grid_spec=pltpu.PrefetchScalarGridSpec(
            num_scalar_prefetch=1,
            grid=(PEERS,),
            in_specs=[whole(p) for p in pieces]
            + [whole(values), whole(probs), whole(normed), whole(key_row)]
            + [HBM],
            out_specs=(result, result),
            scratch_shapes=[
                pltpu.VMEM((PEERS, tokens, width), BF16),
                pltpu.VMEM((tokens, width), F32),
                pltpu.VMEM((tokens, width), BF16),
                pltpu.VMEM((tokens, width), F32),
            ]
            + stream_scratch(PEERS, width),
        ),
        compiler_params=params(),
        cost_estimate=cost(2 * tokens * full * width, 2 * full * width),
        name="attention_grad",
    )(idx, *pieces, values, probs, normed, key_row, weight)


def back_project_call(idx, grad_values, direct, weight):
    tokens, width = grad_values.shape
    full = width * PEERS
    share = tokens // PEERS

    def body(
        idx, grad_values, direct, weight, here, plus, far, minus, blocks, sems
    ):
        step = pl.program_id(0)

        @pl.when(step == 0)
        def _():
            for k in range(PEERS):
                pltpu.make_async_copy(row_block(weight, k), blocks.at[k], sems.at[k]).start()

        wait_block(weight, blocks, sems, step, row_block)
        product = lax.dot_general(
            grad_values[...], blocks[step], NT, preferred_element_type=F32
        )
        mine = (step == idx[0]).astype(F32)
        product = (product + direct[...] * mine).astype(BF16)

        def piece(r):
            return product[r * share : (r + 1) * share]

        for k, part in enumerate((here, plus, far, minus)):
            for dz in range(2):
                part[dz, 0] = piece(2 * k + dz)

    return pl.pallas_call(
        body,
        out_shape=[jax.ShapeDtypeStruct((2, PEERS, share, width), BF16)] * RINGX,
        grid_spec=pltpu.PrefetchScalarGridSpec(
            num_scalar_prefetch=1,
            grid=(PEERS,),
            in_specs=[
                pl.BlockSpec((tokens, width), lambda c, idx: (0, 0)),
                pl.BlockSpec((tokens, width), lambda c, idx: (0, 0)),
                HBM,
            ],
            scratch_shapes=stream_scratch(PEERS, width),
            out_specs=[pl.BlockSpec((2, 1, share, width), lambda c, idx: (0, c, 0, 0))] * RINGX,
        ),
        compiler_params=params(),
        cost_estimate=cost(2 * tokens * full * width, 2 * full * width),
        name="back_project",
    )(idx, grad_values, direct, weight)


def norm_grad_call(parts, gain, centered, inv_std, grad_own):
    _, blocks, share, width = parts[0].shape
    full = blocks * width

    def body(*refs):
        parts, (gain, centered, inv_std, grad_own, out) = refs[:RINGX], refs[RINGX:]
        for dz in range(2):
            scaled = sum(part[dz].astype(F32) for part in parts) * gain[...]
            mid = centered[dz]
            first = jnp.sum(jnp.sum(scaled, 0), -1, keepdims=True) / full
            second = jnp.sum(jnp.sum(scaled * mid, 0), -1, keepdims=True) / full
            result = inv_std[dz][:, :1][None] * (scaled - first[None] - mid * second[None])
            if dz == 0:
                result = result + grad_own[...].astype(F32)
            out[dz] = result.astype(BF16)

    return pl.pallas_call(
        body,
        out_shape=jax.ShapeDtypeStruct(parts[0].shape, BF16),
        compiler_params=pltpu.CompilerParams(vmem_limit_bytes=VMEM_LIMIT),
        cost_estimate=cost(1, 1),
        name="norm_grad",
    )(*parts, gain, centered, inv_std, grad_own)


def swap_layout(array):
    return lax.all_to_all(array, "tp", split_axis=0, concat_axis=0, tiled=True)


def per_device(
    inputs, cotangents, carried, pending, stash, stash_plan, gain, key_gain, w_value, w_out
):
    steps = inputs.shape[0] + 1
    tokens = carried.shape[1]
    width = key_gain.shape[-1]
    share = tokens // PEERS
    me = lax.axis_index("tp")
    places = [place(me, r // 2, r % 2) for r in range(PEERS)]
    relative = jnp.stack(places + [jnp.zeros_like(me), me, me ^ 1]).astype(jnp.int32)
    natural = jnp.stack(
        [jnp.full_like(me, r) for r in range(PEERS)] + [me, me, me ^ 1]
    ).astype(jnp.int32)
    section = lax.axis_index("section")
    sections = lax.axis_size("section")
    mirror = sections - 1 - section
    gain_blocks = gain[0].reshape(PEERS, 1, width)
    held = stash[0]
    place_of = jnp.stack([mirror, section]).astype(jnp.int32)

    order = Order()
    pin = order.pin

    def from_mirror(array):
        return lax.ppermute(array, "section", [(i, sections - 1 - i) for i in range(sections)])

    def finished(parts):
        own = jnp.stack([p[0] for p in parts])
        return own, shift(pin(jnp.stack([p[1] for p in parts])), 0, 1)

    def mix(pieces):
        mixed = pin(layer_call(False, relative, pin(*pieces), gain_blocks, key_gain, tiles))
        far, plus, minus, here = pin(*project_call(relative, mixed, tiles))
        return ScatterSum(order, far, plus, minus), here

    def stash_layer(idx, pieces):
        pieces = pin(*pieces)
        pieces = pieces if isinstance(pieces, list) else [pieces]
        return pin(*layer_call(True, idx, pieces, gain_blocks, key_gain, tiles))

    is_first = section == 0
    is_last = section == sections - 1
    residual_place = (jnp.arange(2) == 0).astype(F32)[:, None, None]

    own = pin(carried[0])
    partner = shift(own, 0, 1)
    sent = pin(sent_call(stash_plan, place_of, held))
    mirrored = from_mirror(pin(sent[:1]))
    spread = swap_layout(
        pin(
            jnp.concatenate([pending, cotangents])
            .reshape(steps, PEERS, share, width)
            .transpose(1, 0, 2, 3)
        )
    )
    fwd_pair = jnp.stack([own, pin(partner)])
    fwd_gather = Gather(order, fwd_pair)
    stash_own = pin(chosen_call(stash_plan, place_of, held, pin(mirrored), 0))[0]
    stash_partner = shift(stash_own, 0, 1)
    tiles = pin(tile_call(*pin(w_value[0], w_out[0])))
    stash_gather = Gather(order, jnp.stack([stash_own, pin(stash_partner)]))
    spread = pin(spread).transpose(1, 0, 2, 3)
    grad_own = pin(spread[0])
    grad_partner = shift(grad_own, 0, 1)
    fwd_sums, here = mix(fwd_gather.done())
    grad_pair = jnp.stack([grad_own, pin(grad_partner)])
    grad_gather = Gather(order, grad_pair)
    late = from_mirror(pin(sent[1:]))

    forward_parts = []
    backward_parts = []
    grad_sums = None
    for t in range(steps):
        if t > 0:
            backward_parts.append(
                pin(
                    norm_grad_call(
                        (here_grad, *grad_sums.done()),
                        gain_blocks,
                        centered,
                        inv_std,
                        grad_pair[0],
                    )
                )
            )
            grad_hop = Hop(order, backward_parts[-1], -1)
            stashed = stash_layer(natural, (stash_later[t - 1],))
        else:
            stashed = stash_layer(relative, stash_gather.done())
            input_pairs = jnp.stack([inputs, partner_in(pin(inputs), 0)], 1)
            cotangent_pairs = jnp.stack(
                [spread[1:], partner_in(pin(spread[1:]), sections - 1)], 1
            )
        forward_parts.append(
            (
                sum(part.astype(F32) for part in (here, *fwd_sums.done()))
                + fwd_pair[:1].astype(F32) * residual_place
            ).astype(BF16)
        )
        if t + 1 < steps:
            fwd_hop = Hop(order, forward_parts[-1], 1)
        else:
            forward_last = finished(forward_parts[-1:])
        if t > 0:
            grad_pair = grad_hop.done(is_last, cotangent_pairs[t - 1])
            grad_gather = Gather(order, grad_pair)
        else:
            late = pin(chosen_call(stash_plan, place_of, held, pin(late), 1))
            stash_later = [
                lax.all_gather(late[k], "tp", axis=0) for k in range(steps - 1)
            ]
        if t + 1 < steps:
            fwd_pair = fwd_hop.done(is_first, input_pairs[t])
            fwd_gather = Gather(order, fwd_pair)
        else:
            forward_early = finished(forward_parts[:-1])
            backward_early = finished(backward_parts)
        values, probs, normed, centered, inv_std = stashed
        grad_values, direct = pin(
            *attention_grad_call(
                relative, grad_gather.done(), (values, probs, normed), key_gain, tiles
            )
        )
        here_grad, plus, far, minus = pin(
            *back_project_call(relative, grad_values, direct, tiles)
        )
        grad_sums = ScatterSum(order, far, plus, minus)
        if t + 1 < steps:
            fwd_sums, here = mix(fwd_gather.done())

    early = add(*pin(*backward_early)).transpose(1, 0, 2, 3)
    early = swap_layout(pin(early))
    last_part = norm_grad_call(
        (here_grad, *grad_sums.done()), gain_blocks, centered, inv_std, grad_pair[0]
    )
    backward_last = finished([last_part])
    forward = jnp.concatenate([add(*forward_early), add(*forward_last)])
    last = swap_layout(add(*backward_last)[0])[None]
    backward = jnp.concatenate([early.transpose(1, 0, 2, 3), last])
    return (forward[None], backward.reshape(1, steps, tokens, width))


def solution(mesh):
    return jax.shard_map(
        per_device,
        mesh=mesh,
        in_specs=(
            P(None, None, "tp"),
            P(None, None, "tp"),
            P("section", None, "tp"),
            P("section", None, "tp"),
            P("section", None, None, "tp"),
            P(),
            P("section", None),
            P("section", "tp"),
            P("section", None, "tp"),
            P("section", "tp", None),
        ),
        out_specs=(P("section", None, None, "tp"), P("section", None, None, "tp")),
        check_vma=False,
    )
```

time: 627 us -> 530 us (0.85)
  the two profiles are of different devices: /device:TPU:8 before, /device:TPU:24 now
where the time goes in v2:
time: 530 us; the launch traced here: 522 us
  waiting for transfers between devices  163 us (31%)
  Pallas kernels  155 us (29%)
  starting transfers between devices  149 us (28%)
  local copies, waits for them, and re-layouts  19.9 us (4%)
  other arithmetic  19.9 us (4%)
  between operations  15.4 us (3%)
    ppermute x58, waiting for transfers between devices, shift(): lax.ppermute(array, 'tp', [(i, place(i, dx, dz)) for i in range(PEERS)])  126 us
    ppermute x58, starting transfers between devices, shift(): lax.ppermute(array, 'tp', [(i, place(i, dx, dz)) for i in range(PEERS)])  84.8 us
    pallas_call x8, Pallas kernels, layer_call(): pl.pallas_call(body, out_shape=out_shape, grid_spec=pltpu.PrefetchScalarG...  55.4 us
    ppermute x12, starting transfers between devices, hop(): return lax.ppermute(array, ('section', 'tp'), pairs)  43.7 us
    pallas_call x4, Pallas kernels, back_project_call(): pl.pallas_call(body, out_shape=[jax.ShapeDtypeStruct((2, PEERS, share, wi...  28.6 us
    pallas_call x4, Pallas kernels, attention_grad_call(): pl.pallas_call(body, out_shape=(jax.ShapeDtypeStruct((tokens, width), BF1...  27.9 us
    ppermute x12, waiting for transfers between devices, hop(): return lax.ppermute(array, ('section', 'tp'), pairs)  21.7 us
    pallas_call x4, Pallas kernels, project_call(): pl.pallas_call(body, out_shape=[jax.ShapeDtypeStruct((2, tokens, width),...  21 us
  transfers between devices with their start and end apart: 80, of which 31 were waited for; matrix products, arithmetic and copies ran while one was open for 5% of the time, Pallas kernels for 27%

profile of v2, /device:TPU:24, one launch (start us, length us, event | category | flops | bytes accessed | tf_op | source)
XLA Modules:
  0.0 522.0 jit_solution(683960359913338724)
XLA Ops:
  12.0 7.7 %all-to-all-start = ((bf16[8,4,16,768]{3,2,1,0:T(8,128)(2,1)}), bf16[8,4,16,768]{3,2,1,0:T(8,128)(2,1)}, u32[]{:S(2)}, u32[]{:S(2)}) async-start(bf16[8,4,16,768]{3,2,1,0:T(8,128)(2,1)} %copy.21), calls=%async_computation | async-start | bytes 1572864 | tf_op jit(solution)/shard_map/all_to_all | solution.py:562
  23.4 17.1 %collective-permute-done = bf16[128,768]{1,0:T(8,128)(2,1)S(1)} collective-permute-done((bf16[128,768]{1,0:T(8,128)(2,1)S(1)}, bf16[128,768]{1,0:T(8,128)(2,1)S(1)}, u32[]{:S(2)}, u32[]{:S(2)}) %collective-permute-start) | collective-permute-done | bytes 196640 | tf_op jit(solution)/shard_map/ppermute | solution.py:38
  47.1 14.8 %weight_tiles.1 = bf16[2,8,768,768]{3,2,1,0:T(8,128)(2,1)} custom-call(bf16[6144,768]{1,0:T(8,128)(2,1)} %bitcast.139, bf16[768,6144]{1,0:T(8,128)(2,1)} %bitcast.140), custom_call_target="tpu_custom_call" | custom-call | flops 1 | bytes 1 | tf_op jit(solution)/shard_map/weight_tiles/pallas_call | solution.py:139
  72.0 7.7 %mix_layer.4.mixed = bf16[128,768]{1,0:T(8,128)(2,1)S(1)} custom-call(s32[11]{0:T(128)S(1)} %stack.120.refs_0_.idx, bf16[2,128,768]{2,1,0:T(8,128)(2,1)S(1)} %pad_maximum_fusion.7.refs_1_, bf16[2,128,768]{2,1,0:T(8,128)(2,1)} %collective-permute-done.3.refs_2_, bf16[2,128,768]{2,1,0:T(8,128)(2,1)} %collective-permute-done.4.refs_3_, ...), custom_call_target="tpu_custom_call" | custom-call | flops 1 | bytes 1 | tf_op jit(solution)/shard_map/mix_layer/pallas_call | solution.py:275
  92.5 7.5 %stash_layer.4 = (bf16[128,768]{1,0:T(8,128)(2,1)S(1)}, f32[768,128]{1,0:T(8,128)S(1)}, bf16[128,768]{1,0:T(8,128)(2,1)S(1)}, f32[2,8,16,768]{3,2,1,0:T(8,128)S(1)}, f32[2,16,128]{2,1,0:T(8,128)S(1)}) custom-call(s32[11]{0:T(128)S(1)} %stack.120.refs_0_.idx, bf16[2,128,768]{2,1,0:T(8,128)(2,1)S(1)} %pad_maximum_fusion.8.refs_1_, ...), custom_call_target="tpu_custom_call" | custom-call | flops 1 | bytes 1 | tf_op jit(solution)/shard_map/stash_layer/pallas_call | solution.py:275
  120.8 7.5 %collective-permute-done.15 = bf16[2,128,768]{2,1,0:T(8,128)(2,1)} collective-permute-done((bf16[2,128,768]{2,1,0:T(8,128)(2,1)S(1)}, bf16[2,128,768]{2,1,0:T(8,128)(2,1)}, u32[]{:S(2)}, u32[]{:S(2)}) %collective-permute-start.15) | collective-permute-done | bytes 393248 | tf_op jit(solution)/shard_map/ppermute | solution.py:49
  132.8 8.3 %collective-permute-done.19.minus = bf16[2,8,16,768]{3,2,1,0:T(8,128)(2,1)S(1)} collective-permute-done((bf16[2,8,16,768]{3,2,1,0:T(8,128)(2,1)S(1)}, bf16[2,8,16,768]{3,2,1,0:T(8,128)(2,1)S(1)}, u32[]{:S(2)}, u32[]{:S(2)}) %collective-permute-start.19) | collective-permute-done | bytes 393248 | tf_op jit(solution)/shard_map/ppermute | solution.py:38
  141.1 7.0 %attention_grad.4 = (bf16[128,768]{1,0:T(8,128)(2,1)S(1)}, f32[128,768]{1,0:T(8,128)S(1)}) custom-call(s32[11]{0:T(128)S(1)} %stack.120.refs_0_.idx, bf16[2,8,16,768]{3,2,1,0:T(8,128)(2,1)S(1)} %pad_maximum_fusion.9.pair, bf16[2,8,16,768]{3,2,1,0:T(8,128)(2,1)S(1)} %collective-permute-done.17.plus, bf16[2,8,16,768]{3,2,1,0:T(8,128)(2,1)S(1)} %collective-permute-done.18.far, ...), custom_call_target="tpu_custom_call" | custom-call | flops 1 | bytes 1 | tf_op jit(solution)/shard_map/attention_grad/pallas_call | solution.py:460
  148.1 7.3 %back_project.4 = (bf16[2,8,16,768]{3,2,1,0:T(8,128)(2,1)S(1)}, bf16[2,8,16,768]{3,2,1,0:T(8,128)(2,1)}, bf16[2,8,16,768]{3,2,1,0:T(8,128)(2,1)}, bf16[2,8,16,768]{3,2,1,0:T(8,128)(2,1)}) custom-call(s32[11]{0:T(128)S(1)} %stack.120.refs_0_.idx, bf16[128,768]{1,0:T(8,128)(2,1)S(1)} %get-tuple-element.451.grad_values, ...), custom_call_target="tpu_custom_call" | custom-call | flops 1 | bytes 1 | tf_op jit(solution)/shard_map/back_project/pallas_call | solution.py:516
  160.4 7.4 %mix_layer.5.mixed = bf16[128,768]{1,0:T(8,128)(2,1)S(1)} custom-call(s32[11]{0:T(128)S(1)} %stack.120.refs_0_.idx, bf16[2,128,768]{2,1,0:T(8,128)(2,1)S(1)} %fusion.1.refs_1_, bf16[2,128,768]{2,1,0:T(8,128)(2,1)S(1)} %collective-permute-done.20.refs_2_, bf16[2,128,768]{2,1,0:T(8,128)(2,1)S(1)} %collective-permute-done.21.refs_3_, ...), custom_call_target="tpu_custom_call" | custom-call | flops 1 | bytes 1 | tf_op jit(solution)/shard_map/mix_layer/pallas_call | solution.py:275
  189.6 6.3 %stash_layer.5 = (bf16[128,768]{1,0:T(8,128)(2,1)S(1)}, f32[768,128]{1,0:T(8,128)S(1)}, bf16[128,768]{1,0:T(8,128)(2,1)S(1)}, f32[2,8,16,768]{3,2,1,0:T(8,128)S(1)}, f32[2,16,128]{2,1,0:T(8,128)S(1)}) custom-call(s32[11]{0:T(128)S(1)} %stack.127.refs_0_, bf16[8,128,768]{2,1,0:T(8,128)(2,1)S(1)} %copy-done.5, f32[8,1,768]{2,1,0:T(1,128)S(1)} %bitcast.104, ...), custom_call_target="tpu_custom_call" | custom-call | flops 1 | bytes 1 | tf_op jit(solution)/shard_map/stash_layer/pallas_call | solution.py:275
  195.9 11.5 %collective-permute-start.30 = (bf16[2,8,16,768]{3,2,1,0:T(8,128)(2,1)S(1)}, bf16[2,8,16,768]{3,2,1,0:T(8,128)(2,1)}, u32[]{:S(2)}, u32[]{:S(2)}) collective-permute-start(bf16[2,8,16,768]{3,2,1,0:T(8,128)(2,1)S(1)} %norm_grad.4), channel_id=1, source_target_pairs={{8,1},{9,0},{10,3},{11,2},{12,5},{13,4},{14,7},{15,6},{16,9},{17,8... | collective-permute-start | bytes 1179656 | tf_op jit(solution)/shard_map/ppermute | solution.py:49
  220.7 8.0 %collective-permute-done.33 = bf16[2,128,768]{2,1,0:T(8,128)(2,1)} collective-permute-done((bf16[2,128,768]{2,1,0:T(8,128)(2,1)}, bf16[2,128,768]{2,1,0:T(8,128)(2,1)}, u32[]{:S(2)}, u32[]{:S(2)}) %collective-permute-start.33) | collective-permute-done | bytes 393248 | tf_op jit(solution)/shard_map/ppermute | solution.py:49
  238.4 12.5 %collective-permute-done.36.minus = bf16[2,8,16,768]{3,2,1,0:T(8,128)(2,1)S(1)} collective-permute-done((bf16[2,8,16,768]{3,2,1,0:T(8,128)(2,1)S(1)}, bf16[2,8,16,768]{3,2,1,0:T(8,128)(2,1)S(1)}, u32[]{:S(2)}, u32[]{:S(2)}) %collective-permute-start.36) | collective-permute-done | bytes 393248 | tf_op jit(solution)/shard_map/ppermute | solution.py:38
  250.9 7.0 %attention_grad.5 = (bf16[128,768]{1,0:T(8,128)(2,1)S(1)}, f32[128,768]{1,0:T(8,128)S(1)}) custom-call(s32[11]{0:T(128)S(1)} %stack.120.refs_0_.idx, bf16[2,8,16,768]{3,2,1,0:T(8,128)(2,1)S(1)} %fusion.2.pair, bf16[2,8,16,768]{3,2,1,0:T(8,128)(2,1)S(1)} %collective-permute-done.34.plus, bf16[2,8,16,768]{3,2,1,0:T(8,128)(2,1)S(1)} %collective-permute-done.35.far, ...), custom_call_target="tpu_custom_call" | custom-call | flops 1 | bytes 1 | tf_op jit(solution)/shard_map/attention_grad/pallas_call | solution.py:460
  257.8 7.4 %back_project.5 = (bf16[2,8,16,768]{3,2,1,0:T(8,128)(2,1)S(1)}, bf16[2,8,16,768]{3,2,1,0:T(8,128)(2,1)}, bf16[2,8,16,768]{3,2,1,0:T(8,128)(2,1)}, bf16[2,8,16,768]{3,2,1,0:T(8,128)(2,1)}) custom-call(s32[11]{0:T(128)S(1)} %stack.120.refs_0_.idx, bf16[128,768]{1,0:T(8,128)(2,1)S(1)} %get-tuple-element.534.grad_values, ...), custom_call_target="tpu_custom_call" | custom-call | flops 1 | bytes 1 | tf_op jit(solution)/shard_map/back_project/pallas_call | solution.py:516
  272.3 6.3 %stash_layer.7 = (bf16[128,768]{1,0:T(8,128)(2,1)S(1)}, f32[768,128]{1,0:T(8,128)S(1)}, bf16[128,768]{1,0:T(8,128)(2,1)S(1)}, f32[2,8,16,768]{3,2,1,0:T(8,128)S(1)}, f32[2,16,128]{2,1,0:T(8,128)S(1)}) custom-call(s32[11]{0:T(128)S(1)} %stack.127.refs_0_, bf16[8,128,768]{2,1,0:T(8,128)(2,1)S(1)} %copy-done.3, f32[8,1,768]{2,1,0:T(1,128)S(1)} %bitcast.106, ...), custom_call_target="tpu_custom_call" | custom-call | flops 1 | bytes 1 | tf_op jit(solution)/shard_map/stash_layer/pallas_call | solution.py:275
  278.6 7.6 %mix_layer.6.mixed = bf16[128,768]{1,0:T(8,128)(2,1)S(1)} custom-call(s32[11]{0:T(128)S(1)} %stack.120.refs_0_.idx, bf16[2,128,768]{2,1,0:T(8,128)(2,1)S(1)} %fusion.3.refs_1_, bf16[2,128,768]{2,1,0:T(8,128)(2,1)S(1)} %copy-done.16, bf16[2,128,768]{2,1,0:T(8,128)(2,1)} %collective-permute-done.38.refs_3_, ...), custom_call_target="tpu_custom_call" | custom-call | flops 1 | bytes 1 | tf_op jit(solution)/shard_map/mix_layer/pallas_call | solution.py:275
  313.3 6.3 %stash_layer.6 = (bf16[128,768]{1,0:T(8,128)(2,1)S(1)}, f32[768,128]{1,0:T(8,128)S(1)}, bf16[128,768]{1,0:T(8,128)(2,1)S(1)}, f32[2,8,16,768]{3,2,1,0:T(8,128)S(1)}, f32[2,16,128]{2,1,0:T(8,128)S(1)}) custom-call(s32[11]{0:T(128)S(1)} %stack.127.refs_0_, bf16[8,128,768]{2,1,0:T(8,128)(2,1)S(1)} %copy-done.4, f32[8,1,768]{2,1,0:T(1,128)S(1)} %bitcast.111, ...), custom_call_target="tpu_custom_call" | custom-call | flops 1 | bytes 1 | tf_op jit(solution)/shard_map/stash_layer/pallas_call | solution.py:275
  323.3 6.7 %collective-permute-start.50 = (bf16[2,128,768]{2,1,0:T(8,128)(2,1)S(1)}, bf16[2,128,768]{2,1,0:T(8,128)(2,1)S(1)}, u32[]{:S(2)}, u32[]{:S(2)}) collective-permute-start(bf16[2,128,768]{2,1,0:T(8,128)(2,1)S(1)} %add_convert_fusion.6), channel_id=1, source_target_pairs={{0,9},{1,8},{2,11},{3,10},{4,13},{5,12},{6,15},{7,14},{8,17},{9,16... | collective-permute-start | bytes 1179656 | tf_op jit(solution)/shard_map/ppermute | solution.py:49
  351.8 7.0 %attention_grad.6 = (bf16[128,768]{1,0:T(8,128)(2,1)S(1)}, f32[128,768]{1,0:T(8,128)S(1)}) custom-call(s32[11]{0:T(128)S(1)} %stack.120.refs_0_.idx, bf16[2,8,16,768]{3,2,1,0:T(8,128)(2,1)S(1)} %fusion.4.pair, bf16[2,8,16,768]{3,2,1,0:T(8,128)(2,1)S(1)} %collective-permute-done.51.plus, bf16[2,8,16,768]{3,2,1,0:T(8,128)(2,1)S(1)} %collective-permute-done.52.far, ...), custom_call_target="tpu_custom_call" | custom-call | flops 1 | bytes 1 | tf_op jit(solution)/shard_map/attention_grad/pallas_call | solution.py:460
  358.8 6.5 %back_project.6 = (bf16[2,8,16,768]{3,2,1,0:T(8,128)(2,1)S(1)}, bf16[2,8,16,768]{3,2,1,0:T(8,128)(2,1)S(1)}, bf16[2,8,16,768]{3,2,1,0:T(8,128)(2,1)S(1)}, bf16[2,8,16,768]{3,2,1,0:T(8,128)(2,1)S(1)}) custom-call(s32[11]{0:T(128)S(1)} %stack.120.refs_0_.idx, bf16[128,768]{1,0:T(8,128)(2,1)S(1)} %get-tuple-element.615.grad_values, ...), custom_call_target="tpu_custom_call" | custom-call | flops 1 | bytes 1 | tf_op jit(solution)/shard_map/back_project/pallas_call | solution.py:516
  372.8 6.2 %collective-permute-done.61.refs_1_ = bf16[2,8,16,768]{3,2,1,0:T(8,128)(2,1)S(1)} collective-permute-done((bf16[2,8,16,768]{3,2,1,0:T(8,128)(2,1)S(1)}, bf16[2,8,16,768]{3,2,1,0:T(8,128)(2,1)S(1)}, u32[]{:S(2)}, u32[]{:S(2)}) %collective-permute-start.61) | collective-permute-done | bytes 393248 | tf_op jit(solution)/shard_map/ppermute | solution.py:38
  379.2 8.3 %collective-permute-done.62.refs_2_ = bf16[2,8,16,768]{3,2,1,0:T(8,128)(2,1)S(1)} collective-permute-done((bf16[2,8,16,768]{3,2,1,0:T(8,128)(2,1)S(1)}, bf16[2,8,16,768]{3,2,1,0:T(8,128)(2,1)S(1)}, u32[]{:S(2)}, u32[]{:S(2)}) %collective-permute-start.62) | collective-permute-done | bytes 393248 | tf_op jit(solution)/shard_map/ppermute | solution.py:38
  403.3 6.5 %mix_layer.7.mixed = bf16[128,768]{1,0:T(8,128)(2,1)S(1)} custom-call(s32[11]{0:T(128)S(1)} %stack.120.refs_0_.idx, bf16[2,128,768]{2,1,0:T(8,128)(2,1)S(1)} %fusion.5.refs_1_, bf16[2,128,768]{2,1,0:T(8,128)(2,1)S(1)} %collective-permute-done.54.refs_2_, bf16[2,128,768]{2,1,0:T(8,128)(2,1)S(1)} %collective-permute-done.55.refs_3_, ...), custom_call_target="tpu_custom_call" | custom-call | flops 1 | bytes 1 | tf_op jit(solution)/shard_map/mix_layer/pallas_call | solution.py:275
  421.9 6.4 %collective-permute-done.57 = bf16[2,128,768]{2,1,0:T(8,128)(2,1)S(1)} collective-permute-done((bf16[2,128,768]{2,1,0:T(8,128)(2,1)S(1)}, bf16[2,128,768]{2,1,0:T(8,128)(2,1)S(1)}, u32[]{:S(2)}, u32[]{:S(2)}) %collective-permute-start.57) | collective-permute-done | bytes 393248 | tf_op jit(solution)/shard_map/ppermute | solution.py:38
  428.4 8.3 %collective-permute-done.58 = bf16[2,128,768]{2,1,0:T(8,128)(2,1)S(1)} collective-permute-done((bf16[2,128,768]{2,1,0:T(8,128)(2,1)S(1)}, bf16[2,128,768]{2,1,0:T(8,128)(2,1)S(1)}, u32[]{:S(2)}, u32[]{:S(2)}) %collective-permute-start.58) | collective-permute-done | bytes 393248 | tf_op jit(solution)/shard_map/ppermute | solution.py:38
  445.2 7.4 %collective-permute-done.69.minus = bf16[2,8,16,768]{3,2,1,0:T(8,128)(2,1)S(1)} collective-permute-done((bf16[2,8,16,768]{3,2,1,0:T(8,128)(2,1)S(1)}, bf16[2,8,16,768]{3,2,1,0:T(8,128)(2,1)S(1)}, u32[]{:S(2)}, u32[]{:S(2)}) %collective-permute-start.69) | collective-permute-done | bytes 393248 | tf_op jit(solution)/shard_map/ppermute | solution.py:38
  452.6 7.0 %attention_grad.7 = (bf16[128,768]{1,0:T(8,128)(2,1)S(1)}, f32[128,768]{1,0:T(8,128)S(1)}) custom-call(s32[11]{0:T(128)S(1)} %stack.120.refs_0_.idx, bf16[2,8,16,768]{3,2,1,0:T(8,128)(2,1)S(1)} %fusion.6.pair, bf16[2,8,16,768]{3,2,1,0:T(8,128)(2,1)S(1)} %collective-permute-done.67.plus, bf16[2,8,16,768]{3,2,1,0:T(8,128)(2,1)S(1)} %collective-permute-done.68.far, ...), custom_call_target="tpu_custom_call" | custom-call | flops 1 | bytes 1 | tf_op jit(solution)/shard_map/attention_grad/pallas_call | solution.py:460
  459.6 7.4 %back_project.7 = (bf16[2,8,16,768]{3,2,1,0:T(8,128)(2,1)S(1)}, bf16[2,8,16,768]{3,2,1,0:T(8,128)(2,1)}, bf16[2,8,16,768]{3,2,1,0:T(8,128)(2,1)}, bf16[2,8,16,768]{3,2,1,0:T(8,128)(2,1)}) custom-call(s32[11]{0:T(128)S(1)} %stack.120.refs_0_.idx, bf16[128,768]{1,0:T(8,128)(2,1)S(1)} %get-tuple-element.686.grad_values, ...), custom_call_target="tpu_custom_call" | custom-call | flops 1 | bytes 1 | tf_op jit(solution)/shard_map/back_project/pallas_call | solution.py:516
  480.8 7.6 %collective-permute-done.71.refs_2_ = bf16[2,8,16,768]{3,2,1,0:T(8,128)(2,1)S(1)} collective-permute-done((bf16[2,8,16,768]{3,2,1,0:T(8,128)(2,1)}, bf16[2,8,16,768]{3,2,1,0:T(8,128)(2,1)S(1)}, u32[]{:S(2)}, u32[]{:S(2)}) %collective-permute-start.71) | collective-permute-done | bytes 393248 | tf_op jit(solution)/shard_map/ppermute | solution.py:38
  508.1 6.0 %all-to-all-done.2 = bf16[8,16,768]{2,1,0:T(8,128)(2,1)S(1)} async-done(((bf16[8,16,768]{2,1,0:T(8,128)(2,1)}), bf16[8,16,768]{2,1,0:T(8,128)(2,1)S(1)}, u32[]{:S(2)}, u32[]{:S(2)}) %all-to-all-start.2) | async-done | bytes 196640 | tf_op jit(solution)/shard_map/all_to_all | solution.py:562
  (313 shorter events, 250.3 us)
Async XLA Ops:
  12.0 53.5 %all-to-all-start = ((bf16[8,4,16,768]{3,2,1,0:T(8,128)(2,1)}), bf16[8,4,16,768]{3,2,1,0:T(8,128)(2,1)}, u32[]{:S(2)}, u32[]{:S(2)}) async-start(bf16[8,4,16,768]{3,2,1,0:T(8,128)(2,1)} %copy.21), calls=%async_computation | async-start | bytes 1572864 | tf_op jit(solution)/shard_map/all_to_all | solution.py:562
  19.8 168.4 %all-gather.4.cloned.1.call-start = ((), (), s32[]{:S(2)}) async-start(), calls=%async_computation.3 | async-start | bytes 1769472 | tf_op jit(solution)/shard_map/all_gather | solution.py:674
  45.1 26.7 %collective-permute-start.4 = (bf16[2,128,768]{2,1,0:T(8,128)(2,1)S(1)}, bf16[2,128,768]{2,1,0:T(8,128)(2,1)}, u32[]{:S(2)}, u32[]{:S(2)}) collective-permute-start(bf16[2,128,768]{2,1,0:T(8,128)(2,1)S(1)} %pad_maximum_fusion.7.refs_1_), channel_id=1, source_target_pairs={{0,4},{1,5},{2,6},{3,7},{4,0},{5,1},{6,2},{7,3},{8,12},{9,13},{10,... | collective-permute-start | bytes 1179656 | tf_op jit(solution)/shard_map/ppermute | solution.py:38
  61.9 26.9 %collective-permute-start.7 = (bf16[2,128,768]{2,1,0:T(8,128)(2,1)S(1)}, bf16[2,128,768]{2,1,0:T(8,128)(2,1)}, u32[]{:S(2)}, u32[]{:S(2)}) collective-permute-start(bf16[2,128,768]{2,1,0:T(8,128)(2,1)S(1)} %pad_maximum_fusion.8.refs_1_), channel_id=1, source_target_pairs={{0,6},{1,7},{2,0},{3,1},{4,2},{5,3},{6,4},{7,5},{8,14},{9,15},{10,... | collective-permute-start | bytes 1179656 | tf_op jit(solution)/shard_map/ppermute | solution.py:38
  64.1 27.1 %collective-permute-start.8 = (bf16[2,128,768]{2,1,0:T(8,128)(2,1)S(1)}, bf16[2,128,768]{2,1,0:T(8,128)(2,1)}, u32[]{:S(2)}, u32[]{:S(2)}) collective-permute-start(bf16[2,128,768]{2,1,0:T(8,128)(2,1)S(1)} %pad_maximum_fusion.8.refs_1_), channel_id=1, source_target_pairs={{0,4},{1,5},{2,6},{3,7},{4,0},{5,1},{6,2},{7,3},{8,12},{9,13},{10,... | collective-permute-start | bytes 1179656 | tf_op jit(solution)/shard_map/ppermute | solution.py:38
  107.8 163.1 %all-gather.8.cloned.1.call-start = ((), (), s32[]{:S(2)}) async-start(), calls=%async_computation.5 | async-start | bytes 1769472 | tf_op jit(solution)/shard_map/all_gather | solution.py:674
  108.5 203.4 %all-gather.6.cloned.1.call-start = ((), (), s32[]{:S(2)}) async-start(), calls=%async_computation.4 | async-start | bytes 1769472 | tf_op jit(solution)/shard_map/all_gather | solution.py:674
  129.8 27.4 %collective-permute-start.20 = (bf16[2,128,768]{2,1,0:T(8,128)(2,1)S(1)}, bf16[2,128,768]{2,1,0:T(8,128)(2,1)S(1)}, u32[]{:S(2)}, u32[]{:S(2)}) collective-permute-start(bf16[2,128,768]{2,1,0:T(8,128)(2,1)S(1)} %fusion.1.refs_1_), channel_id=1, source_target_pairs={{0,6},{1,7},{2,0},{3,1},{4,2},{5,3},{6,4},{7,5},{8,14},{9,15},{10,... | collective-permute-start | bytes 1179656 | tf_op jit(solution)/shard_map/ppermute | solution.py:38
  130.6 29.9 %collective-permute-start.21 = (bf16[2,128,768]{2,1,0:T(8,128)(2,1)S(1)}, bf16[2,128,768]{2,1,0:T(8,128)(2,1)S(1)}, u32[]{:S(2)}, u32[]{:S(2)}) collective-permute-start(bf16[2,128,768]{2,1,0:T(8,128)(2,1)S(1)} %fusion.1.refs_1_), channel_id=1, source_target_pairs={{0,4},{1,5},{2,6},{3,7},{4,0},{5,1},{6,2},{7,3},{8,12},{9,13},{10,... | collective-permute-start | bytes 1179656 | tf_op jit(solution)/shard_map/ppermute | solution.py:38
  132.1 28.4 %collective-permute-start.22 = (bf16[2,128,768]{2,1,0:T(8,128)(2,1)S(1)}, bf16[2,128,768]{2,1,0:T(8,128)(2,1)}, u32[]{:S(2)}, u32[]{:S(2)}) collective-permute-start(bf16[2,128,768]{2,1,0:T(8,128)(2,1)S(1)} %fusion.1.refs_1_), channel_id=1, source_target_pairs={{0,2},{1,3},{2,4},{3,5},{4,6},{5,7},{6,0},{7,1},{8,10},{9,11},{10,... | collective-permute-start | bytes 1179656 | tf_op jit(solution)/shard_map/ppermute | solution.py:38
  157.2 26.1 %collective-permute-start.25 = (bf16[2,8,16,768]{3,2,1,0:T(8,128)(2,1)}, bf16[2,8,16,768]{3,2,1,0:T(8,128)(2,1)}, u32[]{:S(2)}, u32[]{:S(2)}) collective-permute-start(bf16[2,8,16,768]{3,2,1,0:T(8,128)(2,1)} %get-tuple-element.486), channel_id=1, source_target_pairs={{0,6},{1,7},{2,0},{3,1},{4,2},{5,3},{6,4},{7,5},{8,14},{9,15},{10,... | collective-permute-start | bytes 1179656 | tf_op jit(solution)/shard_map/ppermute | solution.py:38
  174.4 33.1 %collective-permute-start.27 = (bf16[2,128,768]{2,1,0:T(8,128)(2,1)}, bf16[2,128,768]{2,1,0:T(8,128)(2,1)}, u32[]{:S(2)}, u32[]{:S(2)}) collective-permute-start(bf16[2,128,768]{2,1,0:T(8,128)(2,1)} %get-tuple-element.505), channel_id=1, source_target_pairs={{0,2},{1,3},{2,4},{3,5},{4,6},{5,7},{6,0},{7,1},{8,10},{9,11},{10,... | collective-permute-start | bytes 1179656 | tf_op jit(solution)/shard_map/ppermute | solution.py:38
  174.8 32.6 %collective-permute-start.28 = (bf16[2,128,768]{2,1,0:T(8,128)(2,1)}, bf16[2,128,768]{2,1,0:T(8,128)(2,1)}, u32[]{:S(2)}, u32[]{:S(2)}) collective-permute-start(bf16[2,128,768]{2,1,0:T(8,128)(2,1)} %get-tuple-element.506), channel_id=1, source_target_pairs={{0,6},{1,7},{2,0},{3,1},{4,2},{5,3},{6,4},{7,5},{8,14},{9,15},{10,... | collective-permute-start | bytes 1179656 | tf_op jit(solution)/shard_map/ppermute | solution.py:38
  181.1 34.9 %collective-permute-start.31 = (bf16[3,8,16,768]{3,2,1,0:T(8,128)(2,1)}, bf16[3,8,16,768]{3,2,1,0:T(8,128)(2,1)}, u32[]{:S(2)}, u32[]{:S(2)}) collective-permute-start(bf16[3,8,16,768]{3,2,1,0:T(8,128)(2,1)} %get-tuple-element.514), channel_id=1, source_target_pairs={{120,121},{121,120},{122,123},{123,122},{124,125},{125,124},{126,1... | collective-permute-start | bytes 1769480 | tf_op jit(solution)/shard_map/ppermute | solution.py:54
  186.0 27.5 %collective-permute-start.29 = (bf16[2,8,16,768]{3,2,1,0:T(8,128)(2,1)S(1)}, bf16[2,8,16,768]{3,2,1,0:T(8,128)(2,1)}, u32[]{:S(2)}, u32[]{:S(2)}) collective-permute-start(bf16[2,8,16,768]{3,2,1,0:T(8,128)(2,1)S(1)} %norm_grad.4), channel_id=1, source_target_pairs={{8,0},{9,1},{10,2},{11,3},{12,4},{13,5},{14,6},{15,7},{16,8},{17,9... | collective-permute-start | bytes 1179656 | tf_op jit(solution)/shard_map/ppermute | solution.py:49
  218.3 32.5 %collective-permute-start.36 = (bf16[2,8,16,768]{3,2,1,0:T(8,128)(2,1)S(1)}, bf16[2,8,16,768]{3,2,1,0:T(8,128)(2,1)S(1)}, u32[]{:S(2)}, u32[]{:S(2)}) collective-permute-start(bf16[2,8,16,768]{3,2,1,0:T(8,128)(2,1)S(1)} %fusion.2.pair), channel_id=1, source_target_pairs={{0,2},{1,3},{2,4},{3,5},{4,6},{5,7},{6,0},{7,1},{8,10},{9,11},{10,... | collective-permute-start | bytes 1179656 | tf_op jit(solution)/shard_map/ppermute | solution.py:38
  230.2 36.7 %collective-permute-start.37 = (bf16[2,128,768]{2,1,0:T(8,128)(2,1)S(1)}, bf16[2,128,768]{2,1,0:T(8,128)(2,1)S(1)}, u32[]{:S(2)}, u32[]{:S(2)}) collective-permute-start(bf16[2,128,768]{2,1,0:T(8,128)(2,1)S(1)} %fusion.3.refs_1_), channel_id=1, source_target_pairs={{0,6},{1,7},{2,0},{3,1},{4,2},{5,3},{6,4},{7,5},{8,14},{9,15},{10,... | collective-permute-start | bytes 1179656 | tf_op jit(solution)/shard_map/ppermute | solution.py:38
  232.5 46.0 %collective-permute-start.38 = (bf16[2,128,768]{2,1,0:T(8,128)(2,1)S(1)}, bf16[2,128,768]{2,1,0:T(8,128)(2,1)}, u32[]{:S(2)}, u32[]{:S(2)}) collective-permute-start(bf16[2,128,768]{2,1,0:T(8,128)(2,1)S(1)} %fusion.3.refs_1_), channel_id=1, source_target_pairs={{0,4},{1,5},{2,6},{3,7},{4,0},{5,1},{6,2},{7,3},{8,12},{9,13},{10,... | collective-permute-start | bytes 1179656 | tf_op jit(solution)/shard_map/ppermute | solution.py:38
  238.4 40.2 %collective-permute-start.39 = (bf16[2,128,768]{2,1,0:T(8,128)(2,1)S(1)}, bf16[2,128,768]{2,1,0:T(8,128)(2,1)}, u32[]{:S(2)}, u32[]{:S(2)}) collective-permute-start(bf16[2,128,768]{2,1,0:T(8,128)(2,1)S(1)} %fusion.3.refs_1_), channel_id=1, source_target_pairs={{0,2},{1,3},{2,4},{3,5},{4,6},{5,7},{6,0},{7,1},{8,10},{9,11},{10,... | collective-permute-start | bytes 1179656 | tf_op jit(solution)/shard_map/ppermute | solution.py:38
  266.0 27.4 %collective-permute-start.40 = (bf16[2,8,16,768]{3,2,1,0:T(8,128)(2,1)}, bf16[2,8,16,768]{3,2,1,0:T(8,128)(2,1)}, u32[]{:S(2)}, u32[]{:S(2)}) collective-permute-start(bf16[2,8,16,768]{3,2,1,0:T(8,128)(2,1)} %get-tuple-element.567), channel_id=1, source_target_pairs={{0,4},{1,5},{2,6},{3,7},{4,0},{5,1},{6,2},{7,3},{8,12},{9,13},{10,... | collective-permute-start | bytes 1179656 | tf_op jit(solution)/shard_map/ppermute | solution.py:38
  266.8 29.8 %collective-permute-start.41 = (bf16[2,8,16,768]{3,2,1,0:T(8,128)(2,1)}, bf16[2,8,16,768]{3,2,1,0:T(8,128)(2,1)}, u32[]{:S(2)}, u32[]{:S(2)}) collective-permute-start(bf16[2,8,16,768]{3,2,1,0:T(8,128)(2,1)} %get-tuple-element.568), channel_id=1, source_target_pairs={{0,2},{1,3},{2,4},{3,5},{4,6},{5,7},{6,0},{7,1},{8,10},{9,11},{10,... | collective-permute-start | bytes 1179656 | tf_op jit(solution)/shard_map/ppermute | solution.py:38
  266.8 29.8 %collective-permute-start.42 = (bf16[2,8,16,768]{3,2,1,0:T(8,128)(2,1)}, bf16[2,8,16,768]{3,2,1,0:T(8,128)(2,1)}, u32[]{:S(2)}, u32[]{:S(2)}) collective-permute-start(bf16[2,8,16,768]{3,2,1,0:T(8,128)(2,1)} %get-tuple-element.569), channel_id=1, source_target_pairs={{0,6},{1,7},{2,0},{3,1},{4,2},{5,3},{6,4},{7,5},{8,14},{9,15},{10,... | collective-permute-start | bytes 1179656 | tf_op jit(solution)/shard_map/ppermute | solution.py:38
  291.8 27.8 %collective-permute-start.43 = (bf16[2,128,768]{2,1,0:T(8,128)(2,1)}, bf16[2,128,768]{2,1,0:T(8,128)(2,1)}, u32[]{:S(2)}, u32[]{:S(2)}) collective-permute-start(bf16[2,128,768]{2,1,0:T(8,128)(2,1)} %get-tuple-element.586), channel_id=1, source_target_pairs={{0,4},{1,5},{2,6},{3,7},{4,0},{5,1},{6,2},{7,3},{8,12},{9,13},{10,... | collective-permute-start | bytes 1179656 | tf_op jit(solution)/shard_map/ppermute | solution.py:38
  293.4 26.2 %collective-permute-start.44 = (bf16[2,128,768]{2,1,0:T(8,128)(2,1)}, bf16[2,128,768]{2,1,0:T(8,128)(2,1)}, u32[]{:S(2)}, u32[]{:S(2)}) collective-permute-start(bf16[2,128,768]{2,1,0:T(8,128)(2,1)} %get-tuple-element.587), channel_id=1, source_target_pairs={{0,2},{1,3},{2,4},{3,5},{4,6},{5,7},{6,0},{7,1},{8,10},{9,11},{10,... | collective-permute-start | bytes 1179656 | tf_op jit(solution)/shard_map/ppermute | solution.py:38
  293.4 26.3 %collective-permute-start.45 = (bf16[2,128,768]{2,1,0:T(8,128)(2,1)}, bf16[2,128,768]{2,1,0:T(8,128)(2,1)}, u32[]{:S(2)}, u32[]{:S(2)}) collective-permute-start(bf16[2,128,768]{2,1,0:T(8,128)(2,1)} %get-tuple-element.588), channel_id=1, source_target_pairs={{0,6},{1,7},{2,0},{3,1},{4,2},{5,3},{6,4},{7,5},{8,14},{9,15},{10,... | collective-permute-start | bytes 1179656 | tf_op jit(solution)/shard_map/ppermute | solution.py:38
  298.5 31.4 %collective-permute-start.47 = (bf16[2,8,16,768]{3,2,1,0:T(8,128)(2,1)S(1)}, bf16[2,8,16,768]{3,2,1,0:T(8,128)(2,1)}, u32[]{:S(2)}, u32[]{:S(2)}) collective-permute-start(bf16[2,8,16,768]{3,2,1,0:T(8,128)(2,1)S(1)} %norm_grad.5), channel_id=1, source_target_pairs={{8,0},{9,1},{10,2},{11,3},{12,4},{13,5},{14,6},{15,7},{16,8},{17,9... | collective-permute-start | bytes 1179656 | tf_op jit(solution)/shard_map/ppermute | solution.py:49
  300.5 29.5 %collective-permute-start.48 = (bf16[2,8,16,768]{3,2,1,0:T(8,128)(2,1)S(1)}, bf16[2,8,16,768]{3,2,1,0:T(8,128)(2,1)}, u32[]{:S(2)}, u32[]{:S(2)}) collective-permute-start(bf16[2,8,16,768]{3,2,1,0:T(8,128)(2,1)S(1)} %norm_grad.5), channel_id=1, source_target_pairs={{8,1},{9,0},{10,3},{11,2},{12,5},{13,4},{14,7},{15,6},{16,9},{17,8... | collective-permute-start | bytes 1179656 | tf_op jit(solution)/shard_map/ppermute | solution.py:49
  368.1 28.4 %collective-permute-start.54 = (bf16[2,128,768]{2,1,0:T(8,128)(2,1)S(1)}, bf16[2,128,768]{2,1,0:T(8,128)(2,1)S(1)}, u32[]{:S(2)}, u32[]{:S(2)}) collective-permute-start(bf16[2,128,768]{2,1,0:T(8,128)(2,1)S(1)} %fusion.5.refs_1_), channel_id=1, source_target_pairs={{0,6},{1,7},{2,0},{3,1},{4,2},{5,3},{6,4},{7,5},{8,14},{9,15},{10,... | collective-permute-start | bytes 1179656 | tf_op jit(solution)/shard_map/ppermute | solution.py:38
  372.7 27.1 %collective-permute-start.55 = (bf16[2,128,768]{2,1,0:T(8,128)(2,1)S(1)}, bf16[2,128,768]{2,1,0:T(8,128)(2,1)S(1)}, u32[]{:S(2)}, u32[]{:S(2)}) collective-permute-start(bf16[2,128,768]{2,1,0:T(8,128)(2,1)S(1)} %fusion.5.refs_1_), channel_id=1, source_target_pairs={{0,4},{1,5},{2,6},{3,7},{4,0},{5,1},{6,2},{7,3},{8,12},{9,13},{10,... | collective-permute-start | bytes 1179656 | tf_op jit(solution)/shard_map/ppermute | solution.py:38
  387.5 33.6 %collective-permute-start.46 = (bf16[3,128,768]{2,1,0:T(8,128)(2,1)S(1)}, bf16[3,128,768]{2,1,0:T(8,128)(2,1)S(1)}, u32[]{:S(2)}, u32[]{:S(2)}) collective-permute-start(bf16[3,128,768]{2,1,0:T(8,128)(2,1)S(1)} %pad_maximum_fusion.2), channel_id=1, source_target_pairs={{0,1},{1,0},{2,3},{3,2},{4,5},{5,4},{6,7},{7,6},{8,9},{9,8},{10,11... | collective-permute-start | bytes 1769480 | tf_op jit(solution)/shard_map/ppermute | solution.py:38
  436.7 35.6 %collective-permute-start.64 = (bf16[3,8,16,768]{3,2,1,0:T(8,128)(2,1)S(1)}, bf16[3,8,16,768]{3,2,1,0:T(8,128)(2,1)S(1)}, u32[]{:S(2)}, u32[]{:S(2)}) collective-permute-start(bf16[3,8,16,768]{3,2,1,0:T(8,128)(2,1)S(1)} %pad_maximum_fusion.4), channel_id=1, source_target_pairs={{0,1},{1,0},{2,3},{3,2},{4,5},{5,4},{6,7},{7,6},{8,9},{9,8},{10,11... | collective-permute-start | bytes 1769480 | tf_op jit(solution)/shard_map/ppermute | solution.py:38
  473.3 28.0 %all-to-all-start.1 = ((bf16[8,3,16,768]{3,2,1,0:T(8,128)(2,1)}), bf16[8,3,16,768]{3,2,1,0:T(8,128)(2,1)}, u32[]{:S(2)}, u32[]{:S(2)}) async-start(bf16[8,3,16,768]{3,2,1,0:T(8,128)(2,1)} %copy.24), calls=%async_computation.1 | async-start | bytes 1179648 | tf_op jit(solution)/shard_map/all_to_all | solution.py:562
  (99 other events, 1323.1 us)
Sparse Core Ops, SparseCore 0:
  107.9 68.3 all-gather.3
  178.5 61.8 all-gather.7
  242.8 69.0 all-gather.5

commit v3 on v2

--- a/solution.py
+++ b/solution.py
@@ -76,6 +76,21 @@
 
     def done(self):
         return self.pair, *self.order.pin(*self.rest)
+
+
+class GatherQuads:
+    def __init__(self, order, own):
+        self.order = order
+        own = order.pin(own)
+        far = shift(own, 2, 0)
+        self.got = own, shift(own, -1, 0), far, shift(own, 1, 0)
+
+    def second(self):
+        self.quad = jnp.stack(self.order.pin(*self.got))
+        self.other = shift(self.quad, 0, 1)
+
+    def done(self):
+        return self.quad, self.order.pin(self.other)
 
 
 class ScatterSum:
@@ -160,12 +175,9 @@
     pltpu.make_async_copy(block_of(weight, 0), blocks.at[step], sems.at[step]).wait()
 
 
-def layer_body(stashed, natural, tokens, width, *refs):
+def layer_body(stashed, count, tokens, width, *refs):
     idx = refs[0]
-    if natural:
-        pieces, rest = refs[1], refs[2:]
-    else:
-        pairs, pieces, rest = refs[1:5], refs[-1], refs[5:-1]
+    parts, pieces, rest = refs[1 : 1 + count], refs[-1], refs[1 + count : -1]
     gain, gain_own, key_row, weight = rest[:4]
     if stashed:
         out_values, out_probs, out_normed, out_centered, out_inv = rest[4:9]
@@ -180,9 +192,8 @@
     def _():
         for k in range(PEERS):
             pltpu.make_async_copy(row_block(weight, idx[k]), blocks.at[k], sems.at[k]).start()
-        if not natural:
-            for k in range(RINGX):
-                pieces[2 * k : 2 * k + 2] = pairs[k][...]
+        for k in range(PEERS):
+            pieces[k] = parts[k // 2][k % 2] if count == RINGX else parts[k % 2][k // 2]
         sums = jnp.zeros((tokens, HEAD), F32)
         squares = jnp.zeros((tokens, HEAD), F32)
         for r in range(PEERS):
@@ -236,7 +247,7 @@
 
 
 def layer_call(stashed, idx, pieces, gain, key_row, weight):
-    natural = len(pieces) == 1
+    count = len(pieces)
     tokens, width = pieces[0].shape[-2:]
     full = width * PEERS
     share = tokens // PEERS
@@ -261,7 +272,7 @@
         out_specs = pl.BlockSpec((tokens, width), lambda r, idx: (0, 0))
 
     def body(*refs):
-        layer_body(stashed, natural, tokens, width, *refs)
+        layer_body(stashed, count, tokens, width, *refs)
 
     scratch = [
         pltpu.VMEM((tokens, width), F32),
@@ -270,8 +281,7 @@
         pltpu.VMEM((tokens, HEAD), F32),
         pltpu.VMEM((heads * tokens, tokens), BF16),
     ] + stream_scratch(PEERS, width)
-    if not natural:
-        scratch.append(pltpu.VMEM((PEERS, tokens, width), BF16))
+    scratch.append(pltpu.VMEM((PEERS, tokens, width), BF16))
     return pl.pallas_call(
         body,
         out_shape=out_shape,
@@ -533,7 +543,7 @@
     )(idx, grad_values, direct, weight)
 
 
-def norm_grad_call(parts, gain, centered, inv_std, grad_own):
+def norm_grad_call(parts, gain, centered, inv_std, grad_own, last=False):
     _, blocks, share, width = parts[0].shape
     full = blocks * width
 
@@ -547,11 +557,15 @@
             result = inv_std[dz][:, :1][None] * (scaled - first[None] - mid * second[None])
             if dz == 0:
                 result = result + grad_own[...].astype(F32)
-            out[dz] = result.astype(BF16)
-
+            if last:
+                out[:, dz] = result.astype(BF16)
+            else:
+                out[dz] = result.astype(BF16)
+
+    shape = (blocks, 2, share, width) if last else parts[0].shape
     return pl.pallas_call(
         body,
-        out_shape=jax.ShapeDtypeStruct(parts[0].shape, BF16),
+        out_shape=jax.ShapeDtypeStruct(shape, BF16),
         compiler_params=pltpu.CompilerParams(vmem_limit_bytes=VMEM_LIMIT),
         cost_estimate=cost(1, 1),
         name="norm_grad",
@@ -572,9 +586,6 @@
     me = lax.axis_index("tp")
     places = [place(me, r // 2, r % 2) for r in range(PEERS)]
     relative = jnp.stack(places + [jnp.zeros_like(me), me, me ^ 1]).astype(jnp.int32)
-    natural = jnp.stack(
-        [jnp.full_like(me, r) for r in range(PEERS)] + [me, me, me ^ 1]
-    ).astype(jnp.int32)
     section = lax.axis_index("section")
     sections = lax.axis_size("section")
     mirror = sections - 1 - section
@@ -606,10 +617,6 @@
     is_last = section == sections - 1
     residual_place = (jnp.arange(2) == 0).astype(F32)[:, None, None]
 
-    own = pin(carried[0])
-    partner = shift(own, 0, 1)
-    sent = pin(sent_call(stash_plan, place_of, held))
-    mirrored = from_mirror(pin(sent[:1]))
     spread = swap_layout(
         pin(
             jnp.concatenate([pending, cotangents])
@@ -617,15 +624,19 @@
             .transpose(1, 0, 2, 3)
         )
     )
+    own = pin(carried[0])
+    partner = shift(own, 0, 1)
+    sent = pin(sent_call(stash_plan, place_of, held))
+    mirrored = from_mirror(sent[:1])
+    tiles = pin(tile_call(*pin(w_value[0], w_out[0])))
     fwd_pair = jnp.stack([own, pin(partner)])
     fwd_gather = Gather(order, fwd_pair)
     stash_own = pin(chosen_call(stash_plan, place_of, held, pin(mirrored), 0))[0]
     stash_partner = shift(stash_own, 0, 1)
-    tiles = pin(tile_call(*pin(w_value[0], w_out[0])))
-    stash_gather = Gather(order, jnp.stack([stash_own, pin(stash_partner)]))
     spread = pin(spread).transpose(1, 0, 2, 3)
     grad_own = pin(spread[0])
     grad_partner = shift(grad_own, 0, 1)
+    stash_gather = Gather(order, jnp.stack([stash_own, pin(stash_partner)]))
     fwd_sums, here = mix(fwd_gather.done())
     grad_pair = jnp.stack([grad_own, pin(grad_partner)])
     grad_gather = Gather(order, grad_pair)
@@ -633,7 +644,6 @@
 
     forward_parts = []
     backward_parts = []
-    grad_sums = None
     for t in range(steps):
         if t > 0:
             backward_parts.append(
@@ -648,13 +658,9 @@
                 )
             )
             grad_hop = Hop(order, backward_parts[-1], -1)
-            stashed = stash_layer(natural, (stash_later[t - 1],))
         else:
             stashed = stash_layer(relative, stash_gather.done())
-            input_pairs = jnp.stack([inputs, partner_in(pin(inputs), 0)], 1)
-            cotangent_pairs = jnp.stack(
-                [spread[1:], partner_in(pin(spread[1:]), sections - 1)], 1
-            )
+            grad_pieces = grad_gather.done()
         forward_parts.append(
             (
                 sum(part.astype(F32) for part in (here, *fwd_sums.done()))
@@ -666,40 +672,48 @@
         else:
             forward_last = finished(forward_parts[-1:])
         if t > 0:
+            stashed = stash_layer(relative, stash_gather.done())
             grad_pair = grad_hop.done(is_last, cotangent_pairs[t - 1])
             grad_gather = Gather(order, grad_pair)
         else:
             late = pin(chosen_call(stash_plan, place_of, held, pin(late), 1))
-            stash_later = [
-                lax.all_gather(late[k], "tp", axis=0) for k in range(steps - 1)
-            ]
+            input_pairs = jnp.stack([inputs, partner_in(pin(inputs), 0)], 1)
+            cotangent_pairs = jnp.stack(
+                [spread[1:], partner_in(pin(spread[1:]), sections - 1)], 1
+            )
+        if t + 1 == steps:
+            forward_early = finished(forward_parts[:-1])
+            backward_early = finished(backward_parts)
+        if t > 0:
+            grad_pieces = grad_gather.done()
+        values, probs, normed, centered, inv_std = stashed
+        grad_values, direct = pin(
+            *attention_grad_call(
+                relative, grad_pieces, (values, probs, normed), key_gain, tiles
+            )
+        )
         if t + 1 < steps:
             fwd_pair = fwd_hop.done(is_first, input_pairs[t])
             fwd_gather = Gather(order, fwd_pair)
-        else:
-            forward_early = finished(forward_parts[:-1])
-            backward_early = finished(backward_parts)
-        values, probs, normed, centered, inv_std = stashed
-        grad_values, direct = pin(
-            *attention_grad_call(
-                relative, grad_gather.done(), (values, probs, normed), key_gain, tiles
-            )
+        here_grad, plus, far, minus = pin(
+            *back_project_call(relative, *pin(grad_values, direct), tiles)
         )
-        here_grad, plus, far, minus = pin(
-            *back_project_call(relative, grad_values, direct, tiles)
-        )
+        if t + 1 < steps:
+            stash_gather = GatherQuads(order, late[t])
         grad_sums = ScatterSum(order, far, plus, minus)
         if t + 1 < steps:
-            fwd_sums, here = mix(fwd_gather.done())
+            pieces = fwd_gather.done()
+            fwd_sums, here = mix(pieces)
+            stash_gather.second()
 
     early = add(*pin(*backward_early)).transpose(1, 0, 2, 3)
     early = swap_layout(pin(early))
     last_part = norm_grad_call(
-        (here_grad, *grad_sums.done()), gain_blocks, centered, inv_std, grad_pair[0]
+        (here_grad, *grad_sums.done()), gain_blocks, centered, inv_std, grad_pair[0], True
     )
-    backward_last = finished([last_part])
+    last = swap_layout(last_part).reshape(RINGX, 2, 2, share, width)
+    last = add(last[:, :, 0], last[:, ::-1, 1]).reshape(1, PEERS, share, width)
     forward = jnp.concatenate([add(*forward_early), add(*forward_last)])
-    last = swap_layout(add(*backward_last)[0])[None]
     backward = jnp.concatenate([early.transpose(1, 0, 2, 3), last])
     return (forward[None], backward.reshape(1, steps, tokens, width))
 

time: 530 us -> 516 us (0.974)
  the two profiles are of different devices: /device:TPU:24 before, /device:TPU:8 now
where the time goes in v3:
time: 516 us; the launch traced here: 507 us
  starting transfers between devices  187 us (36%)
  Pallas kernels  145 us (28%)
  waiting for transfers between devices  135 us (26%)
  local copies, waits for them, and re-layouts  20.7 us (4%)
  other arithmetic  17.9 us (3%)
    ppermute x69, waiting for transfers between devices, shift(): lax.ppermute(array, 'tp', [(i, place(i, dx, dz)) for i in range(PEERS)])  120 us
    ppermute x69, starting transfers between devices, shift(): lax.ppermute(array, 'tp', [(i, place(i, dx, dz)) for i in range(PEERS)])  116 us
    pallas_call x8, Pallas kernels, layer_call(): pl.pallas_call(body, out_shape=out_shape, grid_spec=pltpu.PrefetchScalarG...  51 us
    ppermute x12, starting transfers between devices, hop(): return lax.ppermute(array, ('section', 'tp'), pairs)  49.4 us
    pallas_call x4, Pallas kernels, attention_grad_call(): pl.pallas_call(body, out_shape=(jax.ShapeDtypeStruct((tokens, width), BF1...  27.9 us
    pallas_call x4, Pallas kernels, back_project_call(): pl.pallas_call(body, out_shape=[jax.ShapeDtypeStruct((2, PEERS, share, wi...  26.1 us
    pallas_call x4, Pallas kernels, project_call(): pl.pallas_call(body, out_shape=[jax.ShapeDtypeStruct((2, tokens, width),...  20.4 us
    all_to_all x3, starting transfers between devices, swap_layout(): return lax.all_to_all(array, 'tp', split_axis=0, concat_axis=0, tiled=True)  17 us
  transfers between devices with their start and end apart: 88, of which 28 were waited for; matrix products, arithmetic and copies ran while one was open for 4% of the time, Pallas kernels for 29%

profile of v3, /device:TPU:8, one launch (start us, length us, event | category | flops | bytes accessed | tf_op | source)
XLA Modules:
  0.0 507.3 jit_solution(1847490010384116481)
XLA Ops:
  2.8 7.7 %all-to-all-start = ((bf16[8,4,16,768]{3,2,1,0:T(8,128)(2,1)}), bf16[8,4,16,768]{3,2,1,0:T(8,128)(2,1)}, u32[]{:S(2)}, u32[]{:S(2)}) async-start(bf16[8,4,16,768]{3,2,1,0:T(8,128)(2,1)} %copy.21), calls=%async_computation | async-start | bytes 1572864 | tf_op jit(solution)/shard_map/all_to_all | solution.py:576
  15.8 14.8 %weight_tiles.1 = bf16[2,8,768,768]{3,2,1,0:T(8,128)(2,1)} custom-call(bf16[6144,768]{1,0:T(8,128)(2,1)} %bitcast.156, bf16[768,6144]{1,0:T(8,128)(2,1)} %bitcast.157), custom_call_target="tpu_custom_call" | custom-call | flops 1 | bytes 1 | tf_op jit(solution)/shard_map/weight_tiles/pallas_call | solution.py:154
  57.7 7.7 %mix_layer.4.mixed = bf16[128,768]{1,0:T(8,128)(2,1)S(1)} custom-call(s32[11]{0:T(128)S(1)} %stack.159.refs_0_.idx, bf16[2,128,768]{2,1,0:T(8,128)(2,1)S(1)} %pad_maximum_fusion.10.refs_1_, bf16[2,128,768]{2,1,0:T(8,128)(2,1)} %collective-permute-done.3.refs_2_, bf16[2,128,768]{2,1,0:T(8,128)(2,1)} %collective-permute-done.4.refs_3_, ...), custom_call_target="tpu_custom_call" | custom-call | flops 1 | bytes 1 | tf_op jit(solution)/shard_map/mix_layer/pallas_call | solution.py:285
  77.1 6.4 %collective-permute-done.10.plus = bf16[2,8,16,768]{3,2,1,0:T(8,128)(2,1)S(1)} collective-permute-done((bf16[2,8,16,768]{3,2,1,0:T(8,128)(2,1)S(1)}, bf16[2,8,16,768]{3,2,1,0:T(8,128)(2,1)S(1)}, u32[]{:S(2)}, u32[]{:S(2)}) %collective-permute-start.10) | collective-permute-done | bytes 393248 | tf_op jit(solution)/shard_map/ppermute | solution.py:38
  86.2 6.1 %stash_layer.4 = (bf16[128,768]{1,0:T(8,128)(2,1)S(1)}, f32[768,128]{1,0:T(8,128)S(1)}, bf16[128,768]{1,0:T(8,128)(2,1)S(1)}, f32[2,8,16,768]{3,2,1,0:T(8,128)S(1)}, f32[2,16,128]{2,1,0:T(8,128)S(1)}) custom-call(s32[11]{0:T(128)S(1)} %stack.159.refs_0_.idx, bf16[2,128,768]{2,1,0:T(8,128)(2,1)S(1)} %pad_maximum_fusion.11.refs_1_, ...), custom_call_target="tpu_custom_call" | custom-call | flops 1 | bytes 1 | tf_op jit(solution)/shard_map/stash_layer/pallas_call | solution.py:285
  92.3 7.8 %collective-permute-done.12.minus = bf16[2,8,16,768]{3,2,1,0:T(8,128)(2,1)S(1)} collective-permute-done((bf16[2,8,16,768]{3,2,1,0:T(8,128)(2,1)S(1)}, bf16[2,8,16,768]{3,2,1,0:T(8,128)(2,1)S(1)}, u32[]{:S(2)}, u32[]{:S(2)}) %collective-permute-start.12) | collective-permute-done | bytes 393248 | tf_op jit(solution)/shard_map/ppermute | solution.py:38
  100.2 8.3 %collective-permute-done.14 = bf16[2,128,768]{2,1,0:T(8,128)(2,1)S(1)} collective-permute-done((bf16[2,128,768]{2,1,0:T(8,128)(2,1)S(1)}, bf16[2,128,768]{2,1,0:T(8,128)(2,1)S(1)}, u32[]{:S(2)}, u32[]{:S(2)}) %collective-permute-start.14) | collective-permute-done | bytes 393248 | tf_op jit(solution)/shard_map/ppermute | solution.py:38
  120.1 7.0 %attention_grad.4 = (bf16[128,768]{1,0:T(8,128)(2,1)S(1)}, f32[128,768]{1,0:T(8,128)S(1)}) custom-call(s32[11]{0:T(128)S(1)} %stack.159.refs_0_.idx, bf16[2,8,16,768]{3,2,1,0:T(8,128)(2,1)S(1)} %pad_maximum_fusion.12.pair, bf16[2,8,16,768]{3,2,1,0:T(8,128)(2,1)S(1)} %copy-done.18, bf16[2,8,16,768]{3,2,1,0:T(8,128)(2,1)S(1)} %copy-done.20, ...), custom_call_target="tpu_custom_call" | custom-call | flops 1 | bytes 1 | tf_op jit(solution)/shard_map/attention_grad/pallas_call | solution.py:470
  135.9 6.5 %back_project.4 = (bf16[2,8,16,768]{3,2,1,0:T(8,128)(2,1)S(1)}, bf16[2,8,16,768]{3,2,1,0:T(8,128)(2,1)S(1)}, bf16[2,8,16,768]{3,2,1,0:T(8,128)(2,1)S(1)}, bf16[2,8,16,768]{3,2,1,0:T(8,128)(2,1)S(1)}) custom-call(s32[11]{0:T(128)S(1)} %stack.159.refs_0_.idx, bf16[128,768]{1,0:T(8,128)(2,1)S(1)} %get-tuple-element.485.grad_values, ...), custom_call_target="tpu_custom_call" | custom-call | flops 1 | bytes 1 | tf_op jit(solution)/shard_map/back_project/pallas_call | solution.py:526
  146.0 10.5 %collective-permute-done.23 = bf16[128,768]{1,0:T(8,128)(2,1)S(1)} collective-permute-done((bf16[128,768]{1,0:T(8,128)(2,1)S(1)}, bf16[128,768]{1,0:T(8,128)(2,1)S(1)}, u32[]{:S(2)}, u32[]{:S(2)}) %collective-permute-start.23) | collective-permute-done | bytes 196640 | tf_op jit(solution)/shard_map/ppermute | solution.py:38
  163.1 6.4 %mix_layer.5.mixed = bf16[128,768]{1,0:T(8,128)(2,1)S(1)} custom-call(s32[11]{0:T(128)S(1)} %stack.159.refs_0_.idx, bf16[2,128,768]{2,1,0:T(8,128)(2,1)S(1)} %fusion.1.refs_1_, bf16[2,128,768]{2,1,0:T(8,128)(2,1)S(1)} %collective-permute-done.20.refs_2_, bf16[2,128,768]{2,1,0:T(8,128)(2,1)S(1)} %collective-permute-done.21.refs_3_, ...), custom_call_target="tpu_custom_call" | custom-call | flops 1 | bytes 1 | tf_op jit(solution)/shard_map/mix_layer/pallas_call | solution.py:285
  177.6 8.2 %collective-permute-start.32 = (bf16[4,128,768]{2,1,0:T(8,128)(2,1)S(1)}, bf16[4,128,768]{2,1,0:T(8,128)(2,1)S(1)}, u32[]{:S(2)}, u32[]{:S(2)}) collective-permute-start(bf16[4,128,768]{2,1,0:T(8,128)(2,1)S(1)} %pad_maximum_fusion.1.refs_1_), channel_id=1, source_target_pairs={{0,1},{1,0},{2,3},{3,2},{4,5},{5,4},{6,7},{7,6},{8,9},{9,8},{10,11... | collective-permute-start | bytes 2359304 | tf_op jit(solution)/shard_map/ppermute | solution.py:38
  198.2 6.0 %collective-permute-start.34 = (bf16[2,8,16,768]{3,2,1,0:T(8,128)(2,1)S(1)}, bf16[2,8,16,768]{3,2,1,0:T(8,128)(2,1)S(1)}, u32[]{:S(2)}, u32[]{:S(2)}) collective-permute-start(bf16[2,8,16,768]{3,2,1,0:T(8,128)(2,1)S(1)} %norm_grad.4), channel_id=1, source_target_pairs={{8,1},{9,0},{10,3},{11,2},{12,5},{13,4},{14,7},{15,6},{16,9},{17,8... | collective-permute-start | bytes 1179656 | tf_op jit(solution)/shard_map/ppermute | solution.py:49
  227.9 8.0 %collective-permute-done.36.plus = bf16[2,8,16,768]{3,2,1,0:T(8,128)(2,1)S(1)} collective-permute-done((bf16[2,8,16,768]{3,2,1,0:T(8,128)(2,1)S(1)}, bf16[2,8,16,768]{3,2,1,0:T(8,128)(2,1)S(1)}, u32[]{:S(2)}, u32[]{:S(2)}) %collective-permute-start.36) | collective-permute-done | bytes 393248 | tf_op jit(solution)/shard_map/ppermute | solution.py:38
  240.4 7.0 %attention_grad.5 = (bf16[128,768]{1,0:T(8,128)(2,1)S(1)}, f32[128,768]{1,0:T(8,128)S(1)}) custom-call(s32[11]{0:T(128)S(1)} %stack.159.refs_0_.idx, bf16[2,8,16,768]{3,2,1,0:T(8,128)(2,1)S(1)} %fusion.2.pair, bf16[2,8,16,768]{3,2,1,0:T(8,128)(2,1)S(1)} %collective-permute-done.36.plus, bf16[2,8,16,768]{3,2,1,0:T(8,128)(2,1)S(1)} %collective-permute-done.37.far, ...), custom_call_target="tpu_custom_call" | custom-call | flops 1 | bytes 1 | tf_op jit(solution)/shard_map/attention_grad/pallas_call | solution.py:470
  251.5 6.5 %back_project.5 = (bf16[2,8,16,768]{3,2,1,0:T(8,128)(2,1)S(1)}, bf16[2,8,16,768]{3,2,1,0:T(8,128)(2,1)S(1)}, bf16[2,8,16,768]{3,2,1,0:T(8,128)(2,1)S(1)}, bf16[2,8,16,768]{3,2,1,0:T(8,128)(2,1)S(1)}) custom-call(s32[11]{0:T(128)S(1)} %stack.159.refs_0_.idx, bf16[128,768]{1,0:T(8,128)(2,1)S(1)} %get-tuple-element.581.grad_values, ...), custom_call_target="tpu_custom_call" | custom-call | flops 1 | bytes 1 | tf_op jit(solution)/shard_map/back_project/pallas_call | solution.py:526
  261.0 10.2 %collective-permute-done.44 = bf16[128,768]{1,0:T(8,128)(2,1)S(1)} collective-permute-done((bf16[128,768]{1,0:T(8,128)(2,1)S(1)}, bf16[128,768]{1,0:T(8,128)(2,1)S(1)}, u32[]{:S(2)}, u32[]{:S(2)}) %collective-permute-start.44) | collective-permute-done | bytes 196640 | tf_op jit(solution)/shard_map/ppermute | solution.py:38
  276.7 6.5 %mix_layer.6.mixed = bf16[128,768]{1,0:T(8,128)(2,1)S(1)} custom-call(s32[11]{0:T(128)S(1)} %stack.159.refs_0_.idx, bf16[2,128,768]{2,1,0:T(8,128)(2,1)S(1)} %fusion.3.refs_1_, bf16[2,128,768]{2,1,0:T(8,128)(2,1)S(1)} %collective-permute-done.41.refs_2_, bf16[2,128,768]{2,1,0:T(8,128)(2,1)S(1)} %collective-permute-done.42.refs_3_, ...), custom_call_target="tpu_custom_call" | custom-call | flops 1 | bytes 1 | tf_op jit(solution)/shard_map/mix_layer/pallas_call | solution.py:285
  310.1 9.8 %collective-permute-start.56 = (bf16[2,8,16,768]{3,2,1,0:T(8,128)(2,1)S(1)}, bf16[2,8,16,768]{3,2,1,0:T(8,128)(2,1)S(1)}, u32[]{:S(2)}, u32[]{:S(2)}) collective-permute-start(bf16[2,8,16,768]{3,2,1,0:T(8,128)(2,1)S(1)} %norm_grad.5), channel_id=1, source_target_pairs={{8,1},{9,0},{10,3},{11,2},{12,5},{13,4},{14,7},{15,6},{16,9},{17,8... | collective-permute-start | bytes 1179656 | tf_op jit(solution)/shard_map/ppermute | solution.py:49
  338.2 6.6 %collective-permute-done.57.plus = bf16[2,8,16,768]{3,2,1,0:T(8,128)(2,1)S(1)} collective-permute-done((bf16[2,8,16,768]{3,2,1,0:T(8,128)(2,1)S(1)}, bf16[2,8,16,768]{3,2,1,0:T(8,128)(2,1)S(1)}, u32[]{:S(2)}, u32[]{:S(2)}) %collective-permute-start.57) | collective-permute-done | bytes 393248 | tf_op jit(solution)/shard_map/ppermute | solution.py:38
  348.2 7.0 %attention_grad.6 = (bf16[128,768]{1,0:T(8,128)(2,1)S(1)}, f32[128,768]{1,0:T(8,128)S(1)}) custom-call(s32[11]{0:T(128)S(1)} %stack.159.refs_0_.idx, bf16[2,8,16,768]{3,2,1,0:T(8,128)(2,1)S(1)} %fusion.4.pair, bf16[2,8,16,768]{3,2,1,0:T(8,128)(2,1)S(1)} %collective-permute-done.57.plus, bf16[2,8,16,768]{3,2,1,0:T(8,128)(2,1)S(1)} %collective-permute-done.58.far, ...), custom_call_target="tpu_custom_call" | custom-call | flops 1 | bytes 1 | tf_op jit(solution)/shard_map/attention_grad/pallas_call | solution.py:470
  355.2 6.5 %back_project.6 = (bf16[2,8,16,768]{3,2,1,0:T(8,128)(2,1)S(1)}, bf16[2,8,16,768]{3,2,1,0:T(8,128)(2,1)S(1)}, bf16[2,8,16,768]{3,2,1,0:T(8,128)(2,1)S(1)}, bf16[2,8,16,768]{3,2,1,0:T(8,128)(2,1)S(1)}) custom-call(s32[11]{0:T(128)S(1)} %stack.159.refs_0_.idx, bf16[128,768]{1,0:T(8,128)(2,1)S(1)} %get-tuple-element.675.grad_values, ...), custom_call_target="tpu_custom_call" | custom-call | flops 1 | bytes 1 | tf_op jit(solution)/shard_map/back_project/pallas_call | solution.py:526
  369.1 6.2 %collective-permute-done.68.refs_1_ = bf16[2,8,16,768]{3,2,1,0:T(8,128)(2,1)S(1)} collective-permute-done((bf16[2,8,16,768]{3,2,1,0:T(8,128)(2,1)S(1)}, bf16[2,8,16,768]{3,2,1,0:T(8,128)(2,1)S(1)}, u32[]{:S(2)}, u32[]{:S(2)}) %collective-permute-start.68) | collective-permute-done | bytes 393248 | tf_op jit(solution)/shard_map/ppermute | solution.py:38
  375.4 8.5 %collective-permute-done.69.refs_2_ = bf16[2,8,16,768]{3,2,1,0:T(8,128)(2,1)S(1)} collective-permute-done((bf16[2,8,16,768]{3,2,1,0:T(8,128)(2,1)S(1)}, bf16[2,8,16,768]{3,2,1,0:T(8,128)(2,1)S(1)}, u32[]{:S(2)}, u32[]{:S(2)}) %collective-permute-start.69) | collective-permute-done | bytes 393248 | tf_op jit(solution)/shard_map/ppermute | solution.py:38
  388.6 6.5 %collective-permute-start.76 = (bf16[2,8,16,768]{3,2,1,0:T(8,128)(2,1)S(1)}, bf16[2,8,16,768]{3,2,1,0:T(8,128)(2,1)S(1)}, u32[]{:S(2)}, u32[]{:S(2)}) collective-permute-start(bf16[2,8,16,768]{3,2,1,0:T(8,128)(2,1)S(1)} %norm_grad.6), channel_id=1, source_target_pairs={{8,0},{9,1},{10,2},{11,3},{12,4},{13,5},{14,6},{15,7},{16,8},{17,9... | collective-permute-start | bytes 1179656 | tf_op jit(solution)/shard_map/ppermute | solution.py:49
  398.3 6.5 %mix_layer.7.mixed = bf16[128,768]{1,0:T(8,128)(2,1)S(1)} custom-call(s32[11]{0:T(128)S(1)} %stack.159.refs_0_.idx, bf16[2,128,768]{2,1,0:T(8,128)(2,1)S(1)} %fusion.5.refs_1_, bf16[2,128,768]{2,1,0:T(8,128)(2,1)S(1)} %collective-permute-done.62.refs_2_, bf16[2,128,768]{2,1,0:T(8,128)(2,1)S(1)} %collective-permute-done.63.refs_3_, ...), custom_call_target="tpu_custom_call" | custom-call | flops 1 | bytes 1 | tf_op jit(solution)/shard_map/mix_layer/pallas_call | solution.py:285
  411.3 10.3 %collective-permute-start.77 = (bf16[2,8,16,768]{3,2,1,0:T(8,128)(2,1)S(1)}, bf16[2,8,16,768]{3,2,1,0:T(8,128)(2,1)S(1)}, u32[]{:S(2)}, u32[]{:S(2)}) collective-permute-start(bf16[2,8,16,768]{3,2,1,0:T(8,128)(2,1)S(1)} %norm_grad.6), channel_id=1, source_target_pairs={{8,1},{9,0},{10,3},{11,2},{12,5},{13,4},{14,7},{15,6},{16,9},{17,8... | collective-permute-start | bytes 1179656 | tf_op jit(solution)/shard_map/ppermute | solution.py:49
  444.4 9.9 %collective-permute-done.80.minus = bf16[2,8,16,768]{3,2,1,0:T(8,128)(2,1)S(1)} collective-permute-done((bf16[2,8,16,768]{3,2,1,0:T(8,128)(2,1)S(1)}, bf16[2,8,16,768]{3,2,1,0:T(8,128)(2,1)S(1)}, u32[]{:S(2)}, u32[]{:S(2)}) %collective-permute-start.80) | collective-permute-done | bytes 393248 | tf_op jit(solution)/shard_map/ppermute | solution.py:38
  455.3 7.0 %attention_grad.7 = (bf16[128,768]{1,0:T(8,128)(2,1)S(1)}, f32[128,768]{1,0:T(8,128)S(1)}) custom-call(s32[11]{0:T(128)S(1)} %stack.159.refs_0_.idx, bf16[2,8,16,768]{3,2,1,0:T(8,128)(2,1)S(1)} %fusion.6.pair, bf16[2,8,16,768]{3,2,1,0:T(8,128)(2,1)S(1)} %collective-permute-done.78.plus, bf16[2,8,16,768]{3,2,1,0:T(8,128)(2,1)S(1)} %collective-permute-done.79.far, ...), custom_call_target="tpu_custom_call" | custom-call | flops 1 | bytes 1 | tf_op jit(solution)/shard_map/attention_grad/pallas_call | solution.py:470
  462.3 6.5 %back_project.7 = (bf16[2,8,16,768]{3,2,1,0:T(8,128)(2,1)S(1)}, bf16[2,8,16,768]{3,2,1,0:T(8,128)(2,1)S(1)}, bf16[2,8,16,768]{3,2,1,0:T(8,128)(2,1)S(1)}, bf16[2,8,16,768]{3,2,1,0:T(8,128)(2,1)S(1)}) custom-call(s32[11]{0:T(128)S(1)} %stack.159.refs_0_.idx, bf16[128,768]{1,0:T(8,128)(2,1)S(1)} %get-tuple-element.750.grad_values, ...), custom_call_target="tpu_custom_call" | custom-call | flops 1 | bytes 1 | tf_op jit(solution)/shard_map/back_project/pallas_call | solution.py:526
  478.6 12.1 %collective-permute-done.83.refs_2_ = bf16[2,8,16,768]{3,2,1,0:T(8,128)(2,1)S(1)} collective-permute-done((bf16[2,8,16,768]{3,2,1,0:T(8,128)(2,1)S(1)}, bf16[2,8,16,768]{3,2,1,0:T(8,128)(2,1)S(1)}, u32[]{:S(2)}, u32[]{:S(2)}) %collective-permute-start.83) | collective-permute-done | bytes 393248 | tf_op jit(solution)/shard_map/ppermute | solution.py:38
  497.8 8.0 %all-to-all-done.2 = bf16[8,2,16,768]{3,2,1,0:T(8,128)(2,1)S(1)} async-done(((bf16[8,2,16,768]{3,2,1,0:T(8,128)(2,1)}), bf16[8,2,16,768]{3,2,1,0:T(8,128)(2,1)S(1)}, u32[]{:S(2)}, u32[]{:S(2)}) %all-to-all-start.2) | async-done | bytes 393248 | tf_op jit(solution)/shard_map/all_to_all | solution.py:576
  (312 shorter events, 252.0 us)
Async XLA Ops:
  2.8 35.2 %all-to-all-start = ((bf16[8,4,16,768]{3,2,1,0:T(8,128)(2,1)}), bf16[8,4,16,768]{3,2,1,0:T(8,128)(2,1)}, u32[]{:S(2)}, u32[]{:S(2)}) async-start(bf16[8,4,16,768]{3,2,1,0:T(8,128)(2,1)} %copy.21), calls=%async_computation | async-start | bytes 1572864 | tf_op jit(solution)/shard_map/all_to_all | solution.py:576
  41.0 29.3 %collective-permute-start.6 = (bf16[8,16,768]{2,1,0:T(8,128)(2,1)S(1)}, bf16[8,16,768]{2,1,0:T(8,128)(2,1)}, u32[]{:S(2)}, u32[]{:S(2)}) collective-permute-start(bf16[8,16,768]{2,1,0:T(8,128)(2,1)S(1)} %slice_bitcast_fusion.6.refs_7_), channel_id=1, source_target_pairs={{0,1},{1,0},{2,3},{3,2},{4,5},{5,4},{6,7},{7,6},{8,9},{9,8},{10,11... | collective-permute-start | bytes 589832 | tf_op jit(solution)/shard_map/ppermute | solution.py:38
  45.9 27.6 %collective-permute-start.7 = (bf16[2,128,768]{2,1,0:T(8,128)(2,1)S(1)}, bf16[2,128,768]{2,1,0:T(8,128)(2,1)S(1)}, u32[]{:S(2)}, u32[]{:S(2)}) collective-permute-start(bf16[2,128,768]{2,1,0:T(8,128)(2,1)S(1)} %pad_maximum_fusion.11.refs_1_), channel_id=1, source_target_pairs={{0,6},{1,7},{2,0},{3,1},{4,2},{5,3},{6,4},{7,5},{8,14},{9,15},{10,... | collective-permute-start | bytes 1179656 | tf_op jit(solution)/shard_map/ppermute | solution.py:38
  52.9 24.1 %collective-permute-start.9 = (bf16[2,128,768]{2,1,0:T(8,128)(2,1)S(1)}, bf16[2,128,768]{2,1,0:T(8,128)(2,1)S(1)}, u32[]{:S(2)}, u32[]{:S(2)}) collective-permute-start(bf16[2,128,768]{2,1,0:T(8,128)(2,1)S(1)} %pad_maximum_fusion.11.refs_1_), channel_id=1, source_target_pairs={{0,2},{1,3},{2,4},{3,5},{4,6},{5,7},{6,0},{7,1},{8,10},{9,11},{10,... | collective-permute-start | bytes 1179656 | tf_op jit(solution)/shard_map/ppermute | solution.py:38
  73.5 26.7 %collective-permute-start.13 = (bf16[2,128,768]{2,1,0:T(8,128)(2,1)S(1)}, bf16[2,128,768]{2,1,0:T(8,128)(2,1)S(1)}, u32[]{:S(2)}, u32[]{:S(2)}) collective-permute-start(bf16[2,128,768]{2,1,0:T(8,128)(2,1)S(1)} %get-tuple-element.453), channel_id=1, source_target_pairs={{0,4},{1,5},{2,6},{3,7},{4,0},{5,1},{6,2},{7,3},{8,12},{9,13},{10,... | collective-permute-start | bytes 1179656 | tf_op jit(solution)/shard_map/ppermute | solution.py:38
  75.0 25.1 %collective-permute-start.12 = (bf16[2,8,16,768]{3,2,1,0:T(8,128)(2,1)S(1)}, bf16[2,8,16,768]{3,2,1,0:T(8,128)(2,1)S(1)}, u32[]{:S(2)}, u32[]{:S(2)}) collective-permute-start(bf16[2,8,16,768]{3,2,1,0:T(8,128)(2,1)S(1)} %pad_maximum_fusion.12.pair), channel_id=1, source_target_pairs={{0,2},{1,3},{2,4},{3,5},{4,6},{5,7},{6,0},{7,1},{8,10},{9,11},{10,... | collective-permute-start | bytes 1179656 | tf_op jit(solution)/shard_map/ppermute | solution.py:38
  77.0 31.5 %collective-permute-start.14 = (bf16[2,128,768]{2,1,0:T(8,128)(2,1)S(1)}, bf16[2,128,768]{2,1,0:T(8,128)(2,1)S(1)}, u32[]{:S(2)}, u32[]{:S(2)}) collective-permute-start(bf16[2,128,768]{2,1,0:T(8,128)(2,1)S(1)} %get-tuple-element.454), channel_id=1, source_target_pairs={{0,2},{1,3},{2,4},{3,5},{4,6},{5,7},{6,0},{7,1},{8,10},{9,11},{10,... | collective-permute-start | bytes 1179656 | tf_op jit(solution)/shard_map/ppermute | solution.py:38
  83.5 25.0 %collective-permute-start.15 = (bf16[2,128,768]{2,1,0:T(8,128)(2,1)S(1)}, bf16[2,128,768]{2,1,0:T(8,128)(2,1)S(1)}, u32[]{:S(2)}, u32[]{:S(2)}) collective-permute-start(bf16[2,128,768]{2,1,0:T(8,128)(2,1)S(1)} %get-tuple-element.455), channel_id=1, source_target_pairs={{0,6},{1,7},{2,0},{3,1},{4,2},{5,3},{6,4},{7,5},{8,14},{9,15},{10,... | collective-permute-start | bytes 1179656 | tf_op jit(solution)/shard_map/ppermute | solution.py:38
  131.7 26.8 %collective-permute-start.20 = (bf16[2,128,768]{2,1,0:T(8,128)(2,1)S(1)}, bf16[2,128,768]{2,1,0:T(8,128)(2,1)S(1)}, u32[]{:S(2)}, u32[]{:S(2)}) collective-permute-start(bf16[2,128,768]{2,1,0:T(8,128)(2,1)S(1)} %fusion.1.refs_1_), channel_id=1, source_target_pairs={{0,6},{1,7},{2,0},{3,1},{4,2},{5,3},{6,4},{7,5},{8,14},{9,15},{10,... | collective-permute-start | bytes 1179656 | tf_op jit(solution)/shard_map/ppermute | solution.py:38
  132.3 27.6 %collective-permute-start.21 = (bf16[2,128,768]{2,1,0:T(8,128)(2,1)S(1)}, bf16[2,128,768]{2,1,0:T(8,128)(2,1)S(1)}, u32[]{:S(2)}, u32[]{:S(2)}) collective-permute-start(bf16[2,128,768]{2,1,0:T(8,128)(2,1)S(1)} %fusion.1.refs_1_), channel_id=1, source_target_pairs={{0,4},{1,5},{2,6},{3,7},{4,0},{5,1},{6,2},{7,3},{8,12},{9,13},{10,... | collective-permute-start | bytes 1179656 | tf_op jit(solution)/shard_map/ppermute | solution.py:38
  134.3 25.6 %collective-permute-start.22 = (bf16[2,128,768]{2,1,0:T(8,128)(2,1)S(1)}, bf16[2,128,768]{2,1,0:T(8,128)(2,1)S(1)}, u32[]{:S(2)}, u32[]{:S(2)}) collective-permute-start(bf16[2,128,768]{2,1,0:T(8,128)(2,1)S(1)} %fusion.1.refs_1_), channel_id=1, source_target_pairs={{0,2},{1,3},{2,4},{3,5},{4,6},{5,7},{6,0},{7,1},{8,10},{9,11},{10,... | collective-permute-start | bytes 1179656 | tf_op jit(solution)/shard_map/ppermute | solution.py:38
  145.6 31.2 %collective-permute-start.26 = (bf16[2,8,16,768]{3,2,1,0:T(8,128)(2,1)S(1)}, bf16[2,8,16,768]{3,2,1,0:T(8,128)(2,1)S(1)}, u32[]{:S(2)}, u32[]{:S(2)}) collective-permute-start(bf16[2,8,16,768]{3,2,1,0:T(8,128)(2,1)S(1)} %get-tuple-element.522), channel_id=1, source_target_pairs={{0,4},{1,5},{2,6},{3,7},{4,0},{5,1},{6,2},{7,3},{8,12},{9,13},{10,... | collective-permute-start | bytes 1179656 | tf_op jit(solution)/shard_map/ppermute | solution.py:38
  159.9 25.9 %collective-permute-start.27 = (bf16[2,8,16,768]{3,2,1,0:T(8,128)(2,1)S(1)}, bf16[2,8,16,768]{3,2,1,0:T(8,128)(2,1)S(1)}, u32[]{:S(2)}, u32[]{:S(2)}) collective-permute-start(bf16[2,8,16,768]{3,2,1,0:T(8,128)(2,1)S(1)} %get-tuple-element.523), channel_id=1, source_target_pairs={{0,2},{1,3},{2,4},{3,5},{4,6},{5,7},{6,0},{7,1},{8,10},{9,11},{10,... | collective-permute-start | bytes 1179656 | tf_op jit(solution)/shard_map/ppermute | solution.py:38
  160.0 29.0 %collective-permute-start.28 = (bf16[2,8,16,768]{3,2,1,0:T(8,128)(2,1)S(1)}, bf16[2,8,16,768]{3,2,1,0:T(8,128)(2,1)S(1)}, u32[]{:S(2)}, u32[]{:S(2)}) collective-permute-start(bf16[2,8,16,768]{3,2,1,0:T(8,128)(2,1)S(1)} %get-tuple-element.524), channel_id=1, source_target_pairs={{0,6},{1,7},{2,0},{3,1},{4,2},{5,3},{6,4},{7,5},{8,14},{9,15},{10,... | collective-permute-start | bytes 1179656 | tf_op jit(solution)/shard_map/ppermute | solution.py:38
  177.6 28.6 %collective-permute-start.32 = (bf16[4,128,768]{2,1,0:T(8,128)(2,1)S(1)}, bf16[4,128,768]{2,1,0:T(8,128)(2,1)S(1)}, u32[]{:S(2)}, u32[]{:S(2)}) collective-permute-start(bf16[4,128,768]{2,1,0:T(8,128)(2,1)S(1)} %pad_maximum_fusion.1.refs_1_), channel_id=1, source_target_pairs={{0,1},{1,0},{2,3},{3,2},{4,5},{5,4},{6,7},{7,6},{8,9},{9,8},{10,11... | collective-permute-start | bytes 2359304 | tf_op jit(solution)/shard_map/ppermute | solution.py:38
  189.8 28.1 %collective-permute-start.35 = (bf16[3,8,16,768]{3,2,1,0:T(8,128)(2,1)}, bf16[3,8,16,768]{3,2,1,0:T(8,128)(2,1)}, u32[]{:S(2)}, u32[]{:S(2)}) collective-permute-start(bf16[3,8,16,768]{3,2,1,0:T(8,128)(2,1)} %get-tuple-element.558), channel_id=1, source_target_pairs={{120,121},{121,120},{122,123},{123,122},{124,125},{125,124},{126,1... | collective-permute-start | bytes 1769480 | tf_op jit(solution)/shard_map/ppermute | solution.py:54
  235.9 55.5 %collective-permute-start.81 = (bf16[4,128,768]{2,1,0:T(8,128)(2,1)S(1)}, bf16[4,128,768]{2,1,0:T(8,128)(2,1)S(1)}, u32[]{:S(2)}, u32[]{:S(2)}) collective-permute-start(bf16[4,128,768]{2,1,0:T(8,128)(2,1)S(1)} %pad_maximum_fusion.3.refs_1_), channel_id=1, source_target_pairs={{0,1},{1,0},{2,3},{3,2},{4,5},{5,4},{6,7},{7,6},{8,9},{9,8},{10,11... | collective-permute-start | bytes 2359304 | tf_op jit(solution)/shard_map/ppermute | solution.py:38
  248.6 23.9 %collective-permute-start.41 = (bf16[2,128,768]{2,1,0:T(8,128)(2,1)S(1)}, bf16[2,128,768]{2,1,0:T(8,128)(2,1)S(1)}, u32[]{:S(2)}, u32[]{:S(2)}) collective-permute-start(bf16[2,128,768]{2,1,0:T(8,128)(2,1)S(1)} %fusion.3.refs_1_), channel_id=1, source_target_pairs={{0,6},{1,7},{2,0},{3,1},{4,2},{5,3},{6,4},{7,5},{8,14},{9,15},{10,... | collective-permute-start | bytes 1179656 | tf_op jit(solution)/shard_map/ppermute | solution.py:38
  251.2 24.2 %collective-permute-start.43 = (bf16[2,128,768]{2,1,0:T(8,128)(2,1)S(1)}, bf16[2,128,768]{2,1,0:T(8,128)(2,1)S(1)}, u32[]{:S(2)}, u32[]{:S(2)}) collective-permute-start(bf16[2,128,768]{2,1,0:T(8,128)(2,1)S(1)} %fusion.3.refs_1_), channel_id=1, source_target_pairs={{0,2},{1,3},{2,4},{3,5},{4,6},{5,7},{6,0},{7,1},{8,10},{9,11},{10,... | collective-permute-start | bytes 1179656 | tf_op jit(solution)/shard_map/ppermute | solution.py:38
  274.2 26.9 %collective-permute-start.47 = (bf16[2,8,16,768]{3,2,1,0:T(8,128)(2,1)S(1)}, bf16[2,8,16,768]{3,2,1,0:T(8,128)(2,1)S(1)}, u32[]{:S(2)}, u32[]{:S(2)}) collective-permute-start(bf16[2,8,16,768]{3,2,1,0:T(8,128)(2,1)S(1)} %get-tuple-element.617), channel_id=1, source_target_pairs={{0,4},{1,5},{2,6},{3,7},{4,0},{5,1},{6,2},{7,3},{8,12},{9,13},{10,... | collective-permute-start | bytes 1179656 | tf_op jit(solution)/shard_map/ppermute | solution.py:38
  275.4 26.2 %collective-permute-start.48 = (bf16[2,8,16,768]{3,2,1,0:T(8,128)(2,1)S(1)}, bf16[2,8,16,768]{3,2,1,0:T(8,128)(2,1)S(1)}, u32[]{:S(2)}, u32[]{:S(2)}) collective-permute-start(bf16[2,8,16,768]{3,2,1,0:T(8,128)(2,1)S(1)} %get-tuple-element.618), channel_id=1, source_target_pairs={{0,2},{1,3},{2,4},{3,5},{4,6},{5,7},{6,0},{7,1},{8,10},{9,11},{10,... | collective-permute-start | bytes 1179656 | tf_op jit(solution)/shard_map/ppermute | solution.py:38
  291.4 28.8 %collective-permute-start.54 = (bf16[4,128,768]{2,1,0:T(8,128)(2,1)S(1)}, bf16[4,128,768]{2,1,0:T(8,128)(2,1)S(1)}, u32[]{:S(2)}, u32[]{:S(2)}) collective-permute-start(bf16[4,128,768]{2,1,0:T(8,128)(2,1)S(1)} %pad_maximum_fusion.2.refs_1_), channel_id=1, source_target_pairs={{0,1},{1,0},{2,3},{3,2},{4,5},{5,4},{6,7},{7,6},{8,9},{9,8},{10,11... | collective-permute-start | bytes 2359304 | tf_op jit(solution)/shard_map/ppermute | solution.py:38
  334.1 28.4 %collective-permute-start.60 = (bf16[2,128,768]{2,1,0:T(8,128)(2,1)S(1)}, bf16[2,128,768]{2,1,0:T(8,128)(2,1)S(1)}, u32[]{:S(2)}, u32[]{:S(2)}) collective-permute-start(bf16[2,128,768]{2,1,0:T(8,128)(2,1)S(1)} %add_convert_fusion.6), channel_id=1, source_target_pairs={{0,8},{1,9},{2,10},{3,11},{4,12},{5,13},{6,14},{7,15},{8,16},{9,17... | collective-permute-start | bytes 1179656 | tf_op jit(solution)/shard_map/ppermute | solution.py:49
  336.0 26.5 %collective-permute-start.61 = (bf16[2,128,768]{2,1,0:T(8,128)(2,1)S(1)}, bf16[2,128,768]{2,1,0:T(8,128)(2,1)S(1)}, u32[]{:S(2)}, u32[]{:S(2)}) collective-permute-start(bf16[2,128,768]{2,1,0:T(8,128)(2,1)S(1)} %add_convert_fusion.6), channel_id=1, source_target_pairs={{0,9},{1,8},{2,11},{3,10},{4,13},{5,12},{6,15},{7,14},{8,17},{9,16... | collective-permute-start | bytes 1179656 | tf_op jit(solution)/shard_map/ppermute | solution.py:49
  363.8 24.1 %collective-permute-start.70 = (bf16[2,8,16,768]{3,2,1,0:T(8,128)(2,1)S(1)}, bf16[2,8,16,768]{3,2,1,0:T(8,128)(2,1)S(1)}, u32[]{:S(2)}, u32[]{:S(2)}) collective-permute-start(bf16[2,8,16,768]{3,2,1,0:T(8,128)(2,1)S(1)} %get-tuple-element.713), channel_id=1, source_target_pairs={{0,6},{1,7},{2,0},{3,1},{4,2},{5,3},{6,4},{7,5},{8,14},{9,15},{10,... | collective-permute-start | bytes 1179656 | tf_op jit(solution)/shard_map/ppermute | solution.py:38
  367.0 28.9 %collective-permute-start.62 = (bf16[2,128,768]{2,1,0:T(8,128)(2,1)S(1)}, bf16[2,128,768]{2,1,0:T(8,128)(2,1)S(1)}, u32[]{:S(2)}, u32[]{:S(2)}) collective-permute-start(bf16[2,128,768]{2,1,0:T(8,128)(2,1)S(1)} %fusion.5.refs_1_), channel_id=1, source_target_pairs={{0,6},{1,7},{2,0},{3,1},{4,2},{5,3},{6,4},{7,5},{8,14},{9,15},{10,... | collective-permute-start | bytes 1179656 | tf_op jit(solution)/shard_map/ppermute | solution.py:38
  367.4 28.5 %collective-permute-start.63 = (bf16[2,128,768]{2,1,0:T(8,128)(2,1)S(1)}, bf16[2,128,768]{2,1,0:T(8,128)(2,1)S(1)}, u32[]{:S(2)}, u32[]{:S(2)}) collective-permute-start(bf16[2,128,768]{2,1,0:T(8,128)(2,1)S(1)} %fusion.5.refs_1_), channel_id=1, source_target_pairs={{0,4},{1,5},{2,6},{3,7},{4,0},{5,1},{6,2},{7,3},{8,12},{9,13},{10,... | collective-permute-start | bytes 1179656 | tf_op jit(solution)/shard_map/ppermute | solution.py:38
  383.8 38.0 %collective-permute-start.53 = (bf16[3,128,768]{2,1,0:T(8,128)(2,1)S(1)}, bf16[3,128,768]{2,1,0:T(8,128)(2,1)S(1)}, u32[]{:S(2)}, u32[]{:S(2)}) collective-permute-start(bf16[3,128,768]{2,1,0:T(8,128)(2,1)S(1)} %pad_maximum_fusion.5), channel_id=1, source_target_pairs={{0,1},{1,0},{2,3},{3,2},{4,5},{5,4},{6,7},{7,6},{8,9},{9,8},{10,11... | collective-permute-start | bytes 1769480 | tf_op jit(solution)/shard_map/ppermute | solution.py:38
  388.6 36.2 %collective-permute-start.76 = (bf16[2,8,16,768]{3,2,1,0:T(8,128)(2,1)S(1)}, bf16[2,8,16,768]{3,2,1,0:T(8,128)(2,1)S(1)}, u32[]{:S(2)}, u32[]{:S(2)}) collective-permute-start(bf16[2,8,16,768]{3,2,1,0:T(8,128)(2,1)S(1)} %norm_grad.6), channel_id=1, source_target_pairs={{8,0},{9,1},{10,2},{11,3},{12,4},{13,5},{14,6},{15,7},{16,8},{17,9... | collective-permute-start | bytes 1179656 | tf_op jit(solution)/shard_map/ppermute | solution.py:49
  409.7 24.6 %collective-permute-start.71 = (bf16[2,128,768]{2,1,0:T(8,128)(2,1)S(1)}, bf16[2,128,768]{2,1,0:T(8,128)(2,1)S(1)}, u32[]{:S(2)}, u32[]{:S(2)}) collective-permute-start(bf16[2,128,768]{2,1,0:T(8,128)(2,1)S(1)} %get-tuple-element.722), channel_id=1, source_target_pairs={{0,4},{1,5},{2,6},{3,7},{4,0},{5,1},{6,2},{7,3},{8,12},{9,13},{10,... | collective-permute-start | bytes 1179656 | tf_op jit(solution)/shard_map/ppermute | solution.py:38
  410.1 25.6 %collective-permute-start.72 = (bf16[2,128,768]{2,1,0:T(8,128)(2,1)S(1)}, bf16[2,128,768]{2,1,0:T(8,128)(2,1)S(1)}, u32[]{:S(2)}, u32[]{:S(2)}) collective-permute-start(bf16[2,128,768]{2,1,0:T(8,128)(2,1)S(1)} %get-tuple-element.723), channel_id=1, source_target_pairs={{0,2},{1,3},{2,4},{3,5},{4,6},{5,7},{6,0},{7,1},{8,10},{9,11},{10,... | collective-permute-start | bytes 1179656 | tf_op jit(solution)/shard_map/ppermute | solution.py:38
  438.7 53.4 %all-to-all-start.1 = ((bf16[8,3,16,768]{3,2,1,0:T(8,128)(2,1)}), bf16[8,3,16,768]{3,2,1,0:T(8,128)(2,1)}, u32[]{:S(2)}, u32[]{:S(2)}) async-start(bf16[8,3,16,768]{3,2,1,0:T(8,128)(2,1)} %copy.24), calls=%async_computation.1 | async-start | bytes 1179648 | tf_op jit(solution)/shard_map/all_to_all | solution.py:576
  (99 other events, 1322.2 us)

commit v4 on v3

--- a/solution.py
+++ b/solution.py
@@ -661,6 +661,12 @@
         else:
             stashed = stash_layer(relative, stash_gather.done())
             grad_pieces = grad_gather.done()
+            values, probs, normed, centered, inv_std = stashed
+            grad_values, direct = pin(
+                *attention_grad_call(
+                    relative, grad_pieces, (values, probs, normed), key_gain, tiles
+                )
+            )
         forward_parts.append(
             (
                 sum(part.astype(F32) for part in (here, *fwd_sums.done()))
@@ -681,26 +687,34 @@
             cotangent_pairs = jnp.stack(
                 [spread[1:], partner_in(pin(spread[1:]), sections - 1)], 1
             )
+        if t == 0:
+            here_grad, plus, far, minus = pin(
+                *back_project_call(relative, *pin(grad_values, direct), tiles)
+            )
+            grad_sums = ScatterSum(order, far, plus, minus)
         if t + 1 == steps:
             forward_early = finished(forward_parts[:-1])
             backward_early = finished(backward_parts)
         if t > 0:
             grad_pieces = grad_gather.done()
-        values, probs, normed, centered, inv_std = stashed
-        grad_values, direct = pin(
-            *attention_grad_call(
-                relative, grad_pieces, (values, probs, normed), key_gain, tiles
+        if t > 0:
+            values, probs, normed, centered, inv_std = stashed
+            grad_values, direct = pin(
+                *attention_grad_call(
+                    relative, grad_pieces, (values, probs, normed), key_gain, tiles
+                )
             )
-        )
         if t + 1 < steps:
             fwd_pair = fwd_hop.done(is_first, input_pairs[t])
             fwd_gather = Gather(order, fwd_pair)
-        here_grad, plus, far, minus = pin(
-            *back_project_call(relative, *pin(grad_values, direct), tiles)
-        )
+        if t > 0:
+            here_grad, plus, far, minus = pin(
+                *back_project_call(relative, *pin(grad_values, direct), tiles)
+            )
         if t + 1 < steps:
             stash_gather = GatherQuads(order, late[t])
-        grad_sums = ScatterSum(order, far, plus, minus)
+        if t > 0:
+            grad_sums = ScatterSum(order, far, plus, minus)
         if t + 1 < steps:
             pieces = fwd_gather.done()
             fwd_sums, here = mix(pieces)

time: 516 us -> 509 us (0.986)
  the two profiles are of different devices: /device:TPU:8 before, /device:TPU:48 now
where the time goes in v4:
time: 509 us; the launch traced here: 500 us
  waiting for transfers between devices  166 us (33%)
  starting transfers between devices  149 us (29%)
  Pallas kernels  145 us (28%)
  other arithmetic  18.5 us (4%)
  local copies, waits for them, and re-layouts  18.4 us (4%)
    ppermute x69, waiting for transfers between devices, shift(): lax.ppermute(array, 'tp', [(i, place(i, dx, dz)) for i in range(PEERS)])  123 us
    ppermute x69, starting transfers between devices, shift(): lax.ppermute(array, 'tp', [(i, place(i, dx, dz)) for i in range(PEERS)])  103 us
    pallas_call x8, Pallas kernels, layer_call(): pl.pallas_call(body, out_shape=out_shape, grid_spec=pltpu.PrefetchScalarG...  51 us
    ppermute x12, waiting for transfers between devices, hop(): return lax.ppermute(array, ('section', 'tp'), pairs)  35.8 us
    pallas_call x4, Pallas kernels, attention_grad_call(): pl.pallas_call(body, out_shape=(jax.ShapeDtypeStruct((tokens, width), BF1...  27.9 us
    ppermute x12, starting transfers between devices, hop(): return lax.ppermute(array, ('section', 'tp'), pairs)  26.9 us
    pallas_call x4, Pallas kernels, back_project_call(): pl.pallas_call(body, out_shape=[jax.ShapeDtypeStruct((2, PEERS, share, wi...  26.1 us
    pallas_call x4, Pallas kernels, project_call(): pl.pallas_call(body, out_shape=[jax.ShapeDtypeStruct((2, tokens, width),...  20.4 us
  transfers between devices with their start and end apart: 88, of which 34 were waited for; matrix products, arithmetic and copies ran while one was open for 5% of the time, Pallas kernels for 29%

profile of v4, /device:TPU:48, one launch (start us, length us, event | category | flops | bytes accessed | tf_op | source)
XLA Modules:
  0.0 499.9 jit_solution(17950088309851671607)
XLA Ops:
  2.8 6.8 %all-to-all-start = ((bf16[8,4,16,768]{3,2,1,0:T(8,128)(2,1)}), bf16[8,4,16,768]{3,2,1,0:T(8,128)(2,1)}, u32[]{:S(2)}, u32[]{:S(2)}) async-start(bf16[8,4,16,768]{3,2,1,0:T(8,128)(2,1)} %copy.21), calls=%async_computation | async-start | bytes 1572864 | tf_op jit(solution)/shard_map/all_to_all | solution.py:576
  14.3 14.8 %weight_tiles.1 = bf16[2,8,768,768]{3,2,1,0:T(8,128)(2,1)} custom-call(bf16[6144,768]{1,0:T(8,128)(2,1)} %bitcast.156, bf16[768,6144]{1,0:T(8,128)(2,1)} %bitcast.157), custom_call_target="tpu_custom_call" | custom-call | flops 1 | bytes 1 | tf_op jit(solution)/shard_map/weight_tiles/pallas_call | solution.py:154
  56.5 7.7 %mix_layer.4.mixed = bf16[128,768]{1,0:T(8,128)(2,1)S(1)} custom-call(s32[11]{0:T(128)S(1)} %stack.159.refs_0_.idx, bf16[2,128,768]{2,1,0:T(8,128)(2,1)S(1)} %pad_maximum_fusion.10.refs_1_, bf16[2,128,768]{2,1,0:T(8,128)(2,1)} %collective-permute-done.3.refs_2_, bf16[2,128,768]{2,1,0:T(8,128)(2,1)} %collective-permute-done.4.refs_3_, ...), custom_call_target="tpu_custom_call" | custom-call | flops 1 | bytes 1 | tf_op jit(solution)/shard_map/mix_layer/pallas_call | solution.py:285
  76.4 5.8 %collective-permute-done.10.plus = bf16[2,8,16,768]{3,2,1,0:T(8,128)(2,1)S(1)} collective-permute-done((bf16[2,8,16,768]{3,2,1,0:T(8,128)(2,1)S(1)}, bf16[2,8,16,768]{3,2,1,0:T(8,128)(2,1)S(1)}, u32[]{:S(2)}, u32[]{:S(2)}) %collective-permute-start.10) | collective-permute-done | bytes 393248 | tf_op jit(solution)/shard_map/ppermute | solution.py:38
  84.4 6.1 %stash_layer.4 = (bf16[128,768]{1,0:T(8,128)(2,1)S(1)}, f32[768,128]{1,0:T(8,128)S(1)}, bf16[128,768]{1,0:T(8,128)(2,1)S(1)}, f32[2,8,16,768]{3,2,1,0:T(8,128)S(1)}, f32[2,16,128]{2,1,0:T(8,128)S(1)}) custom-call(s32[11]{0:T(128)S(1)} %stack.159.refs_0_.idx, bf16[2,128,768]{2,1,0:T(8,128)(2,1)S(1)} %pad_maximum_fusion.11.refs_1_, ...), custom_call_target="tpu_custom_call" | custom-call | flops 1 | bytes 1 | tf_op jit(solution)/shard_map/stash_layer/pallas_call | solution.py:285
  92.6 7.0 %attention_grad.4 = (bf16[128,768]{1,0:T(8,128)(2,1)S(1)}, f32[128,768]{1,0:T(8,128)S(1)}) custom-call(s32[11]{0:T(128)S(1)} %stack.159.refs_0_.idx, bf16[2,8,16,768]{3,2,1,0:T(8,128)(2,1)S(1)} %pad_maximum_fusion.12.pair, bf16[2,8,16,768]{3,2,1,0:T(8,128)(2,1)S(1)} %collective-permute-done.10.plus, bf16[2,8,16,768]{3,2,1,0:T(8,128)(2,1)S(1)} %collective-permute-done.11.far, ...), custom_call_target="tpu_custom_call" | custom-call | flops 1 | bytes 1 | tf_op jit(solution)/shard_map/attention_grad/pallas_call | solution.py:470
  101.0 6.7 %collective-permute-done.14 = bf16[2,128,768]{2,1,0:T(8,128)(2,1)S(1)} collective-permute-done((bf16[2,128,768]{2,1,0:T(8,128)(2,1)S(1)}, bf16[2,128,768]{2,1,0:T(8,128)(2,1)S(1)}, u32[]{:S(2)}, u32[]{:S(2)}) %collective-permute-start.14) | collective-permute-done | bytes 393248 | tf_op jit(solution)/shard_map/ppermute | solution.py:38
  117.9 6.5 %back_project.4 = (bf16[2,8,16,768]{3,2,1,0:T(8,128)(2,1)S(1)}, bf16[2,8,16,768]{3,2,1,0:T(8,128)(2,1)S(1)}, bf16[2,8,16,768]{3,2,1,0:T(8,128)(2,1)S(1)}, bf16[2,8,16,768]{3,2,1,0:T(8,128)(2,1)S(1)}) custom-call(s32[11]{0:T(128)S(1)} %stack.159.refs_0_.idx, bf16[128,768]{1,0:T(8,128)(2,1)S(1)} %get-tuple-element.479.grad_values, f32[128,768]{1,0:T(8,128)S(1)} %copy-done.16, ...), custom_call_target="tpu_custom_call" | custom-call | flops 1 | bytes 1 | tf_op jit(solution)/shard_map/back_project/pallas_call | solution.py:526
  135.1 17.3 %collective-permute-done.23 = bf16[128,768]{1,0:T(8,128)(2,1)S(1)} collective-permute-done((bf16[128,768]{1,0:T(8,128)(2,1)S(1)}, bf16[128,768]{1,0:T(8,128)(2,1)S(1)}, u32[]{:S(2)}, u32[]{:S(2)}) %collective-permute-start.23) | collective-permute-done | bytes 196640 | tf_op jit(solution)/shard_map/ppermute | solution.py:38
  158.3 6.5 %mix_layer.5.mixed = bf16[128,768]{1,0:T(8,128)(2,1)S(1)} custom-call(s32[11]{0:T(128)S(1)} %stack.159.refs_0_.idx, bf16[2,128,768]{2,1,0:T(8,128)(2,1)S(1)} %fusion.1.refs_1_, bf16[2,128,768]{2,1,0:T(8,128)(2,1)S(1)} %collective-permute-done.20.refs_2_, bf16[2,128,768]{2,1,0:T(8,128)(2,1)S(1)} %collective-permute-done.21.refs_3_, ...), custom_call_target="tpu_custom_call" | custom-call | flops 1 | bytes 1 | tf_op jit(solution)/shard_map/mix_layer/pallas_call | solution.py:285
  164.8 5.6 %project.5 = (bf16[2,128,768]{2,1,0:T(8,128)(2,1)}, bf16[2,128,768]{2,1,0:T(8,128)(2,1)}, bf16[2,128,768]{2,1,0:T(8,128)(2,1)}, bf16[2,128,768]{2,1,0:T(8,128)(2,1)S(1)}) custom-call(s32[11]{0:T(128)S(1)} %stack.159.refs_0_.idx, bf16[128,768]{1,0:T(8,128)(2,1)S(1)} %mix_layer.5.mixed, bf16[16,768,768]{2,1,0:T(8,128)(2,1)} %bitcast.142), custom_call_target="tpu_custom_call" | custom-call | flops 1 | bytes 1 | tf_op jit(solution)/shard_map/project/pallas_call | solution.py:325
  200.0 5.9 %stash_layer.5 = (bf16[128,768]{1,0:T(8,128)(2,1)S(1)}, f32[768,128]{1,0:T(8,128)S(1)}, bf16[128,768]{1,0:T(8,128)(2,1)S(1)}, f32[2,8,16,768]{3,2,1,0:T(8,128)S(1)}, f32[2,16,128]{2,1,0:T(8,128)S(1)}) custom-call(s32[11]{0:T(128)S(1)} %stack.159.refs_0_.idx, bf16[4,128,768]{2,1,0:T(8,128)(2,1)S(1)} %pad_maximum_fusion.1.refs_1_, ...), custom_call_target="tpu_custom_call" | custom-call | flops 1 | bytes 1 | tf_op jit(solution)/shard_map/stash_layer/pallas_call | solution.py:285
  214.4 8.5 %collective-permute-done.67 = bf16[128,768]{1,0:T(8,128)(2,1)S(1)} collective-permute-done((bf16[128,768]{1,0:T(8,128)(2,1)S(1)}, bf16[128,768]{1,0:T(8,128)(2,1)S(1)}, u32[]{:S(2)}, u32[]{:S(2)}) %collective-permute-start.67) | collective-permute-done | bytes 196640 | tf_op jit(solution)/shard_map/ppermute | solution.py:38
  231.6 7.0 %attention_grad.5 = (bf16[128,768]{1,0:T(8,128)(2,1)S(1)}, f32[128,768]{1,0:T(8,128)S(1)}) custom-call(s32[11]{0:T(128)S(1)} %stack.159.refs_0_.idx, bf16[2,8,16,768]{3,2,1,0:T(8,128)(2,1)S(1)} %fusion.2.pair, bf16[2,8,16,768]{3,2,1,0:T(8,128)(2,1)S(1)} %collective-permute-done.36.plus, bf16[2,8,16,768]{3,2,1,0:T(8,128)(2,1)S(1)} %collective-permute-done.37.far, ...), custom_call_target="tpu_custom_call" | custom-call | flops 1 | bytes 1 | tf_op jit(solution)/shard_map/attention_grad/pallas_call | solution.py:470
  238.6 14.5 %collective-permute-done.40 = bf16[2,128,768]{2,1,0:T(8,128)(2,1)S(1)} collective-permute-done((bf16[2,128,768]{2,1,0:T(8,128)(2,1)S(1)}, bf16[2,128,768]{2,1,0:T(8,128)(2,1)S(1)}, u32[]{:S(2)}, u32[]{:S(2)}) %collective-permute-start.40) | collective-permute-done | bytes 393248 | tf_op jit(solution)/shard_map/ppermute | solution.py:49
  256.4 6.5 %back_project.5 = (bf16[2,8,16,768]{3,2,1,0:T(8,128)(2,1)S(1)}, bf16[2,8,16,768]{3,2,1,0:T(8,128)(2,1)S(1)}, bf16[2,8,16,768]{3,2,1,0:T(8,128)(2,1)S(1)}, bf16[2,8,16,768]{3,2,1,0:T(8,128)(2,1)S(1)}) custom-call(s32[11]{0:T(128)S(1)} %stack.159.refs_0_.idx, bf16[128,768]{1,0:T(8,128)(2,1)S(1)} %get-tuple-element.581.grad_values, ...), custom_call_target="tpu_custom_call" | custom-call | flops 1 | bytes 1 | tf_op jit(solution)/shard_map/back_project/pallas_call | solution.py:526
  265.7 9.1 %collective-permute-done.44 = bf16[128,768]{1,0:T(8,128)(2,1)S(1)} collective-permute-done((bf16[128,768]{1,0:T(8,128)(2,1)S(1)}, bf16[128,768]{1,0:T(8,128)(2,1)S(1)}, u32[]{:S(2)}, u32[]{:S(2)}) %collective-permute-start.44) | collective-permute-done | bytes 196640 | tf_op jit(solution)/shard_map/ppermute | solution.py:38
  279.1 6.5 %mix_layer.6.mixed = bf16[128,768]{1,0:T(8,128)(2,1)S(1)} custom-call(s32[11]{0:T(128)S(1)} %stack.159.refs_0_.idx, bf16[2,128,768]{2,1,0:T(8,128)(2,1)S(1)} %fusion.3.refs_1_, bf16[2,128,768]{2,1,0:T(8,128)(2,1)S(1)} %collective-permute-done.41.refs_2_, bf16[2,128,768]{2,1,0:T(8,128)(2,1)S(1)} %collective-permute-done.42.refs_3_, ...), custom_call_target="tpu_custom_call" | custom-call | flops 1 | bytes 1 | tf_op jit(solution)/shard_map/mix_layer/pallas_call | solution.py:285
  297.4 5.9 %stash_layer.7 = (bf16[128,768]{1,0:T(8,128)(2,1)S(1)}, f32[768,128]{1,0:T(8,128)S(1)}, bf16[128,768]{1,0:T(8,128)(2,1)S(1)}, f32[2,8,16,768]{3,2,1,0:T(8,128)S(1)}, f32[2,16,128]{2,1,0:T(8,128)S(1)}) custom-call(s32[11]{0:T(128)S(1)} %stack.159.refs_0_.idx, bf16[4,128,768]{2,1,0:T(8,128)(2,1)S(1)} %pad_maximum_fusion.3.refs_1_, ...), custom_call_target="tpu_custom_call" | custom-call | flops 1 | bytes 1 | tf_op jit(solution)/shard_map/stash_layer/pallas_call | solution.py:285
  312.7 5.9 %stash_layer.6 = (bf16[128,768]{1,0:T(8,128)(2,1)S(1)}, f32[768,128]{1,0:T(8,128)S(1)}, bf16[128,768]{1,0:T(8,128)(2,1)S(1)}, f32[2,8,16,768]{3,2,1,0:T(8,128)S(1)}, f32[2,16,128]{2,1,0:T(8,128)S(1)}) custom-call(s32[11]{0:T(128)S(1)} %stack.159.refs_0_.idx, bf16[4,128,768]{2,1,0:T(8,128)(2,1)S(1)} %pad_maximum_fusion.2.refs_1_, ...), custom_call_target="tpu_custom_call" | custom-call | flops 1 | bytes 1 | tf_op jit(solution)/shard_map/stash_layer/pallas_call | solution.py:285
  339.2 6.4 %collective-permute-done.59.minus = bf16[2,8,16,768]{3,2,1,0:T(8,128)(2,1)S(1)} collective-permute-done((bf16[2,8,16,768]{3,2,1,0:T(8,128)(2,1)S(1)}, bf16[2,8,16,768]{3,2,1,0:T(8,128)(2,1)S(1)}, u32[]{:S(2)}, u32[]{:S(2)}) %collective-permute-start.59) | collective-permute-done | bytes 393248 | tf_op jit(solution)/shard_map/ppermute | solution.py:38
  345.6 7.0 %attention_grad.6 = (bf16[128,768]{1,0:T(8,128)(2,1)S(1)}, f32[128,768]{1,0:T(8,128)S(1)}) custom-call(s32[11]{0:T(128)S(1)} %stack.159.refs_0_.idx, bf16[2,8,16,768]{3,2,1,0:T(8,128)(2,1)S(1)} %fusion.4.pair, bf16[2,8,16,768]{3,2,1,0:T(8,128)(2,1)S(1)} %collective-permute-done.57.plus, bf16[2,8,16,768]{3,2,1,0:T(8,128)(2,1)S(1)} %collective-permute-done.58.far, ...), custom_call_target="tpu_custom_call" | custom-call | flops 1 | bytes 1 | tf_op jit(solution)/shard_map/attention_grad/pallas_call | solution.py:470
  352.6 6.5 %back_project.6 = (bf16[2,8,16,768]{3,2,1,0:T(8,128)(2,1)S(1)}, bf16[2,8,16,768]{3,2,1,0:T(8,128)(2,1)S(1)}, bf16[2,8,16,768]{3,2,1,0:T(8,128)(2,1)S(1)}, bf16[2,8,16,768]{3,2,1,0:T(8,128)(2,1)S(1)}) custom-call(s32[11]{0:T(128)S(1)} %stack.159.refs_0_.idx, bf16[128,768]{1,0:T(8,128)(2,1)S(1)} %get-tuple-element.675.grad_values, ...), custom_call_target="tpu_custom_call" | custom-call | flops 1 | bytes 1 | tf_op jit(solution)/shard_map/back_project/pallas_call | solution.py:526
  366.7 6.0 %collective-permute-done.68.refs_1_ = bf16[2,8,16,768]{3,2,1,0:T(8,128)(2,1)S(1)} collective-permute-done((bf16[2,8,16,768]{3,2,1,0:T(8,128)(2,1)S(1)}, bf16[2,8,16,768]{3,2,1,0:T(8,128)(2,1)S(1)}, u32[]{:S(2)}, u32[]{:S(2)}) %collective-permute-start.68) | collective-permute-done | bytes 393248 | tf_op jit(solution)/shard_map/ppermute | solution.py:38
  372.8 8.5 %collective-permute-done.69.refs_2_ = bf16[2,8,16,768]{3,2,1,0:T(8,128)(2,1)S(1)} collective-permute-done((bf16[2,8,16,768]{3,2,1,0:T(8,128)(2,1)S(1)}, bf16[2,8,16,768]{3,2,1,0:T(8,128)(2,1)S(1)}, u32[]{:S(2)}, u32[]{:S(2)}) %collective-permute-start.69) | collective-permute-done | bytes 393248 | tf_op jit(solution)/shard_map/ppermute | solution.py:38
  389.6 7.4 %collective-permute-done.64.refs_4_ = bf16[2,128,768]{2,1,0:T(8,128)(2,1)S(1)} collective-permute-done((bf16[2,128,768]{2,1,0:T(8,128)(2,1)S(1)}, bf16[2,128,768]{2,1,0:T(8,128)(2,1)S(1)}, u32[]{:S(2)}, u32[]{:S(2)}) %collective-permute-start.64) | collective-permute-done | bytes 393248 | tf_op jit(solution)/shard_map/ppermute | solution.py:38
  397.0 6.5 %mix_layer.7.mixed = bf16[128,768]{1,0:T(8,128)(2,1)S(1)} custom-call(s32[11]{0:T(128)S(1)} %stack.159.refs_0_.idx, bf16[2,128,768]{2,1,0:T(8,128)(2,1)S(1)} %fusion.5.refs_1_, bf16[2,128,768]{2,1,0:T(8,128)(2,1)S(1)} %collective-permute-done.62.refs_2_, bf16[2,128,768]{2,1,0:T(8,128)(2,1)S(1)} %collective-permute-done.63.refs_3_, ...), custom_call_target="tpu_custom_call" | custom-call | flops 1 | bytes 1 | tf_op jit(solution)/shard_map/mix_layer/pallas_call | solution.py:285
  418.5 13.6 %collective-permute-done.77 = bf16[2,8,16,768]{3,2,1,0:T(8,128)(2,1)S(1)} collective-permute-done((bf16[2,8,16,768]{3,2,1,0:T(8,128)(2,1)S(1)}, bf16[2,8,16,768]{3,2,1,0:T(8,128)(2,1)S(1)}, u32[]{:S(2)}, u32[]{:S(2)}) %collective-permute-start.77) | collective-permute-done | bytes 393248 | tf_op jit(solution)/shard_map/ppermute | solution.py:49
  447.2 6.5 %collective-permute-done.80.minus = bf16[2,8,16,768]{3,2,1,0:T(8,128)(2,1)S(1)} collective-permute-done((bf16[2,8,16,768]{3,2,1,0:T(8,128)(2,1)S(1)}, bf16[2,8,16,768]{3,2,1,0:T(8,128)(2,1)S(1)}, u32[]{:S(2)}, u32[]{:S(2)}) %collective-permute-start.80) | collective-permute-done | bytes 393248 | tf_op jit(solution)/shard_map/ppermute | solution.py:38
  454.7 7.0 %attention_grad.7 = (bf16[128,768]{1,0:T(8,128)(2,1)S(1)}, f32[128,768]{1,0:T(8,128)S(1)}) custom-call(s32[11]{0:T(128)S(1)} %stack.159.refs_0_.idx, bf16[2,8,16,768]{3,2,1,0:T(8,128)(2,1)S(1)} %fusion.6.pair, bf16[2,8,16,768]{3,2,1,0:T(8,128)(2,1)S(1)} %collective-permute-done.78.plus, bf16[2,8,16,768]{3,2,1,0:T(8,128)(2,1)S(1)} %collective-permute-done.79.far, ...), custom_call_target="tpu_custom_call" | custom-call | flops 1 | bytes 1 | tf_op jit(solution)/shard_map/attention_grad/pallas_call | solution.py:470
  461.7 6.5 %back_project.7 = (bf16[2,8,16,768]{3,2,1,0:T(8,128)(2,1)S(1)}, bf16[2,8,16,768]{3,2,1,0:T(8,128)(2,1)S(1)}, bf16[2,8,16,768]{3,2,1,0:T(8,128)(2,1)S(1)}, bf16[2,8,16,768]{3,2,1,0:T(8,128)(2,1)S(1)}) custom-call(s32[11]{0:T(128)S(1)} %stack.159.refs_0_.idx, bf16[128,768]{1,0:T(8,128)(2,1)S(1)} %get-tuple-element.750.grad_values, ...), custom_call_target="tpu_custom_call" | custom-call | flops 1 | bytes 1 | tf_op jit(solution)/shard_map/back_project/pallas_call | solution.py:526
  491.6 6.8 %all-to-all-done.2 = bf16[8,2,16,768]{3,2,1,0:T(8,128)(2,1)S(1)} async-done(((bf16[8,2,16,768]{3,2,1,0:T(8,128)(2,1)}), bf16[8,2,16,768]{3,2,1,0:T(8,128)(2,1)S(1)}, u32[]{:S(2)}, u32[]{:S(2)}) %all-to-all-start.2) | async-done | bytes 393248 | tf_op jit(solution)/shard_map/all_to_all | solution.py:576
  (290 shorter events, 248.3 us)
Async XLA Ops:
  2.8 34.3 %all-to-all-start = ((bf16[8,4,16,768]{3,2,1,0:T(8,128)(2,1)}), bf16[8,4,16,768]{3,2,1,0:T(8,128)(2,1)}, u32[]{:S(2)}, u32[]{:S(2)}) async-start(bf16[8,4,16,768]{3,2,1,0:T(8,128)(2,1)} %copy.21), calls=%async_computation | async-start | bytes 1572864 | tf_op jit(solution)/shard_map/all_to_all | solution.py:576
  40.1 29.0 %collective-permute-start.6 = (bf16[8,16,768]{2,1,0:T(8,128)(2,1)S(1)}, bf16[8,16,768]{2,1,0:T(8,128)(2,1)}, u32[]{:S(2)}, u32[]{:S(2)}) collective-permute-start(bf16[8,16,768]{2,1,0:T(8,128)(2,1)S(1)} %slice_bitcast_fusion.6.refs_7_), channel_id=1, source_target_pairs={{0,1},{1,0},{2,3},{3,2},{4,5},{5,4},{6,7},{7,6},{8,9},{9,8},{10,11... | collective-permute-start | bytes 589832 | tf_op jit(solution)/shard_map/ppermute | solution.py:38
  45.2 27.1 %collective-permute-start.7 = (bf16[2,128,768]{2,1,0:T(8,128)(2,1)S(1)}, bf16[2,128,768]{2,1,0:T(8,128)(2,1)S(1)}, u32[]{:S(2)}, u32[]{:S(2)}) collective-permute-start(bf16[2,128,768]{2,1,0:T(8,128)(2,1)S(1)} %pad_maximum_fusion.11.refs_1_), channel_id=1, source_target_pairs={{0,6},{1,7},{2,0},{3,1},{4,2},{5,3},{6,4},{7,5},{8,14},{9,15},{10,... | collective-permute-start | bytes 1179656 | tf_op jit(solution)/shard_map/ppermute | solution.py:38
  51.7 24.7 %collective-permute-start.9 = (bf16[2,128,768]{2,1,0:T(8,128)(2,1)S(1)}, bf16[2,128,768]{2,1,0:T(8,128)(2,1)S(1)}, u32[]{:S(2)}, u32[]{:S(2)}) collective-permute-start(bf16[2,128,768]{2,1,0:T(8,128)(2,1)S(1)} %pad_maximum_fusion.11.refs_1_), channel_id=1, source_target_pairs={{0,2},{1,3},{2,4},{3,5},{4,6},{5,7},{6,0},{7,1},{8,10},{9,11},{10,... | collective-permute-start | bytes 1179656 | tf_op jit(solution)/shard_map/ppermute | solution.py:38
  72.3 28.7 %collective-permute-start.13 = (bf16[2,128,768]{2,1,0:T(8,128)(2,1)S(1)}, bf16[2,128,768]{2,1,0:T(8,128)(2,1)S(1)}, u32[]{:S(2)}, u32[]{:S(2)}) collective-permute-start(bf16[2,128,768]{2,1,0:T(8,128)(2,1)S(1)} %get-tuple-element.462), channel_id=1, source_target_pairs={{0,4},{1,5},{2,6},{3,7},{4,0},{5,1},{6,2},{7,3},{8,12},{9,13},{10,... | collective-permute-start | bytes 1179656 | tf_op jit(solution)/shard_map/ppermute | solution.py:38
  76.4 31.3 %collective-permute-start.14 = (bf16[2,128,768]{2,1,0:T(8,128)(2,1)S(1)}, bf16[2,128,768]{2,1,0:T(8,128)(2,1)S(1)}, u32[]{:S(2)}, u32[]{:S(2)}) collective-permute-start(bf16[2,128,768]{2,1,0:T(8,128)(2,1)S(1)} %get-tuple-element.463), channel_id=1, source_target_pairs={{0,2},{1,3},{2,4},{3,5},{4,6},{5,7},{6,0},{7,1},{8,10},{9,11},{10,... | collective-permute-start | bytes 1179656 | tf_op jit(solution)/shard_map/ppermute | solution.py:38
  82.3 25.5 %collective-permute-start.15 = (bf16[2,128,768]{2,1,0:T(8,128)(2,1)S(1)}, bf16[2,128,768]{2,1,0:T(8,128)(2,1)S(1)}, u32[]{:S(2)}, u32[]{:S(2)}) collective-permute-start(bf16[2,128,768]{2,1,0:T(8,128)(2,1)S(1)} %get-tuple-element.464), channel_id=1, source_target_pairs={{0,6},{1,7},{2,0},{3,1},{4,2},{5,3},{6,4},{7,5},{8,14},{9,15},{10,... | collective-permute-start | bytes 1179656 | tf_op jit(solution)/shard_map/ppermute | solution.py:38
  84.1 24.6 %collective-permute-start.16 = (bf16[3,128,768]{2,1,0:T(8,128)(2,1)S(1)}, bf16[3,128,768]{2,1,0:T(8,128)(2,1)S(1)}, u32[]{:S(2)}, u32[]{:S(2)}) collective-permute-start(bf16[3,128,768]{2,1,0:T(8,128)(2,1)S(1)} %slice.108), channel_id=1, source_target_pairs={{0,120},{8,112},{16,104},{24,96},{32,88},{40,80},{48,72},{56,64},{... | collective-permute-start | bytes 1769480 | tf_op jit(solution)/shard_map/ppermute | solution.py:600
  127.7 25.5 %collective-permute-start.20 = (bf16[2,128,768]{2,1,0:T(8,128)(2,1)S(1)}, bf16[2,128,768]{2,1,0:T(8,128)(2,1)S(1)}, u32[]{:S(2)}, u32[]{:S(2)}) collective-permute-start(bf16[2,128,768]{2,1,0:T(8,128)(2,1)S(1)} %fusion.1.refs_1_), channel_id=1, source_target_pairs={{0,6},{1,7},{2,0},{3,1},{4,2},{5,3},{6,4},{7,5},{8,14},{9,15},{10,... | collective-permute-start | bytes 1179656 | tf_op jit(solution)/shard_map/ppermute | solution.py:38
  128.8 26.3 %collective-permute-start.21 = (bf16[2,128,768]{2,1,0:T(8,128)(2,1)S(1)}, bf16[2,128,768]{2,1,0:T(8,128)(2,1)S(1)}, u32[]{:S(2)}, u32[]{:S(2)}) collective-permute-start(bf16[2,128,768]{2,1,0:T(8,128)(2,1)S(1)} %fusion.1.refs_1_), channel_id=1, source_target_pairs={{0,4},{1,5},{2,6},{3,7},{4,0},{5,1},{6,2},{7,3},{8,12},{9,13},{10,... | collective-permute-start | bytes 1179656 | tf_op jit(solution)/shard_map/ppermute | solution.py:38
  129.3 26.7 %collective-permute-start.22 = (bf16[2,128,768]{2,1,0:T(8,128)(2,1)S(1)}, bf16[2,128,768]{2,1,0:T(8,128)(2,1)S(1)}, u32[]{:S(2)}, u32[]{:S(2)}) collective-permute-start(bf16[2,128,768]{2,1,0:T(8,128)(2,1)S(1)} %fusion.1.refs_1_), channel_id=1, source_target_pairs={{0,2},{1,3},{2,4},{3,5},{4,6},{5,7},{6,0},{7,1},{8,10},{9,11},{10,... | collective-permute-start | bytes 1179656 | tf_op jit(solution)/shard_map/ppermute | solution.py:38
  133.3 38.3 %collective-permute-start.26 = (bf16[2,8,16,768]{3,2,1,0:T(8,128)(2,1)S(1)}, bf16[2,8,16,768]{3,2,1,0:T(8,128)(2,1)S(1)}, u32[]{:S(2)}, u32[]{:S(2)}) collective-permute-start(bf16[2,8,16,768]{3,2,1,0:T(8,128)(2,1)S(1)} %get-tuple-element.522), channel_id=1, source_target_pairs={{0,4},{1,5},{2,6},{3,7},{4,0},{5,1},{6,2},{7,3},{8,12},{9,13},{10,... | collective-permute-start | bytes 1179656 | tf_op jit(solution)/shard_map/ppermute | solution.py:38
  155.9 24.6 %collective-permute-start.28 = (bf16[2,8,16,768]{3,2,1,0:T(8,128)(2,1)S(1)}, bf16[2,8,16,768]{3,2,1,0:T(8,128)(2,1)S(1)}, u32[]{:S(2)}, u32[]{:S(2)}) collective-permute-start(bf16[2,8,16,768]{3,2,1,0:T(8,128)(2,1)S(1)} %get-tuple-element.524), channel_id=1, source_target_pairs={{0,6},{1,7},{2,0},{3,1},{4,2},{5,3},{6,4},{7,5},{8,14},{9,15},{10,... | collective-permute-start | bytes 1179656 | tf_op jit(solution)/shard_map/ppermute | solution.py:38
  172.4 25.2 %collective-permute-start.32 = (bf16[4,128,768]{2,1,0:T(8,128)(2,1)S(1)}, bf16[4,128,768]{2,1,0:T(8,128)(2,1)S(1)}, u32[]{:S(2)}, u32[]{:S(2)}) collective-permute-start(bf16[4,128,768]{2,1,0:T(8,128)(2,1)S(1)} %pad_maximum_fusion.1.refs_1_), channel_id=1, source_target_pairs={{0,1},{1,0},{2,3},{3,2},{4,5},{5,4},{6,7},{7,6},{8,9},{9,8},{10,11... | collective-permute-start | bytes 2359304 | tf_op jit(solution)/shard_map/ppermute | solution.py:38
  181.2 25.8 %collective-permute-start.35 = (bf16[3,8,16,768]{3,2,1,0:T(8,128)(2,1)}, bf16[3,8,16,768]{3,2,1,0:T(8,128)(2,1)}, u32[]{:S(2)}, u32[]{:S(2)}) collective-permute-start(bf16[3,8,16,768]{3,2,1,0:T(8,128)(2,1)} %get-tuple-element.558), channel_id=1, source_target_pairs={{120,121},{121,120},{122,123},{123,122},{124,125},{125,124},{126,1... | collective-permute-start | bytes 1769480 | tf_op jit(solution)/shard_map/ppermute | solution.py:54
  212.5 26.1 %collective-permute-start.39 = (bf16[2,128,768]{2,1,0:T(8,128)(2,1)S(1)}, bf16[2,128,768]{2,1,0:T(8,128)(2,1)S(1)}, u32[]{:S(2)}, u32[]{:S(2)}) collective-permute-start(bf16[2,128,768]{2,1,0:T(8,128)(2,1)S(1)} %add_convert_fusion.9), channel_id=1, source_target_pairs={{0,8},{1,9},{2,10},{3,11},{4,12},{5,13},{6,14},{7,15},{8,16},{9,17... | collective-permute-start | bytes 1179656 | tf_op jit(solution)/shard_map/ppermute | solution.py:49
  222.9 30.2 %collective-permute-start.40 = (bf16[2,128,768]{2,1,0:T(8,128)(2,1)S(1)}, bf16[2,128,768]{2,1,0:T(8,128)(2,1)S(1)}, u32[]{:S(2)}, u32[]{:S(2)}) collective-permute-start(bf16[2,128,768]{2,1,0:T(8,128)(2,1)S(1)} %add_convert_fusion.9), channel_id=1, source_target_pairs={{0,9},{1,8},{2,11},{3,10},{4,13},{5,12},{6,15},{7,14},{8,17},{9,16... | collective-permute-start | bytes 1179656 | tf_op jit(solution)/shard_map/ppermute | solution.py:49
  227.8 67.8 %collective-permute-start.81 = (bf16[4,128,768]{2,1,0:T(8,128)(2,1)S(1)}, bf16[4,128,768]{2,1,0:T(8,128)(2,1)S(1)}, u32[]{:S(2)}, u32[]{:S(2)}) collective-permute-start(bf16[4,128,768]{2,1,0:T(8,128)(2,1)S(1)} %pad_maximum_fusion.3.refs_1_), channel_id=1, source_target_pairs={{0,1},{1,0},{2,3},{3,2},{4,5},{5,4},{6,7},{7,6},{8,9},{9,8},{10,11... | collective-permute-start | bytes 2359304 | tf_op jit(solution)/shard_map/ppermute | solution.py:38
  254.3 24.0 %collective-permute-start.42 = (bf16[2,128,768]{2,1,0:T(8,128)(2,1)S(1)}, bf16[2,128,768]{2,1,0:T(8,128)(2,1)S(1)}, u32[]{:S(2)}, u32[]{:S(2)}) collective-permute-start(bf16[2,128,768]{2,1,0:T(8,128)(2,1)S(1)} %fusion.3.refs_1_), channel_id=1, source_target_pairs={{0,4},{1,5},{2,6},{3,7},{4,0},{5,1},{6,2},{7,3},{8,12},{9,13},{10,... | collective-permute-start | bytes 1179656 | tf_op jit(solution)/shard_map/ppermute | solution.py:38
  254.4 24.5 %collective-permute-start.43 = (bf16[2,128,768]{2,1,0:T(8,128)(2,1)S(1)}, bf16[2,128,768]{2,1,0:T(8,128)(2,1)S(1)}, u32[]{:S(2)}, u32[]{:S(2)}) collective-permute-start(bf16[2,128,768]{2,1,0:T(8,128)(2,1)S(1)} %fusion.3.refs_1_), channel_id=1, source_target_pairs={{0,2},{1,3},{2,4},{3,5},{4,6},{5,7},{6,0},{7,1},{8,10},{9,11},{10,... | collective-permute-start | bytes 1179656 | tf_op jit(solution)/shard_map/ppermute | solution.py:38
  278.3 25.1 %collective-permute-start.47 = (bf16[2,8,16,768]{3,2,1,0:T(8,128)(2,1)S(1)}, bf16[2,8,16,768]{3,2,1,0:T(8,128)(2,1)S(1)}, u32[]{:S(2)}, u32[]{:S(2)}) collective-permute-start(bf16[2,8,16,768]{3,2,1,0:T(8,128)(2,1)S(1)} %get-tuple-element.617), channel_id=1, source_target_pairs={{0,4},{1,5},{2,6},{3,7},{4,0},{5,1},{6,2},{7,3},{8,12},{9,13},{10,... | collective-permute-start | bytes 1179656 | tf_op jit(solution)/shard_map/ppermute | solution.py:38
  278.9 25.0 %collective-permute-start.48 = (bf16[2,8,16,768]{3,2,1,0:T(8,128)(2,1)S(1)}, bf16[2,8,16,768]{3,2,1,0:T(8,128)(2,1)S(1)}, u32[]{:S(2)}, u32[]{:S(2)}) collective-permute-start(bf16[2,8,16,768]{3,2,1,0:T(8,128)(2,1)S(1)} %get-tuple-element.618), channel_id=1, source_target_pairs={{0,2},{1,3},{2,4},{3,5},{4,6},{5,7},{6,0},{7,1},{8,10},{9,11},{10,... | collective-permute-start | bytes 1179656 | tf_op jit(solution)/shard_map/ppermute | solution.py:38
  328.5 31.8 %collective-permute-start.60 = (bf16[2,128,768]{2,1,0:T(8,128)(2,1)S(1)}, bf16[2,128,768]{2,1,0:T(8,128)(2,1)S(1)}, u32[]{:S(2)}, u32[]{:S(2)}) collective-permute-start(bf16[2,128,768]{2,1,0:T(8,128)(2,1)S(1)} %add_convert_fusion.6), channel_id=1, source_target_pairs={{0,8},{1,9},{2,10},{3,11},{4,12},{5,13},{6,14},{7,15},{8,16},{9,17... | collective-permute-start | bytes 1179656 | tf_op jit(solution)/shard_map/ppermute | solution.py:49
  330.4 29.9 %collective-permute-start.61 = (bf16[2,128,768]{2,1,0:T(8,128)(2,1)S(1)}, bf16[2,128,768]{2,1,0:T(8,128)(2,1)S(1)}, u32[]{:S(2)}, u32[]{:S(2)}) collective-permute-start(bf16[2,128,768]{2,1,0:T(8,128)(2,1)S(1)} %add_convert_fusion.6), channel_id=1, source_target_pairs={{0,9},{1,8},{2,11},{3,10},{4,13},{5,12},{6,15},{7,14},{8,17},{9,16... | collective-permute-start | bytes 1179656 | tf_op jit(solution)/shard_map/ppermute | solution.py:49
  364.9 24.7 %collective-permute-start.63 = (bf16[2,128,768]{2,1,0:T(8,128)(2,1)S(1)}, bf16[2,128,768]{2,1,0:T(8,128)(2,1)S(1)}, u32[]{:S(2)}, u32[]{:S(2)}) collective-permute-start(bf16[2,128,768]{2,1,0:T(8,128)(2,1)S(1)} %fusion.5.refs_1_), channel_id=1, source_target_pairs={{0,4},{1,5},{2,6},{3,7},{4,0},{5,1},{6,2},{7,3},{8,12},{9,13},{10,... | collective-permute-start | bytes 1179656 | tf_op jit(solution)/shard_map/ppermute | solution.py:38
  372.8 24.3 %collective-permute-start.64 = (bf16[2,128,768]{2,1,0:T(8,128)(2,1)S(1)}, bf16[2,128,768]{2,1,0:T(8,128)(2,1)S(1)}, u32[]{:S(2)}, u32[]{:S(2)}) collective-permute-start(bf16[2,128,768]{2,1,0:T(8,128)(2,1)S(1)} %fusion.5.refs_1_), channel_id=1, source_target_pairs={{0,2},{1,3},{2,4},{3,5},{4,6},{5,7},{6,0},{7,1},{8,10},{9,11},{10,... | collective-permute-start | bytes 1179656 | tf_op jit(solution)/shard_map/ppermute | solution.py:38
  381.2 30.8 %collective-permute-start.53 = (bf16[3,128,768]{2,1,0:T(8,128)(2,1)S(1)}, bf16[3,128,768]{2,1,0:T(8,128)(2,1)S(1)}, u32[]{:S(2)}, u32[]{:S(2)}) collective-permute-start(bf16[3,128,768]{2,1,0:T(8,128)(2,1)S(1)} %pad_maximum_fusion.5), channel_id=1, source_target_pairs={{0,1},{1,0},{2,3},{3,2},{4,5},{5,4},{6,7},{7,6},{8,9},{9,8},{10,11... | collective-permute-start | bytes 1769480 | tf_op jit(solution)/shard_map/ppermute | solution.py:38
  384.9 30.0 %collective-permute-start.76 = (bf16[2,8,16,768]{3,2,1,0:T(8,128)(2,1)S(1)}, bf16[2,8,16,768]{3,2,1,0:T(8,128)(2,1)S(1)}, u32[]{:S(2)}, u32[]{:S(2)}) collective-permute-start(bf16[2,8,16,768]{3,2,1,0:T(8,128)(2,1)S(1)} %norm_grad.6), channel_id=1, source_target_pairs={{8,0},{9,1},{10,2},{11,3},{12,4},{13,5},{14,6},{15,7},{16,8},{17,9... | collective-permute-start | bytes 1179656 | tf_op jit(solution)/shard_map/ppermute | solution.py:49
  408.4 27.0 %collective-permute-start.71 = (bf16[2,128,768]{2,1,0:T(8,128)(2,1)S(1)}, bf16[2,128,768]{2,1,0:T(8,128)(2,1)S(1)}, u32[]{:S(2)}, u32[]{:S(2)}) collective-permute-start(bf16[2,128,768]{2,1,0:T(8,128)(2,1)S(1)} %get-tuple-element.722), channel_id=1, source_target_pairs={{0,4},{1,5},{2,6},{3,7},{4,0},{5,1},{6,2},{7,3},{8,12},{9,13},{10,... | collective-permute-start | bytes 1179656 | tf_op jit(solution)/shard_map/ppermute | solution.py:38
  409.5 27.7 %collective-permute-start.72 = (bf16[2,128,768]{2,1,0:T(8,128)(2,1)S(1)}, bf16[2,128,768]{2,1,0:T(8,128)(2,1)S(1)}, u32[]{:S(2)}, u32[]{:S(2)}) collective-permute-start(bf16[2,128,768]{2,1,0:T(8,128)(2,1)S(1)} %get-tuple-element.723), channel_id=1, source_target_pairs={{0,2},{1,3},{2,4},{3,5},{4,6},{5,7},{6,0},{7,1},{8,10},{9,11},{10,... | collective-permute-start | bytes 1179656 | tf_op jit(solution)/shard_map/ppermute | solution.py:38
  412.1 25.3 %collective-permute-start.73 = (bf16[2,128,768]{2,1,0:T(8,128)(2,1)S(1)}, bf16[2,128,768]{2,1,0:T(8,128)(2,1)S(1)}, u32[]{:S(2)}, u32[]{:S(2)}) collective-permute-start(bf16[2,128,768]{2,1,0:T(8,128)(2,1)S(1)} %get-tuple-element.724), channel_id=1, source_target_pairs={{0,6},{1,7},{2,0},{3,1},{4,2},{5,3},{6,4},{7,5},{8,14},{9,15},{10,... | collective-permute-start | bytes 1179656 | tf_op jit(solution)/shard_map/ppermute | solution.py:38
  439.0 46.5 %all-to-all-start.1 = ((bf16[8,3,16,768]{3,2,1,0:T(8,128)(2,1)}), bf16[8,3,16,768]{3,2,1,0:T(8,128)(2,1)}, u32[]{:S(2)}, u32[]{:S(2)}) async-start(bf16[8,3,16,768]{3,2,1,0:T(8,128)(2,1)} %copy.24), calls=%async_computation.1 | async-start | bytes 1179648 | tf_op jit(solution)/shard_map/all_to_all | solution.py:576
  (88 other events, 1148.7 us)
